TPU v7x, 128 devices: a whole 4x4x4 slice. The times are simulated.
128 devices in a mesh: gx: 16 (over y, x), gy: 8 (over z, core).
Axes of the slice: x: 4, y: 4, z: 4, core: 2. Of those that a mesh axis runs over, the one named last changes fastest.
Arguments:
- right_block: bfloat16 [262144, 768], P(('gx', 'gy')), may hold values from -6 to 6
- point_order: int32 [16, 8, 2048], P('gx', 'gy'), may hold values from 0 to 2047, each once within a row
- leaf_dense: bfloat16 [262144, 2048], P(('gx', 'gy')), may hold values from -0.125 to 0.125
- basis_in: bfloat16 [262144, 256], P(('gx', 'gy')), may hold values from -0.125 to 0.125
- basis_out: bfloat16 [262144, 256], P(('gx', 'gy')), may hold values from -0.1875 to 0.1875
- leaf_couple: bfloat16 [16, 8, 4, 256, 256], P('gx', 'gy'), may hold values from -0.375 to 0.375
- coarse_couple: bfloat16 [16, 8, 4, 256, 256], P('gx', 'gy'), may hold values from -1 to 1, as said below
- top_coupling: bfloat16 [2048, 2048], replicated, may hold values from -0.125 to 0.125
Outputs:
- product: bfloat16 [262144, 768], P(('gx', 'gy'))
Inputs may be any that keep to these rules, and one draw needn't show every extreme that they name: coarse_couple[i, j] is equal over each aligned 2 x 2 block of leaves.
All inputs are finite; a program needn't handle non-finite values.
Results may differ from a plain program's by a relative error of at most 0.013.
Values may be sent and summed in bfloat16 or wider, within the bound.
No kernel may reach another device: no remote copies, remote signals or barrier semaphores. Data moves between devices by JAX's collectives and lax.ppermute only.
A program may use at most 128 MiB of HBM per device.

v0:
```python
import jax
import jax.numpy as jnp
from jax import lax
from jax.sharding import PartitionSpec as P


def partner(array, axis, distance):
    return lax.ppermute(array, axis, [(i, i ^ 1 << distance) for i in range(lax.axis_size(axis))])


def local(
    right_block,
    point_order,
    leaf_dense,
    basis_in,
    basis_out,
    leaf_couple,
    coarse_couple,
    top_coupling,
):
    order_local = point_order[0, 0]
    ordered = jnp.take(right_block, order_local, axis=0)
    coefficient = jnp.einsum(
        "lr,ln->rn", basis_in, ordered, preferred_element_type=jnp.float32
    ).astype(jnp.bfloat16)
    factors = [leaf_couple[0, 0], coarse_couple[0, 0]]
    near_terms = []
    for height in range(2):
        factors_here = factors[height]
        lifted = jnp.einsum(
            "rs,rn->sn", factors_here[0], coefficient, preferred_element_type=jnp.float32
        ).astype(jnp.bfloat16)
        side_x, lifted_x = partner((coefficient, lifted), "gx", height)
        pair_sum = (lifted.astype(jnp.float32) + lifted_x.astype(jnp.float32)).astype(jnp.bfloat16)
        side_y, side_xy, pair_y = partner((coefficient, side_x, pair_sum), "gy", height)
        near_sum = jnp.dot(factors_here[1], side_x, preferred_element_type=jnp.float32)
        near_sum = near_sum + jnp.dot(factors_here[2], side_y, preferred_element_type=jnp.float32)
        near_sum = near_sum + jnp.dot(factors_here[3], side_xy, preferred_element_type=jnp.float32)
        near_terms.append(near_sum)
        coefficient = (pair_sum.astype(jnp.float32) + pair_y.astype(jnp.float32)).astype(
            jnp.bfloat16
        )
    local_term = jnp.dot(leaf_dense, ordered, preferred_element_type=jnp.float32)
    row_index = lax.axis_index("gx")
    col_index = lax.axis_index("gy")
    tops_x = lax.axis_size("gx") // 4
    tops_y = lax.axis_size("gy") // 4
    width_rank = coefficient.shape[0]
    columns = coefficient.shape[1]
    position = row_index % 4 * 4 + col_index % 4
    portion = lax.dynamic_slice_in_dim(
        coefficient, position * (width_rank // 16), width_rank // 16, 0
    )
    gathered = lax.all_gather(portion, ("gx", "gy"), axis=0, tiled=True)
    top_boxes = gathered.reshape(tops_x, 4, tops_y, 4, width_rank // 16, columns)
    top_boxes = top_boxes.transpose(0, 2, 1, 3, 4, 5).reshape(tops_x * tops_y, width_rank, columns)
    own_box = row_index // 4 * tops_y + col_index // 4
    others = jnp.arange(tops_x * tops_y, dtype=jnp.int32) != own_box
    masked = jnp.where(others[:, None, None], top_boxes, jnp.zeros((), jnp.bfloat16))
    top_rows = lax.dynamic_slice_in_dim(top_coupling, own_box * width_rank, width_rank, 0)
    downward = jnp.dot(
        top_rows,
        masked.reshape(tops_x * tops_y * width_rank, columns),
        preferred_element_type=jnp.float32,
    ).astype(jnp.bfloat16)
    for height in (1, 0):
        lowered = jnp.dot(factors[height][0], downward, preferred_element_type=jnp.float32)
        downward = (near_terms[height] + lowered).astype(jnp.bfloat16)
    leaf_result = (
        local_term + jnp.dot(basis_out, downward, preferred_element_type=jnp.float32)
    ).astype(jnp.bfloat16)
    return jnp.zeros_like(leaf_result).at[order_local].set(leaf_result)


def solution(mesh):
    in_specs = (
        P(("gx", "gy"), None),
        P("gx", "gy", None),
        P(("gx", "gy"), None),
        P(("gx", "gy"), None),
        P(("gx", "gy"), None),
        P("gx", "gy", None, None, None),
        P("gx", "gy", None, None, None),
        P(),
    )
    out_specs = P(("gx", "gy"), None)
    return jax.shard_map(local, mesh=mesh, in_specs=in_specs, out_specs=out_specs, check_vma=False)
```

profile of v0, /device:TPU:1, one launch (start us, length us, event | category | flops | bytes accessed | tf_op | source)
XLA Modules:
  0.0 174.4 jit_solution(11669704465483753549)
XLA Ops:
  8.4 9.4 %gather_fusion = bf16[2048,768]{1,0:T(8,128)(2,1)} fusion(bf16[2048,768]{1,0:T(8,128)(2,1)S(1)} %copy-done, s32[2048]{0:T(1024)S(1)} %broadcast_clamp_fusion), kind=kCustom, calls=%fused_computation | custom fusion | bytes 6299648 | tf_op jit(solution)/shard_map/jit(_take)/gather | solution.py:22
  17.8 3.6 %fusion.7 = bf16[768,256]{1,0:T(8,128)(2,1)S(1)} fusion(bf16[2048,256]{1,0:T(8,128)(2,1)} %param.11, bf16[2048,768]{1,0:T(8,128)(2,1)} %gather_fusion, pred[2048]{0:T(1024)(128)(4,1)S(1)} %compare_and_fusion), kind=kOutput, calls=%fused_computation.16 | convolution fusion | flops 807075840 | bytes 4589568 | tf_op jit(solution)/shard_map/lr,ln->rn/dot_general | solution.py:23
  22.7 2.1 %collective-permute-start.3 = (bf16[256,768]{0,1:T(8,128)(2,1)S(1)}, bf16[256,768]{0,1:T(8,128)(2,1)S(1)}, u32[]{:S(2)}, u32[]{:S(2)}) collective-permute-start(bf16[256,768]{0,1:T(8,128)(2,1)S(1)} %fusion.11), channel_id=1, source_target_pairs={{0,8},{8,0},{16,24},{24,16},{32,40},{40,32},{48,56},{56,48},{64,72... | collective-permute-start | bytes 1179656 | tf_op jit(solution)/shard_map/ppermute | solution.py:8
  24.9 8.3 %collective-permute-done.3 = bf16[256,768]{0,1:T(8,128)(2,1)S(1)} collective-permute-done((bf16[256,768]{0,1:T(8,128)(2,1)S(1)}, bf16[256,768]{0,1:T(8,128)(2,1)S(1)}, u32[]{:S(2)}, u32[]{:S(2)}) %collective-permute-start.3) | collective-permute-done | bytes 393248 | tf_op jit(solution)/shard_map/ppermute | solution.py:8
  33.3 1.8 %collective-permute-start.4 = (bf16[256,768]{0,1:T(8,128)(2,1)S(1)}, bf16[256,768]{0,1:T(8,128)(2,1)S(1)}, u32[]{:S(2)}, u32[]{:S(2)}) collective-permute-start(bf16[256,768]{0,1:T(8,128)(2,1)S(1)} %add_convert_fusion.3), channel_id=1, source_target_pairs={{0,1},{1,0},{2,3},{3,2},{4,5},{5,4},{6,7},{7,6},{8,9},{9,8},{10,11... | collective-permute-start | bytes 1179656 | tf_op jit(solution)/shard_map/ppermute | solution.py:8
  37.8 3.1 %collective-permute-start.8 = (bf16[256,768]{1,0:T(8,128)(2,1)S(1)}, bf16[256,768]{1,0:T(8,128)(2,1)S(1)}, u32[]{:S(2)}, u32[]{:S(2)}) collective-permute-start(bf16[256,768]{1,0:T(8,128)(2,1)S(1)} %fusion.12), channel_id=1, source_target_pairs={{0,16},{8,24},{16,0},{24,8},{32,48},{40,56},{48,32},{56,40},{64,80... | collective-permute-start | bytes 1179656 | tf_op jit(solution)/shard_map/ppermute | solution.py:8
  40.9 8.9 %collective-permute-done.8 = bf16[256,768]{1,0:T(8,128)(2,1)S(1)} collective-permute-done((bf16[256,768]{1,0:T(8,128)(2,1)S(1)}, bf16[256,768]{1,0:T(8,128)(2,1)S(1)}, u32[]{:S(2)}, u32[]{:S(2)}) %collective-permute-start.8) | collective-permute-done | bytes 393248 | tf_op jit(solution)/shard_map/ppermute | solution.py:8
  50.6 1.8 %collective-permute-start.9 = (bf16[256,768]{1,0:T(8,128)(2,1)}, bf16[256,768]{1,0:T(8,128)(2,1)}, u32[]{:S(2)}, u32[]{:S(2)}) collective-permute-start(bf16[256,768]{1,0:T(8,128)(2,1)} %add_convert_fusion.1), channel_id=1, source_target_pairs={{0,2},{1,3},{2,0},{3,1},{4,6},{5,7},{6,4},{7,5},{8,10},{9,11},{10,... | collective-permute-start | bytes 1179656 | tf_op jit(solution)/shard_map/ppermute | solution.py:8
  52.4 8.6 %collective-permute-done.9 = bf16[256,768]{1,0:T(8,128)(2,1)} collective-permute-done((bf16[256,768]{1,0:T(8,128)(2,1)}, bf16[256,768]{1,0:T(8,128)(2,1)}, u32[]{:S(2)}, u32[]{:S(2)}) %collective-permute-start.9) | collective-permute-done | bytes 393248 | tf_op jit(solution)/shard_map/ppermute | solution.py:8
  62.4 1.9 %collective-permute-start.1 = (bf16[256,768]{0,1:T(8,128)(2,1)}, bf16[256,768]{0,1:T(8,128)(2,1)}, u32[]{:S(2)}, u32[]{:S(2)}) collective-permute-start(bf16[256,768]{0,1:T(8,128)(2,1)} %bitcast.60), channel_id=1, source_target_pairs={{0,1},{1,0},{2,3},{3,2},{4,5},{5,4},{6,7},{7,6},{8,9},{9,8},{10,11... | collective-permute-start | bytes 1179656 | tf_op jit(solution)/shard_map/ppermute | solution.py:8
  65.5 12.7 %fusion.6 = f32[768,2048]{1,0:T(8,128)} fusion(bf16[2048,2048]{1,0:T(8,128)(2,1)} %param.10, bf16[2048,768]{1,0:T(8,128)(2,1)} %gather_fusion, pred[2048]{0:T(1024)(128)(4,1)S(1)} %compare_and_fusion), kind=kOutput, calls=%fused_computation.15 | convolution fusion | flops 6444023808 | bytes 17827840 | tf_op jit(solution)/shard_map/dot_general | solution.py:43
  78.3 1.5 collective-permute-start.6
  79.9 2.4 %collective-permute-start.5 = (bf16[256,768]{0,1:T(8,128)(2,1)S(1)}, bf16[256,768]{0,1:T(8,128)(2,1)}, u32[]{:S(2)}, u32[]{:S(2)}) collective-permute-start(bf16[256,768]{0,1:T(8,128)(2,1)S(1)} %add_convert_fusion.2), channel_id=1, source_target_pairs={{0,16},{8,24},{16,0},{24,8},{32,48},{40,56},{48,32},{56,40},{64,80... | collective-permute-start | bytes 1179656 | tf_op jit(solution)/shard_map/ppermute | solution.py:8
  84.7 2.2 %convolution_add_fusion.3 = f32[768,256]{1,0:T(8,128)} fusion(f32[768,256]{1,0:T(8,128)S(1)} %fusion.27, bf16[256,768]{0,1:T(8,128)(2,1)} %collective-permute-done, bf16[1,1,4,256,256]{4,3,2,1,0:T(8,128)(2,1)} %param.13), kind=kOutput, calls=%fused_computation.13 | convolution fusion | flops 100859904 | bytes 2097152 | tf_op jit(solution)/shard_map/dot_general | solution.py:36
  86.9 4.8 %collective-permute-done.5 = bf16[256,768]{0,1:T(8,128)(2,1)} collective-permute-done((bf16[256,768]{0,1:T(8,128)(2,1)S(1)}, bf16[256,768]{0,1:T(8,128)(2,1)}, u32[]{:S(2)}, u32[]{:S(2)}) %collective-permute-start.5) | collective-permute-done | bytes 393248 | tf_op jit(solution)/shard_map/ppermute | solution.py:8
  92.2 2.2 %convolution_add_fusion.1 = f32[768,256]{1,0:T(8,128)} fusion(f32[768,256]{1,0:T(8,128)S(1)} %fusion.20, bf16[256,768]{0,1:T(8,128)(2,1)} %collective-permute-done.5, bf16[1,1,4,256,256]{4,3,2,1,0:T(8,128)(2,1)S(1)} %copy-done.1), kind=kOutput, calls=%fused_computation.10 | convolution fusion | flops 100859904 | bytes 2097152 | tf_op jit(solution)/shard_map/dot_general | solution.py:36
  94.4 37.9 %all-gather.2.cloned.1.call-done = bf16[2048,768]{1,0:T(8,128)(2,1)} async-done(((bf16[16,768]{1,0:T(8,128)(2,1)}), bf16[2048,768]{1,0:T(8,128)(2,1)}) %all-gather.2.cloned.1.call-update) | async-done | bytes 3145744 | tf_op jit(solution)/shard_map/all_gather | solution.py:54
  132.3 2.2 %copy.11 = bf16[4,2,4,4,16,768]{5,4,3,2,1,0:T(8,128)(2,1)S(1)} copy(bf16[4,2,4,4,16,768]{5,4,3,1,2,0:T(8,128)(2,1)} %bitcast.59) | data formatting | bytes 6291456 | tf_op jit(solution)/shard_map/transpose | solution.py:56
  134.5 2.1 %bitcast_select_fusion = bf16[2048,768]{1,0:T(8,128)(2,1)} fusion(bf16[4,2,4,4,16,768]{5,4,3,2,1,0:T(8,128)(2,1)S(1)} %copy.11, pred[2048]{0:T(1024)(128)(4,1)S(1)} %broadcast_in_dim.33), kind=kLoop, calls=%fused_computation.3 | loop fusion | flops 1572864 | bytes 6293504 | tf_op jit(solution)/shard_map/jit(_where)/select_n | solution.py:59
  136.6 4.4 %fusion.10 = f32[768,256]{1,0:T(8,128)} fusion(bf16[2048,768]{1,0:T(8,128)(2,1)} %bitcast_select_fusion, bf16[2048,2048]{1,0:T(8,128)(2,1)} %param.15, s32[]{:T(128)S(6)} %select_n.55, bf16[1,1,4,256,256]{4,3,2,1,0:T(8,128)(2,1)} %param.14), kind=kOutput, calls=%fused_computation.22 | convolution fusion | flops 906166272 | bytes 5111812 | tf_op jit(solution)/shard_map/dot_general | solution.py:67
  141.0 3.0 %fusion.13 = f32[768,256]{1,0:T(8,128)} fusion(f32[768,256]{1,0:T(8,128)} %fusion.10, f32[768,256]{1,0:T(8,128)} %convolution_add_fusion.1, bf16[256,768]{0,1:T(8,128)(2,1)} %collective-permute-done.7, bf16[1,1,4,256,256]{4,3,2,1,0:T(8,128)(2,1)} %param.14, bf16[1,1,4,256,256]{4,3,2,1,0:T(8,128)(2,1)} %param.13), kind=kOutput, calls=%fused_computation.25 | convolution fusion | flops 201916416 | bytes 3014656 | tf_op jit(solution)/shard_map/dot_general | solution.py:67
  143.9 6.6 %fusion = bf16[2048,768]{0,1:T(8,128)(2,1)} fusion(f32[768,2048]{1,0:T(8,128)} %fusion.6, bf16[2048,256]{1,0:T(8,128)(2,1)} %param.12, f32[768,256]{1,0:T(8,128)} %fusion.13, f32[768,256]{1,0:T(8,128)} %convolution_add_fusion.3, bf16[256,768]{0,1:T(8,128)(2,1)} %collective-permute-done.2, bf16[1,1,4,256,256]{4,3,2,1,0:T(8,128)(2,1)} %param.13), kind=kOutput, calls=%fused_computation.5 | convolution fusion | flops 909705216 | bytes 12582912 | tf_op jit(solution)/shard_map/dot_general | solution.py:70
  150.5 4.7 %copy.12 = bf16[2048,768]{1,0:T(8,128)(2,1)} copy(bf16[2048,768]{0,1:T(8,128)(2,1)} %fusion) | data formatting | bytes 6291456 | tf_op jit(solution)/shard_map/convert_element_type | solution.py:71
  155.2 12.3 %scatter_custom_fusion = bf16[2048,768]{1,0:T(8,128)(2,1)} fusion(s32[2048]{0:T(1024)S(1)} %bitcast.64, bf16[2048,768]{1,0:T(8,128)(2,1)} %copy.12, bf16[]{:T(256)} %constant.58.clone.1), kind=kCustom, calls=%fused_computation.6 | custom fusion | bytes 3146240 | tf_op jit(solution)/shard_map/scatter | solution.py:72
  (31 shorter events, 12.3 us)
Async XLA Ops:
  6.5 1.9 %copy-start = (bf16[2048,768]{1,0:T(8,128)(2,1)S(1)}, bf16[2048,768]{1,0:T(8,128)(2,1)}, u32[]{:S(2)}) copy-start(bf16[2048,768]{1,0:T(8,128)(2,1)} %param.8) | copy-start | bytes 9437188
  6.5 125.7 %all-gather.2.cloned.1.call-start = ((), (), s32[]{:S(2)}) async-start(), calls=%async_computation | async-start | bytes 3170304 | tf_op jit(solution)/shard_map/all_gather | solution.py:54
  21.4 29.2 %copy-start.2 = (bf16[768,256]{1,0:T(8,128)(2,1)}, bf16[768,256]{1,0:T(8,128)(2,1)S(1)}, u32[]{:S(2)}) copy-start(bf16[768,256]{1,0:T(8,128)(2,1)S(1)} %fusion.7) | copy-start | bytes 1179652
  22.7 10.4 %collective-permute-start.3 = (bf16[256,768]{0,1:T(8,128)(2,1)S(1)}, bf16[256,768]{0,1:T(8,128)(2,1)S(1)}, u32[]{:S(2)}, u32[]{:S(2)}) collective-permute-start(bf16[256,768]{0,1:T(8,128)(2,1)S(1)} %fusion.11), channel_id=1, source_target_pairs={{0,8},{8,0},{16,24},{24,16},{32,40},{40,32},{48,56},{56,48},{64,72... | collective-permute-start | bytes 1179656 | tf_op jit(solution)/shard_map/ppermute | solution.py:8
  33.3 3.2 %collective-permute-start.4 = (bf16[256,768]{0,1:T(8,128)(2,1)S(1)}, bf16[256,768]{0,1:T(8,128)(2,1)S(1)}, u32[]{:S(2)}, u32[]{:S(2)}) collective-permute-start(bf16[256,768]{0,1:T(8,128)(2,1)S(1)} %add_convert_fusion.3), channel_id=1, source_target_pairs={{0,1},{1,0},{2,3},{3,2},{4,5},{5,4},{6,7},{7,6},{8,9},{9,8},{10,11... | collective-permute-start | bytes 1179656 | tf_op jit(solution)/shard_map/ppermute | solution.py:8
  37.8 12.0 %collective-permute-start.8 = (bf16[256,768]{1,0:T(8,128)(2,1)S(1)}, bf16[256,768]{1,0:T(8,128)(2,1)S(1)}, u32[]{:S(2)}, u32[]{:S(2)}) collective-permute-start(bf16[256,768]{1,0:T(8,128)(2,1)S(1)} %fusion.12), channel_id=1, source_target_pairs={{0,16},{8,24},{16,0},{24,8},{32,48},{40,56},{48,32},{56,40},{64,80... | collective-permute-start | bytes 1179656 | tf_op jit(solution)/shard_map/ppermute | solution.py:8
  50.6 10.4 %collective-permute-start.9 = (bf16[256,768]{1,0:T(8,128)(2,1)}, bf16[256,768]{1,0:T(8,128)(2,1)}, u32[]{:S(2)}, u32[]{:S(2)}) collective-permute-start(bf16[256,768]{1,0:T(8,128)(2,1)} %add_convert_fusion.1), channel_id=1, source_target_pairs={{0,2},{1,3},{2,0},{3,1},{4,6},{5,7},{6,4},{7,5},{8,10},{9,11},{10,... | collective-permute-start | bytes 1179656 | tf_op jit(solution)/shard_map/ppermute | solution.py:8
  62.4 19.9 %collective-permute-start.1 = (bf16[256,768]{0,1:T(8,128)(2,1)}, bf16[256,768]{0,1:T(8,128)(2,1)}, u32[]{:S(2)}, u32[]{:S(2)}) collective-permute-start(bf16[256,768]{0,1:T(8,128)(2,1)} %bitcast.60), channel_id=1, source_target_pairs={{0,1},{1,0},{2,3},{3,2},{4,5},{5,4},{6,7},{7,6},{8,9},{9,8},{10,11... | collective-permute-start | bytes 1179656 | tf_op jit(solution)/shard_map/ppermute | solution.py:8
  64.3 19.4 %collective-permute-start = (bf16[256,768]{0,1:T(8,128)(2,1)}, bf16[256,768]{0,1:T(8,128)(2,1)}, u32[]{:S(2)}, u32[]{:S(2)}) collective-permute-start(bf16[256,768]{0,1:T(8,128)(2,1)} %bitcast.61), channel_id=1, source_target_pairs={{0,8},{8,0},{16,24},{24,16},{32,40},{40,32},{48,56},{56,48},{64,72... | collective-permute-start | bytes 1179656 | tf_op jit(solution)/shard_map/ppermute | solution.py:8
  78.3 13.6 %copy-start.1 = (bf16[1,1,4,256,256]{4,3,2,1,0:T(8,128)(2,1)S(1)}, bf16[1,1,4,256,256]{4,3,2,1,0:T(8,128)(2,1)}, u32[]{:S(2)}) copy-start(bf16[1,1,4,256,256]{4,3,2,1,0:T(8,128)(2,1)} %param.14) | copy-start | bytes 1572868
  78.3 13.6 %collective-permute-start.6 = (bf16[256,768]{0,1:T(8,128)(2,1)S(1)}, bf16[256,768]{0,1:T(8,128)(2,1)S(1)}, u32[]{:S(2)}, u32[]{:S(2)}) collective-permute-start(bf16[256,768]{0,1:T(8,128)(2,1)S(1)} %add_convert_fusion.2), channel_id=1, source_target_pairs={{0,2},{1,3},{2,0},{3,1},{4,6},{5,7},{6,4},{7,5},{8,10},{9,11},{10,... | collective-permute-start | bytes 1179656 | tf_op jit(solution)/shard_map/ppermute | solution.py:8
  79.9 11.8 %collective-permute-start.5 = (bf16[256,768]{0,1:T(8,128)(2,1)S(1)}, bf16[256,768]{0,1:T(8,128)(2,1)}, u32[]{:S(2)}, u32[]{:S(2)}) collective-permute-start(bf16[256,768]{0,1:T(8,128)(2,1)S(1)} %add_convert_fusion.2), channel_id=1, source_target_pairs={{0,16},{8,24},{16,0},{24,8},{32,48},{40,56},{48,32},{56,40},{64,80... | collective-permute-start | bytes 1179656 | tf_op jit(solution)/shard_map/ppermute | solution.py:8
  83.7 60.3 %collective-permute-start.2 = (bf16[256,768]{0,1:T(8,128)(2,1)}, bf16[256,768]{0,1:T(8,128)(2,1)}, u32[]{:S(2)}, u32[]{:S(2)}) collective-permute-start(bf16[256,768]{0,1:T(8,128)(2,1)} %collective-permute-done), channel_id=1, source_target_pairs={{0,1},{1,0},{2,3},{3,2},{4,5},{5,4},{6,7},{7,6},{8,9},{9,8},{10,11... | collective-permute-start | bytes 1179656 | tf_op jit(solution)/shard_map/ppermute | solution.py:8
  91.7 49.3 %collective-permute-start.7 = (bf16[256,768]{0,1:T(8,128)(2,1)}, bf16[256,768]{0,1:T(8,128)(2,1)}, u32[]{:S(2)}, u32[]{:S(2)}) collective-permute-start(bf16[256,768]{0,1:T(8,128)(2,1)} %collective-permute-done.5), channel_id=1, source_target_pairs={{0,2},{1,3},{2,0},{3,1},{4,6},{5,7},{6,4},{7,5},{8,10},{9,11},{10,... | collective-permute-start | bytes 1179656 | tf_op jit(solution)/shard_map/ppermute | solution.py:8
Sparse Core Ops, SparseCore 0:
  62.5 69.6 all-gather.1
where the time goes:
time: 175 us; the launch traced here: 174 us
  waiting for transfers between devices  69.9 us (40%)
  matrix products  38.7 us (22%)
  local copies, waits for them, and re-layouts  28.9 us (17%)
  starting transfers between devices  17.2 us (10%)
  between operations  13.5 us (8%)
  other arithmetic  6.19 us (4%)
    all_gather x1, waiting for transfers between devices, local(): gathered = lax.all_gather(portion, ('gx', 'gy'), axis=0, tiled=True)  37.9 us
    ppermute x10, waiting for transfers between devices, partner(): lax.ppermute(array, axis, [(i, i ^ 1 << distance) for i in range(lax.axis...  31.9 us
    ppermute x10, starting transfers between devices, partner(): lax.ppermute(array, axis, [(i, i ^ 1 << distance) for i in range(lax.axis...  17.2 us
    dot_general x1, matrix products, local(): jnp.dot(leaf_dense, ordered, preferred_element_type=jnp.float32)  12.7 us
    scatter x1, local copies, waits for them, and re-layouts, local(): return jnp.zeros_like(leaf_result).at[order_local].set(leaf_result)  12.3 us
    gather x1, local copies, waits for them, and re-layouts, local(): ordered = jnp.take(right_block, order_local, axis=0)  9.4 us
    dot_general x2, matrix products, local(): jnp.dot(factors[height][0], downward, preferred_element_type=jnp.float32)  7.35 us
    dot_general x1, matrix products, local(): jnp.dot(basis_out, downward, preferred_element_type=jnp.float32)  6.59 us
  transfers between devices with their start and end apart: 11, of which 6 were waited for; matrix products, arithmetic and copies ran while one was open for 17% of the time, Pallas kernels for 0%

commit v1 on v0

v1 whole, which is shorter than its diff:
```python
import functools

import jax
import jax.numpy as jnp
from jax import lax
from jax.experimental import pallas as pl
from jax.experimental.pallas import tpu as pltpu
from jax.sharding import PartitionSpec as P

AXES = ("gx", "gy")
F32 = jnp.float32
BF16 = jnp.bfloat16
LEAF = 2048
RANK = 256
NCOL = 768
HALF = NCOL // 2
QUARTER = NCOL // 4
VMEM = pl.BlockSpec(memory_space=pltpu.VMEM)
SMEM = pl.BlockSpec(memory_space=pltpu.SMEM)
ANY = pl.BlockSpec(memory_space=pl.ANY)
MIB = 1 << 20


def permute(array, dx=0, dy=0, turn=0):
    pairs = []
    for gx in range(16):
        for gy in range(8):
            to = ((gx + 4 * turn) % 16) ^ dx
            pairs.append((gx * 8 + gy, to * 8 + (gy ^ dy)))
    return lax.ppermute(array, AXES, pairs)


def nn(a, b):
    return jnp.dot(a, b, preferred_element_type=F32)


def nt(a, b):
    return lax.dot_general(a, b, (((1,), (1,)), ((), ())), preferred_element_type=F32)


def call(kernel, name, outs, in_specs, flops=0, moved=0, scratch=(), limit=16, aliases=None, grid=None, out_specs=None):
    shapes = [jax.ShapeDtypeStruct(*o) for o in outs]
    extra = {} if grid is None else {"grid": grid}
    return pl.pallas_call(
        kernel,
        out_shape=shapes,
        in_specs=in_specs,
        out_specs=[VMEM] * len(outs) if out_specs is None else out_specs,
        scratch_shapes=list(scratch),
        input_output_aliases=aliases or {},
        compiler_params=pltpu.CompilerParams(vmem_limit_bytes=limit * MIB),
        cost_estimate=pl.CostEstimate(flops=flops, bytes_accessed=moved, transcendentals=0),
        name=name,
        **extra,
    )


def picks(order_row, base, rows):
    it = lax.broadcasted_iota(jnp.int32, (rows, LEAF), 0)
    return jnp.where(it == (order_row - base), 1.0, 0.0).astype(BF16)


def front_kernel(pos, order, basis, x_hbm, couple, c0, send, keep, turned, x, lift, sem):
    fetch = pltpu.make_async_copy(x_hbm, x, sem)
    fetch.start()
    for j in range(LEAF // 512):
        block = nn(picks(order[...], j * 512, 512), basis[...]).astype(BF16)
        turned[:, j * 512 : (j + 1) * 512] = block.T
    fetch.wait()
    c = nn(turned[...], x[...]).astype(BF16).T
    c0[...] = c
    lift[...] = nn(c, couple[0]).astype(BF16)
    core = pos[0]
    keep[...] = lift[pl.ds(pl.multiple_of(core * HALF, HALF), HALF), :]
    send[...] = lift[pl.ds(pl.multiple_of((1 - core) * HALF, HALF), HALF), :]


def pair_kernel(pos, keep, recv, send2, keep2, total):
    total[...] = (keep[...].astype(F32) + recv[...].astype(F32)).astype(BF16)
    part = pos[1]
    keep2[...] = total[pl.ds(pl.multiple_of(part * QUARTER, QUARTER), QUARTER), :]
    send2[...] = total[pl.ds(pl.multiple_of((1 - part) * QUARTER, QUARTER), QUARTER), :]


def coarse_kernel(keep, recv, couple, _c0, _order, coef1, lift1, _c0_out):
    c = (keep[...].astype(F32) + recv[...].astype(F32)).astype(BF16)
    coef1[...] = c
    lift1[...] = nn(c, couple[0]).astype(BF16)


def sum_x_kernel(lift1, recv, coef1, _order, pair, coef1_out):
    pair[...] = (lift1[...].astype(F32) + recv[...].astype(F32)).astype(BF16)
    coef1_out[...] = coef1[...]


def sum_z_kernel(pair, recv, coef1, side_x, _order, coef2, both):
    coef2[...] = (pair[...].astype(F32) + recv[...].astype(F32)).astype(BF16)
    both[:QUARTER] = coef1[...]
    both[QUARTER:] = side_x[...]


def pick_top_kernel(pos, top, _order, rows, sems):
    y, z = pos[2], pos[3]
    copies = []
    for d in range(4):
        there = lax.rem(y + d, 4)
        r = pl.multiple_of((there * 2 + z) * RANK, RANK)
        s = pl.multiple_of(y * 2 * RANK, 2 * RANK)
        copies.append(
            pltpu.make_async_copy(top.at[pl.ds(r, RANK), pl.ds(s, 2 * RANK)], rows.at[d], sems.at[d])
        )
    for copy in copies:
        copy.start()
    for copy in copies:
        copy.wait()


def top_kernel(pos, own, other, rows, _order, q0, q1, q2, q3):
    low = pos[3] == 0
    a, b = own[...], other[...]
    zero = jnp.zeros_like(a)
    first = jnp.where(low, a, b)
    second = jnp.where(low, b, a)
    stay = jnp.concatenate([jnp.where(low, zero, b), jnp.where(low, b, zero)], axis=1)
    both = jnp.concatenate([first, second], axis=1)
    q0[...] = nt(stay, rows[0])
    q1[...] = nt(both, rows[1]).astype(BF16)
    q2[...] = nt(both, rows[2]).astype(BF16)
    q3[...] = nt(both, rows[3]).astype(BF16)


def near1_kernel(side_x, sides, couple, _order, near1):
    near1[...] = (
        nt(side_x[...], couple[1]) + nt(sides[:QUARTER], couple[2]) + nt(sides[QUARTER:], couple[3])
    )


def near0_kernel(side_x, side_y, side_xy, couple, _order, near0):
    near0[...] = nt(couple[1], side_x[...]) + nt(couple[2], side_y[...]) + nt(couple[3], side_xy[...])


def down1_kernel(q0, r1, r2, r3, near1, couple, _order, down1):
    d2 = (q0[...] + r1[...].astype(F32) + r2[...].astype(F32) + r3[...].astype(F32)).astype(BF16)
    down1[...] = (near1[...] + nt(d2, couple[0])).astype(BF16)


def gather_kernel(base, block, order, x, _order, out):
    start = base + pl.program_id(0) * block
    rows = []
    for s in range(block // 128):
        row = order[:, pl.ds(pl.multiple_of(start + s * 128, 128), 128)].astype(F32)
        column = jnp.broadcast_to(row, (128, 128)).T
        lane = lax.broadcasted_iota(jnp.int32, (128, 128), 1).astype(F32)
        rows.append(
            jnp.concatenate(
                [jnp.where(column == lane + 128.0 * j, 1.0, 0.0).astype(BF16) for j in range(LEAF // 128)], axis=1
            )
        )
    out[...] = nn(jnp.concatenate(rows, axis=0), x[...]).astype(BF16)


def dense_kernel(dense, upper, lower, _order, out):
    out[...] = (
        nn(dense[:, : LEAF // 2], upper[...]) + nn(dense[:, LEAF // 2 :], lower[...])
    ).astype(BF16)


def scatter_kernel(base, block, order, upper, lower, basis, _order, out, turned):
    hot = picks(order[...], base + pl.program_id(0) * block, block)
    out[...] = (nn(hot[:, : LEAF // 2], upper[...]) + nn(hot[:, LEAF // 2 :], lower[...])).astype(BF16)
    turned[...] = nn(hot, basis[...]).astype(BF16)


def final_kernel(pos, upper, lower, turned_u, turned_l, own, side, core_own, core_side, near0, couple, out, down1, down0):
    step = pl.program_id(0)

    @pl.when(step == 0)
    def _():
        core, part = pos[0], pos[1]
        for which, half, quarter in (
            (own, core, part),
            (side, core, 1 - part),
            (core_own, 1 - core, part),
            (core_side, 1 - core, 1 - part),
        ):
            down1[pl.ds(pl.multiple_of(half * HALF + quarter * QUARTER, QUARTER), QUARTER), :] = which[...]
        down0[...] = (near0[...] + nt(couple[0], down1[...])).astype(BF16)

    @pl.when(step < 4)
    def _():
        out[...] = (upper[...].astype(F32) + nn(turned_u[...], down0[...])).astype(BF16)

    @pl.when(step >= 4)
    def _():
        out[...] = (lower[...].astype(F32) + nn(turned_l[...], down0[...])).astype(BF16)


def fixed(shape):
    return pl.BlockSpec(shape, lambda i: (0,) * len(shape), pipeline_mode=pl.Buffered(1))


def gather_part(base, order, x, after):
    rows, block = LEAF // 2, 512
    return call(
        functools.partial(gather_kernel, base, block),
        "gather",
        [((rows, NCOL), BF16)],
        [fixed((1, LEAF)), fixed((LEAF, NCOL)), ANY],
        flops=2 * rows * LEAF * NCOL,
        moved=5 * MIB,
        limit=20,
        grid=(rows // block,),
        out_specs=[pl.BlockSpec((block, NCOL), lambda i: (i, 0))],
    )(order, x, after)[0]


def dense_part(part, dense, upper, lower, after):
    rows, block = LEAF // 2, 512
    steps = rows // block
    return call(
        dense_kernel,
        "dense",
        [((rows, NCOL), BF16)],
        [
            pl.BlockSpec((block, LEAF), lambda i: (part * steps + i, 0)),
            fixed((LEAF // 2, NCOL)),
            fixed((LEAF // 2, NCOL)),
            ANY,
        ],
        flops=2 * rows * LEAF * NCOL,
        moved=9 * MIB,
        limit=20,
        grid=(steps,),
        out_specs=[pl.BlockSpec((block, NCOL), lambda i: (i, 0))],
    )(dense, upper, lower, after)[0]


def scatter_part(base, order, upper, lower, basis, after):
    rows, block = LEAF // 2, 512
    return call(
        functools.partial(scatter_kernel, base, block),
        "scatter",
        [((rows, NCOL), BF16), ((rows, RANK), BF16)],
        [fixed((1, LEAF)), fixed((LEAF // 2, NCOL)), fixed((LEAF // 2, NCOL)), fixed((LEAF, RANK)), ANY],
        flops=2 * rows * LEAF * (NCOL + RANK),
        moved=7 * MIB,
        limit=20,
        grid=(rows // block,),
        out_specs=[pl.BlockSpec((block, NCOL), lambda i: (i, 0)), pl.BlockSpec((block, RANK), lambda i: (i, 0))],
    )(order, upper, lower, basis, after)


def local(right_block, point_order, leaf_dense, basis_in, basis_out, leaf_couple, coarse_couple, top_coupling):
    order = point_order.reshape(1, LEAF)
    leaf = leaf_couple.reshape(4, RANK, RANK)
    coarse = coarse_couple.reshape(4, RANK, RANK)
    gx = lax.axis_index("gx")
    gy = lax.axis_index("gy")
    pos = jnp.stack([gy % 2, (gx ^ (gx >> 1)) & 1, gx // 4, gy // 4]).astype(jnp.int32)
    quarter = ((QUARTER, RANK), BF16)
    half = ((HALF, RANK), BF16)
    whole = ((NCOL, RANK), BF16)
    small = 2 * QUARTER * RANK * RANK

    c0, send, keep = call(
        front_kernel,
        "front",
        [whole, half, half],
        [SMEM, VMEM, VMEM, ANY, VMEM],
        flops=2 * LEAF * LEAF * RANK + 2 * LEAF * RANK * NCOL,
        moved=5 * MIB,
        scratch=[
            pltpu.VMEM((RANK, LEAF), BF16),
            pltpu.VMEM((LEAF, NCOL), BF16),
            pltpu.VMEM((NCOL, RANK), BF16),
            pltpu.SemaphoreType.DMA,
        ],
        limit=24,
    )(pos, order, basis_in, right_block, leaf)
    recv = permute(send, dy=1)
    rows = call(
        pick_top_kernel,
        "pick_top",
        [((4, RANK, 2 * RANK), BF16)],
        [SMEM, ANY, ANY],
        moved=2 * MIB,
        scratch=[pltpu.SemaphoreType.DMA((4,))],
    )(pos, top_coupling, send)[0]

    send2, keep2 = call(
        pair_kernel, "pair", [quarter, quarter], [SMEM, VMEM, VMEM], scratch=[pltpu.VMEM((HALF, RANK), BF16)]
    )(pos, keep, recv)
    recv2 = permute(send2, dx=1)
    ordered_u = gather_part(0, order, right_block, send2)

    coef1, lift1, c0 = call(
        coarse_kernel,
        "coarse",
        [quarter, quarter, whole],
        [VMEM, VMEM, VMEM, ANY, ANY],
        flops=small,
        aliases={3: 2},
        out_specs=[VMEM, VMEM, ANY],
    )(keep2, recv2, coarse, c0, ordered_u)
    recv3 = permute(lift1, dx=3)
    side_y = permute(c0, dy=1)
    side_x = permute(c0, dx=1)
    side_xy = permute(side_x, dy=1)
    ordered_l = gather_part(LEAF // 2, order, right_block, lift1)

    pair, coef1 = call(sum_x_kernel, "sum_x", [quarter, quarter], [VMEM, VMEM, VMEM, ANY])(
        lift1, recv3, coef1, ordered_l
    )
    recv4 = permute(pair, dy=2)
    coarse_x = permute(coef1, dx=3)
    dense_u = dense_part(0, leaf_dense, ordered_u, ordered_l, pair)

    coef2, both = call(sum_z_kernel, "sum_z", [quarter, half], [VMEM, VMEM, VMEM, VMEM, ANY])(
        pair, recv4, coef1, coarse_x, dense_u
    )
    recv5 = permute(coef2, dy=6)
    coarse_yz = permute(both, dy=2)
    dense_l = dense_part(1, leaf_dense, ordered_u, ordered_l, coef2)

    q0, q1, q2, q3 = call(
        top_kernel,
        "top",
        [((QUARTER, RANK), F32), quarter, quarter, quarter],
        [SMEM, VMEM, VMEM, VMEM, ANY],
        flops=8 * small,
    )(pos, coef2, recv5, rows, dense_l)
    r2 = permute(q2, turn=2)
    r1 = permute(q1, turn=1)
    r3 = permute(q3, turn=3)
    out_u, turned_u = scatter_part(0, order, dense_u, dense_l, basis_out, q3)
    near1 = call(near1_kernel, "near1", [((QUARTER, RANK), F32)], [VMEM, VMEM, VMEM, ANY], flops=3 * small)(
        coarse_x, coarse_yz, coarse, q3
    )[0]

    down1 = call(down1_kernel, "down1", [quarter], [VMEM] * 6 + [ANY], flops=small)(
        q0, r1, r2, r3, near1, coarse, out_u
    )[0]
    side = permute(down1, dx=1)
    core_own = permute(down1, dy=1)
    core_side = permute(side, dy=1)
    out_l, turned_l = scatter_part(LEAF // 2, order, dense_u, dense_l, basis_out, down1)
    near0 = call(
        near0_kernel, "near0", [((RANK, NCOL), F32)], [VMEM] * 4 + [ANY], flops=12 * small
    )(side_x, side_y, side_xy, leaf, down1)[0]

    block = 256
    return call(
        final_kernel,
        "final",
        [((LEAF, NCOL), BF16)],
        [
            SMEM,
            pl.BlockSpec((block, NCOL), lambda i: (jnp.minimum(i, 3), 0)),
            pl.BlockSpec((block, NCOL), lambda i: (jnp.maximum(i - 4, 0), 0)),
            pl.BlockSpec((block, RANK), lambda i: (jnp.minimum(i, 3), 0)),
            pl.BlockSpec((block, RANK), lambda i: (jnp.maximum(i - 4, 0), 0)),
            fixed((QUARTER, RANK)),
            fixed((QUARTER, RANK)),
            fixed((QUARTER, RANK)),
            fixed((QUARTER, RANK)),
            fixed((RANK, NCOL)),
            fixed((1, RANK, RANK)),
        ],
        flops=2 * LEAF * RANK * NCOL,
        moved=8 * MIB,
        scratch=[pltpu.VMEM((NCOL, RANK), BF16), pltpu.VMEM((RANK, NCOL), BF16)],
        grid=(LEAF // block,),
        out_specs=[pl.BlockSpec((block, NCOL), lambda i: (i, 0))],
    )(pos, out_u, out_l, turned_u, turned_l, down1, side, core_own, core_side, near0, leaf)[0]


def solution(mesh):
    in_specs = (
        P(("gx", "gy"), None),
        P("gx", "gy", None),
        P(("gx", "gy"), None),
        P(("gx", "gy"), None),
        P(("gx", "gy"), None),
        P("gx", "gy", None, None, None),
        P("gx", "gy", None, None, None),
        P(),
    )
    out_specs = P(("gx", "gy"), None)
    return jax.shard_map(local, mesh=mesh, in_specs=in_specs, out_specs=out_specs, check_vma=False)
```

time: 175 us -> 68.8 us (0.39)
  waiting for transfers between devices: 69.9 us -> 0.42 us
  matrix products: 38.7 us -> 0 us
  Pallas kernels: 0 us -> 38.1 us
  local copies, waits for them, and re-layouts: 28.9 us -> 4.9 us
  between operations: 13.5 us -> 0.27 us
  starting transfers between devices: 17.2 us -> 24.8 us
  other arithmetic: 6.19 us -> 0.08 us
    dot_general x11 -> x0, matrix products: 38.7 us -> none  [the longest x1 12.7 us: local(): jnp.dot(leaf_dense, ordered, preferred_element_type=jnp.float32)]
    pallas_call x0 -> x17, Pallas kernels: none -> 38.1 us  [the longest x2 9.47 us: scatter_part(): call(functools.partial(scatter_kernel, base, block), 'scatter', [((rows,...]
    all_gather x1 -> x0, waiting for transfers between devices: 37.9 us -> none  [local(): gathered = lax.all_gather(portion, ('gx', 'gy'), axis=0, tiled=True)]
    ppermute x10 -> x16, waiting for transfers between devices: 31.9 us -> 0.42 us  [permute(): return lax.ppermute(array, AXES, pairs)]
    scatter x1 -> x0, local copies, waits for them, and re-layouts: 12.3 us -> none  [local(): return jnp.zeros_like(leaf_result).at[order_local].set(leaf_result)]
    gather x1 -> x0, local copies, waits for them, and re-layouts: 9.4 us -> none  [local(): ordered = jnp.take(right_block, order_local, axis=0)]
    ppermute x10 -> x16, starting transfers between devices: 17.2 us -> 24.8 us  [permute(): return lax.ppermute(array, AXES, pairs)]
    convert_element_type x1 -> x0, local copies, waits for them, and re-layouts: 4.67 us -> none  [local(): leaf_result = (local_term + jnp.dot(basis_out, downward, preferred_elemen...]
  transfers between devices with their start and end apart: 11 -> 16, of which waited for: 6 -> 1; matrix products, arithmetic and copies ran while one was open for 17% -> 0% of each run, Pallas kernels for 0% -> 39%
where the time goes in v1:
time: 68.8 us; the launch traced here: 68.5 us
  Pallas kernels  38.1 us (55%)
  starting transfers between devices  24.8 us (36%)
  local copies, waits for them, and re-layouts  4.9 us (7%)
    ppermute x16, starting transfers between devices, permute(): return lax.ppermute(array, AXES, pairs)  24.8 us
    pallas_call x2, Pallas kernels, scatter_part(): call(functools.partial(scatter_kernel, base, block), 'scatter', [((rows,...  9.47 us
    pallas_call x2, Pallas kernels, gather_part(): call(functools.partial(gather_kernel, base, block), 'gather', [((rows, NC...  7.43 us
    pallas_call x2, Pallas kernels, dense_part(): call(dense_kernel, 'dense', [((rows, NCOL), BF16)], [pl.BlockSpec((block,...  7.33 us
    pallas_call x1, Pallas kernels, local(): call(final_kernel, 'final', [((LEAF, NCOL), BF16)], [SMEM, pl.BlockSpec((...  5.39 us
    unnamed x24, local copies, waits for them, and re-layouts  4.9 us
    pallas_call x1, Pallas kernels, local(): call(front_kernel, 'front', [whole, half, half], [SMEM, VMEM, VMEM, ANY,...  4.82 us
  transfers between devices with their start and end apart: 16, of which 1 were waited for; matrix products, arithmetic and copies ran while one was open for 0% of the time, Pallas kernels for 39%

profile of v1, /device:TPU:1, one launch (start us, length us, event | category | flops | bytes accessed | tf_op | source)
XLA Modules:
  0.0 68.5 jit_solution(14344843187973377741)
XLA Ops:
  0.1 1.0 %copy-done.2 = bf16[1,1,4,256,256]{4,3,2,1,0:T(8,128)(2,1)S(1)} copy-done((bf16[1,1,4,256,256]{4,3,2,1,0:T(8,128)(2,1)S(1)}, bf16[1,1,4,256,256]{4,3,2,1,0:T(8,128)(2,1)}, u32[]{:S(2)}) %copy-start.2) | copy-done | bytes 524312
  1.1 1.9 %copy-done.4 = bf16[2048,768]{1,0:T(8,128)(2,1)S(1)} copy-done((bf16[2048,768]{1,0:T(8,128)(2,1)S(1)}, bf16[2048,768]{1,0:T(8,128)(2,1)}, u32[]{:S(2)}) %copy-start.4) | copy-done | bytes 3145752
  3.0 1.2 %copy-done.6 = bf16[2048,256]{1,0:T(8,128)(2,1)S(1)} copy-done((bf16[2048,256]{1,0:T(8,128)(2,1)S(1)}, bf16[2048,256]{1,0:T(8,128)(2,1)}, u32[]{:S(2)}) %copy-start.6) | copy-done | bytes 1048600
  4.9 4.8 %front.1 = (bf16[768,256]{1,0:T(8,128)(2,1)S(1)}, bf16[384,256]{1,0:T(8,128)(2,1)S(1)}, bf16[384,256]{1,0:T(8,128)(2,1)S(1)}) custom-call(s32[4]{0:T(128)S(1)} %pad_add_fusion.pos, s32[1,2048]{1,0:T(1,128)S(1)} %bitcast.15, bf16[2048,256]{1,0:T(8,128)(2,1)S(1)} %copy-done.6, bf16[2048,768]{1,0:T(8,128)(2,1)S(1)} %copy-done.4, bf16[4,256,256]{2,1,0:T(8,128)(2,1)S(1)} %bitcast.12), custom_call_target="tpu_custom_call" | custom-call | flops 2952790016 | bytes 5242880 | tf_op jit(solution)/shard_map/front/pallas_call | solution.py:265
  9.8 1.5 %collective-permute-start = (bf16[384,256]{1,0:T(8,128)(2,1)S(1)}, bf16[384,256]{1,0:T(8,128)(2,1)S(1)}, u32[]{:S(2)}, u32[]{:S(2)}) collective-permute-start(bf16[384,256]{1,0:T(8,128)(2,1)S(1)} %get-tuple-element.26._order), channel_id=1, source_target_pairs={{0,1},{1,0},{2,3},{3,2},{4,5},{5,4},{6,7},{7,6},{8,9},{9,8},{10,11... | collective-permute-start | bytes 589832 | tf_op jit(solution)/shard_map/ppermute | solution.py:30
  13.0 1.4 %collective-permute-start.1 = (bf16[192,256]{1,0:T(8,128)(2,1)S(1)}, bf16[192,256]{1,0:T(8,128)(2,1)S(1)}, u32[]{:S(2)}, u32[]{:S(2)}) collective-permute-start(bf16[192,256]{1,0:T(8,128)(2,1)S(1)} %get-tuple-element.27._order), channel_id=1, source_target_pairs={{0,8},{1,9},{2,10},{3,11},{4,12},{5,13},{6,14},{7,15},{8,0},{9,1},... | collective-permute-start | bytes 294920 | tf_op jit(solution)/shard_map/ppermute | solution.py:30
  14.4 3.7 %gather.2._order.upper = bf16[1024,768]{1,0:T(8,128)(2,1)S(1)} custom-call(s32[1,2048]{1,0:T(1,128)S(1)} %bitcast.16, bf16[2048,768]{1,0:T(8,128)(2,1)S(1)} %copy-done.5, bf16[192,256]{1,0:T(8,128)(2,1)S(1)} %get-tuple-element.27._order), custom_call_target="tpu_custom_call" | custom-call | flops 3221225472 | bytes 5242880 | tf_op jit(solution)/shard_map/gather/pallas_call | solution.py:204
  18.3 1.9 %collective-permute-start.2 = (bf16[192,256]{1,0:T(8,128)(2,1)S(1)}, bf16[192,256]{1,0:T(8,128)(2,1)S(1)}, u32[]{:S(2)}, u32[]{:S(2)}) collective-permute-start(bf16[192,256]{1,0:T(8,128)(2,1)S(1)} %get-tuple-element.30._order.lift1), channel_id=1, source_target_pairs={{0,24},{1,25},{2,26},{3,27},{4,28},{5,29},{6,30},{7,31},{8,16},{9,... | collective-permute-start | bytes 294920 | tf_op jit(solution)/shard_map/ppermute | solution.py:30
  20.2 3.7 %gather.3._order.lower = bf16[1024,768]{1,0:T(8,128)(2,1)S(1)} custom-call(s32[1,2048]{1,0:T(1,128)S(1)} %bitcast.17, bf16[2048,768]{1,0:T(8,128)(2,1)S(1)} %copy-done.5, bf16[192,256]{1,0:T(8,128)(2,1)S(1)} %get-tuple-element.30._order.lift1), custom_call_target="tpu_custom_call" | custom-call | flops 3221225472 | bytes 5242880 | tf_op jit(solution)/shard_map/gather/pallas_call | solution.py:204
  24.4 1.7 %collective-permute-start.3 = (bf16[192,256]{1,0:T(8,128)(2,1)S(1)}, bf16[192,256]{1,0:T(8,128)(2,1)S(1)}, u32[]{:S(2)}, u32[]{:S(2)}) collective-permute-start(bf16[192,256]{1,0:T(8,128)(2,1)S(1)} %get-tuple-element.32._order.pair), channel_id=1, source_target_pairs={{0,2},{1,3},{2,0},{3,1},{4,6},{5,7},{6,4},{7,5},{8,10},{9,11},{10,... | collective-permute-start | bytes 294920 | tf_op jit(solution)/shard_map/ppermute | solution.py:30
  26.1 1.0 %collective-permute-start.4 = (bf16[192,256]{1,0:T(8,128)(2,1)S(1)}, bf16[192,256]{1,0:T(8,128)(2,1)S(1)}, u32[]{:S(2)}, u32[]{:S(2)}) collective-permute-start(bf16[192,256]{1,0:T(8,128)(2,1)S(1)} %get-tuple-element.33.coef1), channel_id=1, source_target_pairs={{0,24},{1,25},{2,26},{3,27},{4,28},{5,29},{6,30},{7,31},{8,16},{9,... | collective-permute-start | bytes 294920 | tf_op jit(solution)/shard_map/ppermute | solution.py:30
  27.1 3.7 %dense.4._order.upper = bf16[1024,768]{1,0:T(8,128)(2,1)S(1)} custom-call(bf16[2048,2048]{1,0:T(8,128)(2,1)S(1)} %bitcast.8, bf16[1024,768]{1,0:T(8,128)(2,1)S(1)} %gather.2._order.upper, bf16[1024,768]{1,0:T(8,128)(2,1)S(1)} %gather.3._order.lower, bf16[192,256]{1,0:T(8,128)(2,1)S(1)} %get-tuple-element.32._order.pair), custom_call_target="tpu_custom_call" | custom-call | flops 3221225472 | bytes 9437184 | tf_op jit(solution)/shard_map/dense/pallas_call | solution.py:220
  30.8 2.3 %collective-permute-start.5 = (bf16[192,256]{1,0:T(8,128)(2,1)S(1)}, bf16[192,256]{1,0:T(8,128)(2,1)S(1)}, u32[]{:S(2)}, u32[]{:S(2)}) collective-permute-start(bf16[192,256]{1,0:T(8,128)(2,1)S(1)} %get-tuple-element.34._order.own), channel_id=1, source_target_pairs={{0,6},{1,7},{2,4},{3,5},{4,2},{5,3},{6,0},{7,1},{8,14},{9,15},{10,... | collective-permute-start | bytes 294920 | tf_op jit(solution)/shard_map/ppermute | solution.py:30
  33.1 3.7 %dense.6._order.lower = bf16[1024,768]{1,0:T(8,128)(2,1)S(1)} custom-call(bf16[2048,2048]{1,0:T(8,128)(2,1)S(1)} %bitcast.8, bf16[1024,768]{1,0:T(8,128)(2,1)S(1)} %gather.2._order.upper, bf16[1024,768]{1,0:T(8,128)(2,1)S(1)} %gather.3._order.lower, bf16[192,256]{1,0:T(8,128)(2,1)S(1)} %get-tuple-element.34._order.own), custom_call_target="tpu_custom_call" | custom-call | flops 3221225472 | bytes 9437184 | tf_op jit(solution)/shard_map/dense/pallas_call | solution.py:220
  36.8 0.8 %collective-permute-start.9 = (bf16[384,256]{1,0:T(8,128)(2,1)S(1)}, bf16[384,256]{1,0:T(8,128)(2,1)S(1)}, u32[]{:S(2)}, u32[]{:S(2)}) collective-permute-start(bf16[384,256]{1,0:T(8,128)(2,1)S(1)} %get-tuple-element.40), channel_id=1, source_target_pairs={{0,2},{1,3},{2,0},{3,1},{4,6},{5,7},{6,4},{7,5},{8,10},{9,11},{10,... | collective-permute-start | bytes 589832 | tf_op jit(solution)/shard_map/ppermute | solution.py:30
  37.6 1.0 %top.3 = (f32[192,256]{1,0:T(8,128)S(1)}, bf16[192,256]{1,0:T(8,128)(2,1)S(1)}, bf16[192,256]{1,0:T(8,128)(2,1)S(1)}, bf16[192,256]{1,0:T(8,128)(2,1)S(1)}) custom-call(s32[4]{0:T(128)S(1)} %pad_add_fusion.pos, bf16[192,256]{1,0:T(8,128)(2,1)S(1)} %get-tuple-element.34._order.own, bf16[192,256]{1,0:T(8,128)(2,1)S(1)} %collective-permute-done.5.other, ...), custom_call_target="tpu_custom_call" | custom-call | flops 201326592 | tf_op jit(solution)/shard_map/top/pallas_call | solution.py:325
  38.7 1.4 %collective-permute-start.6 = (bf16[192,256]{1,0:T(8,128)(2,1)S(1)}, bf16[192,256]{1,0:T(8,128)(2,1)S(1)}, u32[]{:S(2)}, u32[]{:S(2)}) collective-permute-start(bf16[192,256]{1,0:T(8,128)(2,1)S(1)} %get-tuple-element.38), channel_id=1, source_target_pairs={{0,32},{1,33},{2,34},{3,35},{4,36},{5,37},{6,38},{7,39},{8,40},{9,... | collective-permute-start | bytes 294920 | tf_op jit(solution)/shard_map/ppermute | solution.py:30
  40.1 2.6 %collective-permute-start.7 = (bf16[192,256]{1,0:T(8,128)(2,1)S(1)}, bf16[192,256]{1,0:T(8,128)(2,1)S(1)}, u32[]{:S(2)}, u32[]{:S(2)}) collective-permute-start(bf16[192,256]{1,0:T(8,128)(2,1)S(1)} %get-tuple-element.39), channel_id=1, source_target_pairs={{0,64},{1,65},{2,66},{3,67},{4,68},{5,69},{6,70},{7,71},{8,72},{9,... | collective-permute-start | bytes 294920 | tf_op jit(solution)/shard_map/ppermute | solution.py:30
  42.7 1.1 %collective-permute-start.8 = (bf16[192,256]{1,0:T(8,128)(2,1)S(1)}, bf16[192,256]{1,0:T(8,128)(2,1)S(1)}, u32[]{:S(2)}, u32[]{:S(2)}) collective-permute-start(bf16[192,256]{1,0:T(8,128)(2,1)S(1)} %get-tuple-element.35._order), channel_id=1, source_target_pairs={{0,96},{1,97},{2,98},{3,99},{4,100},{5,101},{6,102},{7,103},{8,104... | collective-permute-start | bytes 294920 | tf_op jit(solution)/shard_map/ppermute | solution.py:30
  43.8 4.7 %scatter.2 = (bf16[1024,768]{1,0:T(8,128)(2,1)S(1)}, bf16[1024,256]{1,0:T(8,128)(2,1)S(1)}) custom-call(s32[1,2048]{1,0:T(1,128)S(1)} %bitcast.18, bf16[1024,768]{1,0:T(8,128)(2,1)S(1)} %dense.4._order.upper, bf16[1024,768]{1,0:T(8,128)(2,1)S(1)} %dense.6._order.lower, bf16[2048,256]{1,0:T(8,128)(2,1)S(1)} %copy-done.7, ...), custom_call_target="tpu_custom_call" | custom-call | flops 4294967296 | bytes 7340032 | tf_op jit(solution)/shard_map/scatter/pallas_call | solution.py:240
  49.6 4.1 %collective-permute-start.14 = (bf16[768,256]{1,0:T(8,128)(2,1)S(1)}, bf16[768,256]{1,0:T(8,128)(2,1)S(1)}, u32[]{:S(2)}, u32[]{:S(2)}) collective-permute-start(bf16[768,256]{1,0:T(8,128)(2,1)S(1)} %get-tuple-element.44), channel_id=1, source_target_pairs={{0,1},{1,0},{2,3},{3,2},{4,5},{5,4},{6,7},{7,6},{8,9},{9,8},{10,11... | collective-permute-start | bytes 1179656 | tf_op jit(solution)/shard_map/ppermute | solution.py:30
  54.2 3.6 %collective-permute-start.12 = (bf16[192,256]{1,0:T(8,128)(2,1)S(1)}, bf16[192,256]{1,0:T(8,128)(2,1)S(1)}, u32[]{:S(2)}, u32[]{:S(2)}) collective-permute-start(bf16[192,256]{1,0:T(8,128)(2,1)S(1)} %collective-permute-done.10.side), channel_id=1, source_target_pairs={{0,1},{1,0},{2,3},{3,2},{4,5},{5,4},{6,7},{7,6},{8,9},{9,8},{10,11... | collective-permute-start | bytes 294920 | tf_op jit(solution)/shard_map/ppermute | solution.py:30
  57.8 4.7 %scatter.3 = (bf16[1024,768]{1,0:T(8,128)(2,1)S(1)}, bf16[1024,256]{1,0:T(8,128)(2,1)S(1)}) custom-call(s32[1,2048]{1,0:T(1,128)S(1)} %bitcast.19, bf16[1024,768]{1,0:T(8,128)(2,1)S(1)} %dense.4._order.upper, bf16[1024,768]{1,0:T(8,128)(2,1)S(1)} %dense.6._order.lower, bf16[2048,256]{1,0:T(8,128)(2,1)S(1)} %copy-done.7, bf16[192,256]{1,0:T(8,128)(2,1)S(1)} %down1.1._order.own), custom_call_target="tpu_custom_call" | custom-call | flops 4294967296 | bytes 7340032 | tf_op jit(solution)/shard_map/scatter/pallas_call | solution.py:240
  63.1 5.4 %final.1 = bf16[2048,768]{1,0:T(8,128)(2,1)} custom-call(s32[4]{0:T(128)S(1)} %pad_add_fusion.pos, bf16[1024,768]{1,0:T(8,128)(2,1)S(1)} %get-tuple-element.36._order.upper, bf16[1024,768]{1,0:T(8,128)(2,1)S(1)} %get-tuple-element.41.lower, bf16[1024,256]{1,0:T(8,128)(2,1)S(1)} %get-tuple-element.42.turned_u, ...), custom_call_target="tpu_custom_call" | custom-call | flops 805306368 | bytes 8388608 | tf_op jit(solution)/shard_map/final/pallas_call | solution.py:352
  (51 shorter events, 5.2 us)
Async XLA Ops:
  4.9 6.3 %copy-start = (bf16[2048,2048]{1,0:T(8,128)(2,1)S(1)}, bf16[2048,2048]{1,0:T(8,128)(2,1)}, u32[]{:S(2)}) copy-start(bf16[2048,2048]{1,0:T(8,128)(2,1)} %top.2) | copy-start | bytes 25165828
  9.8 4.6 %copy-start.5 = (bf16[2048,768]{1,0:T(8,128)(2,1)S(1)}, bf16[2048,768]{1,0:T(8,128)(2,1)}, u32[]{:S(2)}) copy-start(bf16[2048,768]{1,0:T(8,128)(2,1)} %x.3) | copy-start | bytes 9437188
  9.8 2.6 %collective-permute-start = (bf16[384,256]{1,0:T(8,128)(2,1)S(1)}, bf16[384,256]{1,0:T(8,128)(2,1)S(1)}, u32[]{:S(2)}, u32[]{:S(2)}) collective-permute-start(bf16[384,256]{1,0:T(8,128)(2,1)S(1)} %get-tuple-element.26._order), channel_id=1, source_target_pairs={{0,1},{1,0},{2,3},{3,2},{4,5},{5,4},{6,7},{7,6},{8,9},{9,8},{10,11... | collective-permute-start | bytes 589832 | tf_op jit(solution)/shard_map/ppermute | solution.py:30
  13.0 5.1 %copy-start.1 = (bf16[1,1,4,256,256]{4,3,2,1,0:T(8,128)(2,1)S(1)}, bf16[1,1,4,256,256]{4,3,2,1,0:T(8,128)(2,1)}, u32[]{:S(2)}) copy-start(bf16[1,1,4,256,256]{4,3,2,1,0:T(8,128)(2,1)} %param.14) | copy-start | bytes 1572868
  13.0 5.1 %collective-permute-start.1 = (bf16[192,256]{1,0:T(8,128)(2,1)S(1)}, bf16[192,256]{1,0:T(8,128)(2,1)S(1)}, u32[]{:S(2)}, u32[]{:S(2)}) collective-permute-start(bf16[192,256]{1,0:T(8,128)(2,1)S(1)} %get-tuple-element.27._order), channel_id=1, source_target_pairs={{0,8},{1,9},{2,10},{3,11},{4,12},{5,13},{6,14},{7,15},{8,0},{9,1},... | collective-permute-start | bytes 294920 | tf_op jit(solution)/shard_map/ppermute | solution.py:30
  18.1 2.1 %copy-start.9 = (s32[1,1,2048]{2,1,0:T(1,128)S(1)}, s32[1,1,2048]{2,1,0:T(1,128)}, u32[]{:S(2)}) copy-start(s32[1,1,2048]{2,1,0:T(1,128)} %param.9) | copy-start | bytes 24580
  18.1 9.0 %slice-start = ((s8[8388608]{0:T(1024)(128)(4,1)}), s8[4194304]{0:T(1024)(128)(4,1)S(1)}, s32[]{:S(2)}) async-start(s8[8388608]{0:T(1024)(128)(4,1)} %bitcast.7), calls=%async_computation | async-start | bytes 8388608
  18.3 8.8 %slice-start.1 = ((s8[8388608]{0:T(1024)(128)(4,1)}), s8[4194304]{0:T(1024)(128)(4,1)S(1)}, s32[]{:S(2)}) async-start(s8[8388608]{0:T(1024)(128)(4,1)} %bitcast.7), calls=%async_computation.1 | async-start | bytes 8388608
  18.3 6.0 %collective-permute-start.2 = (bf16[192,256]{1,0:T(8,128)(2,1)S(1)}, bf16[192,256]{1,0:T(8,128)(2,1)S(1)}, u32[]{:S(2)}, u32[]{:S(2)}) collective-permute-start(bf16[192,256]{1,0:T(8,128)(2,1)S(1)} %get-tuple-element.30._order.lift1), channel_id=1, source_target_pairs={{0,24},{1,25},{2,26},{3,27},{4,28},{5,29},{6,30},{7,31},{8,16},{9,... | collective-permute-start | bytes 294920 | tf_op jit(solution)/shard_map/ppermute | solution.py:30
  24.0 29.7 %collective-permute-start.13 = (bf16[768,256]{1,0:T(8,128)(2,1)S(1)}, bf16[768,256]{1,0:T(8,128)(2,1)S(1)}, u32[]{:S(2)}, u32[]{:S(2)}) collective-permute-start(bf16[768,256]{1,0:T(8,128)(2,1)S(1)} %get-tuple-element.44), channel_id=1, source_target_pairs={{0,8},{1,9},{2,10},{3,11},{4,12},{5,13},{6,14},{7,15},{8,0},{9,1},... | collective-permute-start | bytes 1179656 | tf_op jit(solution)/shard_map/ppermute | solution.py:30
  24.4 6.4 %collective-permute-start.3 = (bf16[192,256]{1,0:T(8,128)(2,1)S(1)}, bf16[192,256]{1,0:T(8,128)(2,1)S(1)}, u32[]{:S(2)}, u32[]{:S(2)}) collective-permute-start(bf16[192,256]{1,0:T(8,128)(2,1)S(1)} %get-tuple-element.32._order.pair), channel_id=1, source_target_pairs={{0,2},{1,3},{2,0},{3,1},{4,6},{5,7},{6,4},{7,5},{8,10},{9,11},{10,... | collective-permute-start | bytes 294920 | tf_op jit(solution)/shard_map/ppermute | solution.py:30
  26.1 4.7 %collective-permute-start.4 = (bf16[192,256]{1,0:T(8,128)(2,1)S(1)}, bf16[192,256]{1,0:T(8,128)(2,1)S(1)}, u32[]{:S(2)}, u32[]{:S(2)}) collective-permute-start(bf16[192,256]{1,0:T(8,128)(2,1)S(1)} %get-tuple-element.33.coef1), channel_id=1, source_target_pairs={{0,24},{1,25},{2,26},{3,27},{4,28},{5,29},{6,30},{7,31},{8,16},{9,... | collective-permute-start | bytes 294920 | tf_op jit(solution)/shard_map/ppermute | solution.py:30
  30.8 6.8 %collective-permute-start.5 = (bf16[192,256]{1,0:T(8,128)(2,1)S(1)}, bf16[192,256]{1,0:T(8,128)(2,1)S(1)}, u32[]{:S(2)}, u32[]{:S(2)}) collective-permute-start(bf16[192,256]{1,0:T(8,128)(2,1)S(1)} %get-tuple-element.34._order.own), channel_id=1, source_target_pairs={{0,6},{1,7},{2,4},{3,5},{4,2},{5,3},{6,0},{7,1},{8,14},{9,15},{10,... | collective-permute-start | bytes 294920 | tf_op jit(solution)/shard_map/ppermute | solution.py:30
  36.8 6.9 %copy-start.7 = (bf16[2048,256]{1,0:T(8,128)(2,1)S(1)}, bf16[2048,256]{1,0:T(8,128)(2,1)}, u32[]{:S(2)}) copy-start(bf16[2048,256]{1,0:T(8,128)(2,1)} %basis.5) | copy-start | bytes 3145732
  36.8 11.7 %collective-permute-start.9 = (bf16[384,256]{1,0:T(8,128)(2,1)S(1)}, bf16[384,256]{1,0:T(8,128)(2,1)S(1)}, u32[]{:S(2)}, u32[]{:S(2)}) collective-permute-start(bf16[384,256]{1,0:T(8,128)(2,1)S(1)} %get-tuple-element.40), channel_id=1, source_target_pairs={{0,2},{1,3},{2,0},{3,1},{4,6},{5,7},{6,4},{7,5},{8,10},{9,11},{10,... | collective-permute-start | bytes 589832 | tf_op jit(solution)/shard_map/ppermute | solution.py:30
  38.7 10.1 %collective-permute-start.6 = (bf16[192,256]{1,0:T(8,128)(2,1)S(1)}, bf16[192,256]{1,0:T(8,128)(2,1)S(1)}, u32[]{:S(2)}, u32[]{:S(2)}) collective-permute-start(bf16[192,256]{1,0:T(8,128)(2,1)S(1)} %get-tuple-element.38), channel_id=1, source_target_pairs={{0,32},{1,33},{2,34},{3,35},{4,36},{5,37},{6,38},{7,39},{8,40},{9,... | collective-permute-start | bytes 294920 | tf_op jit(solution)/shard_map/ppermute | solution.py:30
  40.1 8.8 %collective-permute-start.7 = (bf16[192,256]{1,0:T(8,128)(2,1)S(1)}, bf16[192,256]{1,0:T(8,128)(2,1)S(1)}, u32[]{:S(2)}, u32[]{:S(2)}) collective-permute-start(bf16[192,256]{1,0:T(8,128)(2,1)S(1)} %get-tuple-element.39), channel_id=1, source_target_pairs={{0,64},{1,65},{2,66},{3,67},{4,68},{5,69},{6,70},{7,71},{8,72},{9,... | collective-permute-start | bytes 294920 | tf_op jit(solution)/shard_map/ppermute | solution.py:30
  42.7 6.1 %collective-permute-start.8 = (bf16[192,256]{1,0:T(8,128)(2,1)S(1)}, bf16[192,256]{1,0:T(8,128)(2,1)S(1)}, u32[]{:S(2)}, u32[]{:S(2)}) collective-permute-start(bf16[192,256]{1,0:T(8,128)(2,1)S(1)} %get-tuple-element.35._order), channel_id=1, source_target_pairs={{0,96},{1,97},{2,98},{3,99},{4,100},{5,101},{6,102},{7,103},{8,104... | collective-permute-start | bytes 294920 | tf_op jit(solution)/shard_map/ppermute | solution.py:30
  49.1 13.5 %copy-start.3 = (bf16[1,1,4,256,256]{4,3,2,1,0:T(8,128)(2,1)S(1)}, bf16[1,1,4,256,256]{4,3,2,1,0:T(8,128)(2,1)}, u32[]{:S(2)}) copy-start(bf16[1,1,4,256,256]{4,3,2,1,0:T(8,128)(2,1)} %param.13) | copy-start | bytes 1572868
  49.1 5.1 %collective-permute-start.10 = (bf16[192,256]{1,0:T(8,128)(2,1)S(1)}, bf16[192,256]{1,0:T(8,128)(2,1)S(1)}, u32[]{:S(2)}, u32[]{:S(2)}) collective-permute-start(bf16[192,256]{1,0:T(8,128)(2,1)S(1)} %down1.1._order.own), channel_id=1, source_target_pairs={{0,8},{1,9},{2,10},{3,11},{4,12},{5,13},{6,14},{7,15},{8,0},{9,1},... | collective-permute-start | bytes 294920 | tf_op jit(solution)/shard_map/ppermute | solution.py:30
  49.6 13.0 %collective-permute-start.14 = (bf16[768,256]{1,0:T(8,128)(2,1)S(1)}, bf16[768,256]{1,0:T(8,128)(2,1)S(1)}, u32[]{:S(2)}, u32[]{:S(2)}) collective-permute-start(bf16[768,256]{1,0:T(8,128)(2,1)S(1)} %get-tuple-element.44), channel_id=1, source_target_pairs={{0,1},{1,0},{2,3},{3,2},{4,5},{5,4},{6,7},{7,6},{8,9},{9,8},{10,11... | collective-permute-start | bytes 1179656 | tf_op jit(solution)/shard_map/ppermute | solution.py:30
  53.7 9.4 %collective-permute-start.11 = (bf16[192,256]{1,0:T(8,128)(2,1)S(1)}, bf16[192,256]{1,0:T(8,128)(2,1)S(1)}, u32[]{:S(2)}, u32[]{:S(2)}) collective-permute-start(bf16[192,256]{1,0:T(8,128)(2,1)S(1)} %down1.1._order.own), channel_id=1, source_target_pairs={{0,1},{1,0},{2,3},{3,2},{4,5},{5,4},{6,7},{7,6},{8,9},{9,8},{10,11... | collective-permute-start | bytes 294920 | tf_op jit(solution)/shard_map/ppermute | solution.py:30
  53.7 8.9 %collective-permute-start.15 = (bf16[768,256]{1,0:T(8,128)(2,1)S(1)}, bf16[768,256]{1,0:T(8,128)(2,1)S(1)}, u32[]{:S(2)}, u32[]{:S(2)}) collective-permute-start(bf16[768,256]{1,0:T(8,128)(2,1)S(1)} %collective-permute-done.13.side_x), channel_id=1, source_target_pairs={{0,1},{1,0},{2,3},{3,2},{4,5},{5,4},{6,7},{7,6},{8,9},{9,8},{10,11... | collective-permute-start | bytes 1179656 | tf_op jit(solution)/shard_map/ppermute | solution.py:30
  54.2 8.9 %collective-permute-start.12 = (bf16[192,256]{1,0:T(8,128)(2,1)S(1)}, bf16[192,256]{1,0:T(8,128)(2,1)S(1)}, u32[]{:S(2)}, u32[]{:S(2)}) collective-permute-start(bf16[192,256]{1,0:T(8,128)(2,1)S(1)} %collective-permute-done.10.side), channel_id=1, source_target_pairs={{0,1},{1,0},{2,3},{3,2},{4,5},{5,4},{6,7},{7,6},{8,9},{9,8},{10,11... | collective-permute-start | bytes 294920 | tf_op jit(solution)/shard_map/ppermute | solution.py:30
  (4 other events, 4.9 us)

commit v2 on v0

v2 whole, which is shorter than its diff:
```python
import functools

import jax
import jax.numpy as jnp
from jax import lax
from jax.experimental import pallas as pl
from jax.experimental.pallas import tpu as pltpu
from jax.sharding import PartitionSpec as P

AXES = ("gx", "gy")
F32 = jnp.float32
BF16 = jnp.bfloat16
LEAF = 2048
RANK = 256
NCOL = 768
HALF = NCOL // 2
QUARTER = NCOL // 4
VMEM = pl.BlockSpec(memory_space=pltpu.VMEM)
HBM = pl.BlockSpec(memory_space=pltpu.HBM)
ANY = pl.BlockSpec(memory_space=pl.ANY)
MIB = 1 << 20


def permute(array, dx=0, dy=0):
    pairs = [(gx * 8 + gy, (gx ^ dx) * 8 + (gy ^ dy)) for gx in range(16) for gy in range(8)]
    return lax.ppermute(array, AXES, pairs)


def nn(a, b):
    return jnp.dot(a, b, preferred_element_type=F32)


def nt(a, b):
    return lax.dot_general(a, b, (((1,), (1,)), ((), ())), preferred_element_type=F32)


def add(a, b):
    return (a[...].astype(F32) + b[...].astype(F32)).astype(BF16)


def core_index():
    return lax.rem(lax.axis_index("gy"), 2)


def part_index():
    x = lax.rem(lax.axis_index("gx"), 4)
    return jnp.where((x == 1) | (x == 2), 1, 0)


def call(kernel, name, outs, in_specs, flops=0, moved=0, scratch=(), limit=16, aliases=None, out_specs=None):
    return pl.pallas_call(
        kernel,
        out_shape=[jax.ShapeDtypeStruct(*o) for o in outs],
        in_specs=in_specs,
        out_specs=[VMEM] * len(outs) if out_specs is None else out_specs,
        scratch_shapes=list(scratch),
        input_output_aliases=aliases or {},
        compiler_params=pltpu.CompilerParams(vmem_limit_bytes=limit * MIB),
        cost_estimate=pl.CostEstimate(flops=flops, bytes_accessed=moved, transcendentals=0),
        name=name,
    )


def picks(order_row, base, rows):
    it = lax.broadcasted_iota(jnp.int32, (rows, LEAF), 0)
    return jnp.where(it == (order_row - base), 1.0, 0.0).astype(BF16)


def front_kernel(order_hbm, basis_hbm, x_hbm, couple_hbm, c0, send, keep, order, basis, x, couple, turned, lift, sems):
    fetches = [
        pltpu.make_async_copy(order_hbm, order, sems.at[0]),
        pltpu.make_async_copy(basis_hbm, basis, sems.at[1]),
        pltpu.make_async_copy(couple_hbm.at[0], couple, sems.at[2]),
        pltpu.make_async_copy(x_hbm, x, sems.at[3]),
    ]
    for fetch in fetches:
        fetch.start()
    fetches[0].wait()
    fetches[1].wait()
    for j in range(LEAF // 512):
        block = nn(picks(order[...], j * 512, 512), basis[...]).astype(BF16)
        turned[:, j * 512 : (j + 1) * 512] = block.T
    fetches[3].wait()
    c = nn(turned[...], x[...]).astype(BF16).T
    c0[...] = c
    fetches[2].wait()
    lift[...] = nn(c, couple[...]).astype(BF16)
    core = core_index()
    keep[...] = lift[pl.ds(pl.multiple_of(core * HALF, HALF), HALF), :]
    send[...] = lift[pl.ds(pl.multiple_of((1 - core) * HALF, HALF), HALF), :]


def pair_kernel(keep, recv, _after, _ordered, send2, keep2, total):
    total[...] = add(keep, recv)
    part = part_index()
    keep2[...] = total[pl.ds(pl.multiple_of(part * QUARTER, QUARTER), QUARTER), :]
    send2[...] = total[pl.ds(pl.multiple_of((1 - part) * QUARTER, QUARTER), QUARTER), :]


def coarse_kernel(keep, recv, couple, _after, coef1, lift1):
    c = add(keep, recv)
    coef1[...] = c
    lift1[...] = nn(c, couple[0]).astype(BF16)


def sum_kernel(mine, recv, _after, total):
    total[...] = add(mine, recv)


def pick_top_kernel(top, _after, rows, sems):
    y = lax.axis_index("gx") // 4
    z = lax.axis_index("gy") // 4
    flip = jnp.where(lax.rem(y, 2) == 0, y + 1, y - 1)
    copies = []
    for d, there in enumerate((y, flip, 3 - y, 3 - flip)):
        r = pl.multiple_of((there * 2 + z) * RANK, RANK)
        s = pl.multiple_of(y * 2 * RANK, 2 * RANK)
        copies.append(
            pltpu.make_async_copy(top.at[pl.ds(r, RANK), pl.ds(s, 2 * RANK)], rows.at[d], sems.at[d])
        )
    for copy in copies:
        copy.start()
    for copy in copies:
        copy.wait()


def top_kernel(own, other, rows, _after, stay0, stay1, send):
    low = lax.axis_index("gy") < 4
    a, b = own[...], other[...]
    zero = jnp.zeros_like(a)
    both = jnp.concatenate([jnp.where(low, a, b), jnp.where(low, b, a)], axis=1)
    others = jnp.concatenate([jnp.where(low, zero, b), jnp.where(low, b, zero)], axis=1)
    send[:QUARTER] = nt(both, rows[2]).astype(BF16)
    send[QUARTER:] = nt(both, rows[3]).astype(BF16)
    stay0[...] = nt(others, rows[0])
    stay1[...] = nt(both, rows[1])


def half_kernel(stay1, recv, _after, send):
    send[...] = (stay1[...] + recv[QUARTER:].astype(F32)).astype(BF16)


def near1_kernel(side_x, sides, couple, _after, near1):
    near1[...] = (
        nt(side_x[...], couple[1]) + nt(sides[:QUARTER], couple[2]) + nt(sides[QUARTER:], couple[3])
    )


def near0_kernel(side_x, side_y, side_xy, couple, _after, near0):
    near0[...] = nt(couple[1], side_x[...]) + nt(couple[2], side_y[...]) + nt(couple[3], side_xy[...])


def down1_kernel(stay0, first, second, near1, couple, _after, _near0, down1):
    d2 = (stay0[...] + first[:QUARTER].astype(F32) + second[...].astype(F32)).astype(BF16)
    down1[...] = (near1[...] + nt(d2, couple[0])).astype(BF16)


def gather_kernel(blocks, first, order, x, _after, *refs):
    out = refs[first]
    for start, size in blocks:
        parts = []
        for s in range(start, start + size, 128):
            column = jnp.broadcast_to(order[:, s : s + 128].astype(F32), (128, 128)).T
            lane = lax.broadcasted_iota(jnp.int32, (128, 128), 1).astype(F32)
            parts.append(
                jnp.concatenate(
                    [jnp.where(column == lane + 128.0 * j, 1.0, 0.0).astype(BF16) for j in range(LEAF // 128)], axis=1
                )
            )
        out[start : start + size] = nn(jnp.concatenate(parts, axis=0), x[...]).astype(BF16)


def dense_kernel(blocks, first, dense, ordered, _after, *refs):
    out = refs[first]
    for start, size in blocks:
        out[start : start + size] = nn(dense[start : start + size], ordered[...]).astype(BF16)


def scatter_kernel(blocks, first, order, result, basis, _after, *refs):
    out, turned = refs[first : first + 2]
    for start, size in blocks:
        hot = picks(order[...], start, size)
        out[start : start + size] = nn(hot, result[...]).astype(BF16)
        turned[start : start + size] = nn(hot, basis[...]).astype(BF16)


def both_kernel(coef1, side_x, _after, both):
    both[:QUARTER] = coef1[...]
    both[QUARTER:] = side_x[...]


def gate_kernel(_array, _after, _out):
    pass


def final_kernel(base, turned, own, side, core_own, core_side, near0, couple, out_hbm, down1, out, sems):
    core, part = core_index(), part_index()
    for which, half, quarter in (
        (own, core, part),
        (side, core, 1 - part),
        (core_own, 1 - core, part),
        (core_side, 1 - core, 1 - part),
    ):
        down1[pl.ds(pl.multiple_of(half * HALF + quarter * QUARTER, QUARTER), QUARTER), :] = which[...]
    down0 = (near0[...] + nt(couple[0], down1[...])).astype(BF16)
    copies = []
    for j in range(4):
        rows = pl.ds(j * 512, 512)
        out[rows] = (base[rows].astype(F32) + nn(turned[rows], down0)).astype(BF16)
        copies.append(pltpu.make_async_copy(out.at[rows], out_hbm.at[rows], sems.at[j]))
        copies[-1].start()
    for copy in copies:
        copy.wait()


def leaf_part(kernel, name, blocks, operands, previous, widths, after, carry=()):
    outs = [((LEAF, width), BF16) for width in widths]
    kept = list(previous) + list(carry)
    count = len(operands) + 1
    skip = len(outs) - len(previous)
    got = call(
        functools.partial(kernel, blocks, len(kept)),
        name,
        outs + [(c.shape, c.dtype) for c in carry],
        [VMEM] * len(operands) + [ANY] + [VMEM] * len(previous) + [ANY] * len(carry),
        flops=2 * sum(size for _, size in blocks) * LEAF * sum(widths),
        moved=4 * MIB,
        aliases={count + i: skip + i for i in range(len(kept))},
        out_specs=[VMEM] * len(outs) + [ANY] * len(carry),
    )(*operands, after, *kept)
    return (got[: len(outs)], *got[len(outs) :])


def gate(array, after):
    return call(
        gate_kernel, "gate", [(array.shape, array.dtype)], [ANY, ANY], aliases={0: 0}, out_specs=[ANY]
    )(array, after)[0]


def local(right_block, point_order, leaf_dense, basis_in, basis_out, leaf_couple, coarse_couple, top_coupling):
    order = point_order.reshape(1, LEAF)
    leaf = leaf_couple.reshape(4, RANK, RANK)
    coarse = coarse_couple.reshape(4, RANK, RANK)
    quarter = ((QUARTER, RANK), BF16)
    quarter_f32 = ((QUARTER, RANK), F32)
    half = ((HALF, RANK), BF16)
    whole = ((NCOL, RANK), BF16)
    small = 2 * QUARTER * RANK * RANK

    c0, send, keep = call(
        front_kernel,
        "front",
        [whole, half, half],
        [HBM] * 4,
        flops=2 * LEAF * LEAF * RANK + 2 * LEAF * RANK * NCOL,
        moved=5 * MIB,
        scratch=[
            pltpu.VMEM((1, LEAF), jnp.int32),
            pltpu.VMEM((LEAF, RANK), BF16),
            pltpu.VMEM((LEAF, NCOL), BF16),
            pltpu.VMEM((RANK, RANK), BF16),
            pltpu.VMEM((RANK, LEAF), BF16),
            pltpu.VMEM((NCOL, RANK), BF16),
            pltpu.SemaphoreType.DMA((4,)),
        ],
        limit=24,
    )(*(pltpu.with_memory_space_constraint(a, pltpu.HBM) for a in (order, basis_in, right_block, leaf)))
    recv = permute(send, dy=1)
    rows = call(
        pick_top_kernel,
        "pick_top",
        [((4, RANK, 2 * RANK), BF16)],
        [HBM, ANY],
        moved=2 * MIB,
        scratch=[pltpu.SemaphoreType.DMA((4,))],
    )(pltpu.with_memory_space_constraint(top_coupling, pltpu.HBM), send)[0]

    gather = functools.partial(leaf_part, gather_kernel, "gather")
    dense = functools.partial(leaf_part, dense_kernel, "dense")
    scatter = functools.partial(leaf_part, scatter_kernel, "scatter")
    (ordered,) = gather([(0, 256)], [order, right_block], [], [NCOL], send)

    send2, keep2 = call(
        pair_kernel, "pair", [quarter, quarter], [VMEM, VMEM, ANY, ANY], scratch=[pltpu.VMEM((HALF, RANK), BF16)]
    )(keep, recv, rows, ordered[0])
    recv2 = permute(send2, dx=1)
    (ordered,) = gather([(256, 512), (768, 384)], [order, right_block], ordered, [NCOL], send2)

    coef1, lift1 = call(coarse_kernel, "coarse", [quarter, quarter], [VMEM, VMEM, VMEM, ANY], flops=small)(
        keep2, recv2, coarse, ordered[0]
    )
    recv3 = permute(lift1, dx=3)
    ordered, c0 = gather([(1152, 512), (1664, 384)], [order, right_block], ordered, [NCOL], lift1, [c0])
    side_y = permute(c0, dy=1)
    side_x = permute(c0, dx=1)

    pair = call(sum_kernel, "sum_x", [quarter], [VMEM, VMEM, ANY])(lift1, recv3, ordered[0])[0]
    recv4 = permute(pair, dy=2)
    result, coef1 = dense([(0, 512), (512, 512)], [leaf_dense, ordered[0]], [], [NCOL], pair, [coef1])
    coarse_x = permute(coef1, dx=3)

    coef2 = call(sum_kernel, "sum_z", [quarter], [VMEM, VMEM, ANY])(pair, recv4, result[0])[0]
    recv5 = permute(coef2, dy=6)
    (result,) = dense([(1024, 512), (1536, 512)], [leaf_dense, ordered[0]], result, [NCOL], coef2)
    both = call(both_kernel, "both", [half], [VMEM, VMEM, ANY])(coef1, coarse_x, result[0])[0]
    coarse_yz = permute(both, dy=2)

    stay0, stay1, send6 = call(
        top_kernel,
        "top",
        [quarter_f32, quarter_f32, half],
        [VMEM, VMEM, VMEM, ANY],
        flops=8 * small,
    )(coef2, recv5, rows, both)
    recv6 = permute(send6, dx=12)
    widths = [NCOL, RANK]
    scattered, side_x = scatter(
        [(0, 384), (384, 384)], [order, result[0], basis_out], [], widths, send6, [side_x]
    )
    side_xy = permute(side_x, dy=1)

    send7 = call(half_kernel, "half", [quarter], [VMEM, VMEM, ANY])(stay1, recv6, scattered[0])[0]
    recv7 = permute(send7, dx=4)
    near1 = call(near1_kernel, "near1", [quarter_f32], [VMEM, VMEM, VMEM, ANY], flops=3 * small)(
        coarse_x, coarse_yz, coarse, send7
    )[0]
    near0 = call(near0_kernel, "near0", [((RANK, NCOL), F32)], [VMEM] * 4 + [ANY], flops=12 * small)(
        side_x, side_y, side_xy, leaf, send7
    )[0]
    (scattered,) = scatter([(768, 320), (1088, 320)], [order, result[0], basis_out], scattered, widths, send7)

    down1 = call(down1_kernel, "down1", [quarter], [VMEM] * 5 + [ANY, ANY], flops=small)(
        stay0, recv6, recv7, near1, coarse, scattered[0], near0
    )[0]
    side = permute(down1, dx=1)
    core_own = permute(down1, dy=1)
    (scattered,) = scatter([(1408, 448)], [order, result[0], basis_out], scattered, widths, down1)
    side = gate(side, scattered[0])
    core_side = permute(side, dy=1)
    (scattered,) = scatter([(1856, 192)], [order, result[0], basis_out], scattered, widths, side)

    return call(
        final_kernel,
        "final",
        [((LEAF, NCOL), BF16)],
        [VMEM] * 8,
        flops=2 * LEAF * RANK * NCOL,
        moved=8 * MIB,
        scratch=[pltpu.VMEM((NCOL, RANK), BF16), pltpu.VMEM((LEAF, NCOL), BF16), pltpu.SemaphoreType.DMA((4,))],
        out_specs=[HBM],
    )(scattered[0], scattered[1], down1, side, core_own, core_side, near0, leaf)[0]


def solution(mesh):
    in_specs = (
        P(("gx", "gy"), None),
        P("gx", "gy", None),
        P(("gx", "gy"), None),
        P(("gx", "gy"), None),
        P(("gx", "gy"), None),
        P("gx", "gy", None, None, None),
        P("gx", "gy", None, None, None),
        P(),
    )
    out_specs = P(("gx", "gy"), None)
    return jax.shard_map(local, mesh=mesh, in_specs=in_specs, out_specs=out_specs, check_vma=False)
```

time: 175 us -> 60.3 us (0.34)
  waiting for transfers between devices: 69.9 us -> 4.6 us
  matrix products: 38.7 us -> 0 us
  Pallas kernels: 0 us -> 34.5 us
  local copies, waits for them, and re-layouts: 28.9 us -> 0.04 us
  between operations: 13.5 us -> 0.47 us
  other arithmetic: 6.19 us -> 0.01 us
  starting transfers between devices: 17.2 us -> 20.6 us
    dot_general x11 -> x0, matrix products: 38.7 us -> none  [the longest x1 12.7 us: local(): jnp.dot(leaf_dense, ordered, preferred_element_type=jnp.float32)]
    all_gather x1 -> x0, waiting for transfers between devices: 37.9 us -> none  [local(): gathered = lax.all_gather(portion, ('gx', 'gy'), axis=0, tiled=True)]
    pallas_call x0 -> x23, Pallas kernels: none -> 34.5 us  [the longest x9 23.4 us: leaf_part(): call(functools.partial(kernel, blocks, len(kept)), name, outs + [(c.shape...]
    ppermute x10 -> x15, waiting for transfers between devices: 31.9 us -> 4.6 us  [permute(): return lax.ppermute(array, AXES, pairs)]
    scatter x1 -> x0, local copies, waits for them, and re-layouts: 12.3 us -> none  [local(): return jnp.zeros_like(leaf_result).at[order_local].set(leaf_result)]
    gather x1 -> x0, local copies, waits for them, and re-layouts: 9.4 us -> none  [local(): ordered = jnp.take(right_block, order_local, axis=0)]
    convert_element_type x1 -> x0, local copies, waits for them, and re-layouts: 4.67 us -> none  [local(): leaf_result = (local_term + jnp.dot(basis_out, downward, preferred_elemen...]
    ppermute x10 -> x15, starting transfers between devices: 17.2 us -> 20.6 us  [permute(): return lax.ppermute(array, AXES, pairs)]
  transfers between devices with their start and end apart: 11 -> 15, of which waited for: 6 -> 2; matrix products, arithmetic and copies ran while one was open for 17% -> 0% of each run, Pallas kernels for 0% -> 43%
where the time goes in v2:
time: 60.3 us; the launch traced here: 60.2 us
  Pallas kernels  34.5 us (57%)
  starting transfers between devices  20.6 us (34%)
  waiting for transfers between devices  4.6 us (8%)
    pallas_call x9, Pallas kernels, leaf_part(): call(functools.partial(kernel, blocks, len(kept)), name, outs + [(c.shape...  23.4 us
    ppermute x15, starting transfers between devices, permute(): return lax.ppermute(array, AXES, pairs)  20.6 us
    pallas_call x1, Pallas kernels, local(): call(front_kernel, 'front', [whole, half, half], [HBM] * 4, flops=2 * LEA...  5.57 us
    ppermute x15, waiting for transfers between devices, permute(): return lax.ppermute(array, AXES, pairs)  4.6 us
    pallas_call x1, Pallas kernels, local(): call(final_kernel, 'final', [((LEAF, NCOL), BF16)], [VMEM] * 8, flops=2 *...  2.42 us
    pallas_call x1, Pallas kernels, local(): call(pick_top_kernel, 'pick_top', [((4, RANK, 2 * RANK), BF16)], [HBM, AN...  1.23 us
  transfers between devices with their start and end apart: 15, of which 2 were waited for; matrix products, arithmetic and copies ran while one was open for 0% of the time, Pallas kernels for 43%

profile of v2, /device:TPU:1, one launch (start us, length us, event | category | flops | bytes accessed | tf_op | source)
XLA Modules:
  0.0 60.2 jit_solution(3068319594388134935)
XLA Ops:
  0.0 5.6 %front.1 = (bf16[768,256]{1,0:T(8,128)(2,1)S(1)}, bf16[384,256]{1,0:T(8,128)(2,1)S(1)}, bf16[384,256]{1,0:T(8,128)(2,1)S(1)}) custom-call(s32[1,2048]{1,0:T(1,128)} %bitcast.11, bf16[2048,256]{1,0:T(8,128)(2,1)} %basis_hbm.1, bf16[2048,768]{1,0:T(8,128)(2,1)} %x.5, bf16[4,256,256]{2,1,0:T(8,128)(2,1)} %bitcast.8), custom_call_target="tpu_custom_call" | custom-call | flops 2952790016 | bytes 5242880 | tf_op jit(solution)/shard_map/front/pallas_call | solution.py:250
  5.6 1.5 %collective-permute-start = (bf16[384,256]{1,0:T(8,128)(2,1)S(1)}, bf16[384,256]{1,0:T(8,128)(2,1)S(1)}, u32[]{:S(2)}, u32[]{:S(2)}) collective-permute-start(bf16[384,256]{1,0:T(8,128)(2,1)S(1)} %get-tuple-element.29._after), channel_id=1, source_target_pairs={{0,1},{1,0},{2,3},{3,2},{4,5},{5,4},{6,7},{7,6},{8,9},{9,8},{10,11... | collective-permute-start | bytes 589832 | tf_op jit(solution)/shard_map/ppermute | solution.py:26
  7.1 1.2 %pick_top.1._after.rows = bf16[4,256,512]{2,1,0:T(8,128)(2,1)S(1)} custom-call(bf16[2048,2048]{1,0:T(8,128)(2,1)} %top.2, bf16[384,256]{1,0:T(8,128)(2,1)S(1)} %get-tuple-element.29._after), custom_call_target="tpu_custom_call" | custom-call | bytes 2097152 | tf_op jit(solution)/shard_map/pick_top/pallas_call | solution.py:269
  8.3 1.0 %gather.3._ordered.refs_0_ = bf16[2048,768]{1,0:T(8,128)(2,1)S(1)} custom-call(s32[1,2048]{1,0:T(1,128)S(1)} %bitcast.12, bf16[2048,768]{1,0:T(8,128)(2,1)S(1)} %copy-done.2, bf16[384,256]{1,0:T(8,128)(2,1)S(1)} %get-tuple-element.29._after), custom_call_target="tpu_custom_call" | custom-call | flops 805306368 | bytes 4194304 | tf_op jit(solution)/shard_map/gather/pallas_call | solution.py:221
  9.5 1.6 %collective-permute-start.1 = (bf16[192,256]{1,0:T(8,128)(2,1)S(1)}, bf16[192,256]{1,0:T(8,128)(2,1)S(1)}, u32[]{:S(2)}, u32[]{:S(2)}) collective-permute-start(bf16[192,256]{1,0:T(8,128)(2,1)S(1)} %get-tuple-element.31._after), channel_id=1, source_target_pairs={{0,8},{1,9},{2,10},{3,11},{4,12},{5,13},{6,14},{7,15},{8,0},{9,1},... | collective-permute-start | bytes 294920 | tf_op jit(solution)/shard_map/ppermute | solution.py:26
  11.1 3.1 %gather.4._after.refs_0_ = bf16[2048,768]{1,0:T(8,128)(2,1)S(1)} custom-call(s32[1,2048]{1,0:T(1,128)S(1)} %bitcast.13, bf16[2048,768]{1,0:T(8,128)(2,1)S(1)} %copy-done.2, bf16[192,256]{1,0:T(8,128)(2,1)S(1)} %get-tuple-element.31._after, bf16[2048,768]{1,0:T(8,128)(2,1)S(1)} %gather.3._ordered.refs_0_), custom_call_target="tpu_custom_call", output_to_operand_aliasing={{}: (3, {})} | custom-call | flops 2818572288 | bytes 4194304 | tf_op jit(solution)/shard_map/gather/pallas_call | solution.py:221
  14.4 1.9 %collective-permute-start.2 = (bf16[192,256]{1,0:T(8,128)(2,1)S(1)}, bf16[192,256]{1,0:T(8,128)(2,1)S(1)}, u32[]{:S(2)}, u32[]{:S(2)}) collective-permute-start(bf16[192,256]{1,0:T(8,128)(2,1)S(1)} %get-tuple-element.32._after.mine), channel_id=1, source_target_pairs={{0,24},{1,25},{2,26},{3,27},{4,28},{5,29},{6,30},{7,31},{8,16},{9,... | collective-permute-start | bytes 294920 | tf_op jit(solution)/shard_map/ppermute | solution.py:26
  16.3 3.1 %gather.5 = (bf16[2048,768]{1,0:T(8,128)(2,1)S(1)}, bf16[768,256]{1,0:T(8,128)(2,1)S(1)}) custom-call(s32[1,2048]{1,0:T(1,128)S(1)} %bitcast.14, bf16[2048,768]{1,0:T(8,128)(2,1)S(1)} %copy-done.2, bf16[192,256]{1,0:T(8,128)(2,1)S(1)} %get-tuple-element.32._after.mine, ...), custom_call_target="tpu_custom_call", output_to_operand_aliasing={{0}: (3, {}), {1}: (4, {})} | custom-call | flops 2818572288 | bytes 4194304 | tf_op jit(solution)/shard_map/gather/pallas_call | solution.py:221
  19.5 1.9 %collective-permute-start.10 = (bf16[768,256]{1,0:T(8,128)(2,1)S(1)}, bf16[768,256]{1,0:T(8,128)(2,1)S(1)}, u32[]{:S(2)}, u32[]{:S(2)}) collective-permute-start(bf16[768,256]{1,0:T(8,128)(2,1)S(1)} %get-tuple-element.41), channel_id=1, source_target_pairs={{0,1},{1,0},{2,3},{3,2},{4,5},{5,4},{6,7},{7,6},{8,9},{9,8},{10,11... | collective-permute-start | bytes 1179656 | tf_op jit(solution)/shard_map/ppermute | solution.py:26
  21.4 1.9 %collective-permute-start.3 = (bf16[192,256]{1,0:T(8,128)(2,1)S(1)}, bf16[192,256]{1,0:T(8,128)(2,1)S(1)}, u32[]{:S(2)}, u32[]{:S(2)}) collective-permute-start(bf16[192,256]{1,0:T(8,128)(2,1)S(1)} %sum_x.1._after.mine), channel_id=1, source_target_pairs={{0,2},{1,3},{2,0},{3,1},{4,6},{5,7},{6,4},{7,5},{8,10},{9,11},{10,... | collective-permute-start | bytes 294920 | tf_op jit(solution)/shard_map/ppermute | solution.py:26
  23.3 3.4 %dense.4 = (bf16[2048,768]{1,0:T(8,128)(2,1)S(1)}, bf16[192,256]{1,0:T(8,128)(2,1)S(1)}) custom-call(bf16[2048,2048]{1,0:T(8,128)(2,1)S(1)} %bitcast.4, bf16[2048,768]{1,0:T(8,128)(2,1)S(1)} %get-tuple-element.34._after.ordered, bf16[192,256]{1,0:T(8,128)(2,1)S(1)} %sum_x.1._after.mine, ...), custom_call_target="tpu_custom_call", output_to_operand_aliasing={{1}: (3, {})} | custom-call | flops 3221225472 | bytes 4194304 | tf_op jit(solution)/shard_map/dense/pallas_call | solution.py:221
  26.8 0.9 %collective-permute-start.5 = (bf16[192,256]{1,0:T(8,128)(2,1)S(1)}, bf16[192,256]{1,0:T(8,128)(2,1)S(1)}, u32[]{:S(2)}, u32[]{:S(2)}) collective-permute-start(bf16[192,256]{1,0:T(8,128)(2,1)S(1)} %get-tuple-element.37.coef1), channel_id=1, source_target_pairs={{0,24},{1,25},{2,26},{3,27},{4,28},{5,29},{6,30},{7,31},{8,16},{9,... | collective-permute-start | bytes 294920 | tf_op jit(solution)/shard_map/ppermute | solution.py:26
  27.7 2.3 %collective-permute-start.4 = (bf16[192,256]{1,0:T(8,128)(2,1)S(1)}, bf16[192,256]{1,0:T(8,128)(2,1)S(1)}, u32[]{:S(2)}, u32[]{:S(2)}) collective-permute-start(bf16[192,256]{1,0:T(8,128)(2,1)S(1)} %sum_z.1._after.own), channel_id=1, source_target_pairs={{0,6},{1,7},{2,4},{3,5},{4,2},{5,3},{6,0},{7,1},{8,14},{9,15},{10,... | collective-permute-start | bytes 294920 | tf_op jit(solution)/shard_map/ppermute | solution.py:26
  30.0 3.4 %dense.6._after.result = bf16[2048,768]{1,0:T(8,128)(2,1)S(1)} custom-call(bf16[2048,2048]{1,0:T(8,128)(2,1)S(1)} %bitcast.4, bf16[2048,768]{1,0:T(8,128)(2,1)S(1)} %get-tuple-element.34._after.ordered, bf16[192,256]{1,0:T(8,128)(2,1)S(1)} %sum_z.1._after.own, bf16[2048,768]{1,0:T(8,128)(2,1)S(1)} %get-tuple-element.36._after.refs_0_), custom_call_target="tpu_custom_call", output_to_operand_aliasing={{}: (3, {})} | custom-call | flops 3221225472 | bytes 4194304 | tf_op jit(solution)/shard_map/dense/pallas_call | solution.py:221
  34.0 2.8 %collective-permute-start.6 = (bf16[384,256]{1,0:T(8,128)(2,1)S(1)}, bf16[384,256]{1,0:T(8,128)(2,1)S(1)}, u32[]{:S(2)}, u32[]{:S(2)}) collective-permute-start(bf16[384,256]{1,0:T(8,128)(2,1)S(1)} %get-tuple-element.39._after), channel_id=1, source_target_pairs={{0,96},{1,97},{2,98},{3,99},{4,100},{5,101},{6,102},{7,103},{8,104... | collective-permute-start | bytes 589832 | tf_op jit(solution)/shard_map/ppermute | solution.py:26
  36.8 3.4 %scatter.4 = (bf16[2048,768]{1,0:T(8,128)(2,1)S(1)}, bf16[2048,256]{1,0:T(8,128)(2,1)S(1)}, bf16[768,256]{1,0:T(8,128)(2,1)S(1)}) custom-call(s32[1,2048]{1,0:T(1,128)S(1)} %bitcast.15, bf16[2048,768]{1,0:T(8,128)(2,1)S(1)} %dense.6._after.result, bf16[2048,256]{1,0:T(8,128)(2,1)S(1)} %copy-done.1, ...), custom_call_target="tpu_custom_call", output_to_operand_aliasing={{2}: (4, {})} | custom-call | flops 3221225472 | bytes 4194304 | tf_op jit(solution)/shard_map/scatter/pallas_call | solution.py:221
  40.2 2.7 %collective-permute-start.11 = (bf16[768,256]{1,0:T(8,128)(2,1)S(1)}, bf16[768,256]{1,0:T(8,128)(2,1)S(1)}, u32[]{:S(2)}, u32[]{:S(2)}) collective-permute-start(bf16[768,256]{1,0:T(8,128)(2,1)S(1)} %get-tuple-element.45.side_x), channel_id=1, source_target_pairs={{0,1},{1,0},{2,3},{3,2},{4,5},{5,4},{6,7},{7,6},{8,9},{9,8},{10,11... | collective-permute-start | bytes 1179656 | tf_op jit(solution)/shard_map/ppermute | solution.py:26
  44.0 2.9 %scatter.5 = (bf16[2048,768]{1,0:T(8,128)(2,1)S(1)}, bf16[2048,256]{1,0:T(8,128)(2,1)S(1)}) custom-call(s32[1,2048]{1,0:T(1,128)S(1)} %bitcast.16, bf16[2048,768]{1,0:T(8,128)(2,1)S(1)} %dense.6._after.result, bf16[2048,256]{1,0:T(8,128)(2,1)S(1)} %copy-done.1, bf16[192,256]{1,0:T(8,128)(2,1)S(1)} %half.1._after, ...), custom_call_target="tpu_custom_call", output_to_operand_aliasing={{0}: (4, {}), {1}: (5, {})} | custom-call | flops 2684354560 | bytes 4194304 | tf_op jit(solution)/shard_map/scatter/pallas_call | solution.py:221
  46.9 2.5 %collective-permute-done.9.sides = bf16[384,256]{1,0:T(8,128)(2,1)S(1)} collective-permute-done((bf16[384,256]{1,0:T(8,128)(2,1)S(1)}, bf16[384,256]{1,0:T(8,128)(2,1)S(1)}, u32[]{:S(2)}, u32[]{:S(2)}) %collective-permute-start.9) | collective-permute-done | bytes 196640 | tf_op jit(solution)/shard_map/ppermute | solution.py:26
  50.4 1.0 %collective-permute-start.13 = (bf16[192,256]{1,0:T(8,128)(2,1)S(1)}, bf16[192,256]{1,0:T(8,128)(2,1)S(1)}, u32[]{:S(2)}, u32[]{:S(2)}) collective-permute-start(bf16[192,256]{1,0:T(8,128)(2,1)S(1)} %down1.1._after.own), channel_id=1, source_target_pairs={{0,1},{1,0},{2,3},{3,2},{4,5},{5,4},{6,7},{7,6},{8,9},{9,8},{10,11... | collective-permute-start | bytes 294920 | tf_op jit(solution)/shard_map/ppermute | solution.py:26
  51.6 2.1 %scatter.6 = (bf16[2048,768]{1,0:T(8,128)(2,1)S(1)}, bf16[2048,256]{1,0:T(8,128)(2,1)S(1)}) custom-call(s32[1,2048]{1,0:T(1,128)S(1)} %bitcast.17, bf16[2048,768]{1,0:T(8,128)(2,1)S(1)} %dense.6._after.result, bf16[2048,256]{1,0:T(8,128)(2,1)S(1)} %copy-done.1, bf16[192,256]{1,0:T(8,128)(2,1)S(1)} %down1.1._after.own, ...), custom_call_target="tpu_custom_call", output_to_operand_aliasing={{0}: (4, {}), {1}: (5, {})} | custom-call | flops 1879048192 | bytes 4194304 | tf_op jit(solution)/shard_map/scatter/pallas_call | solution.py:221
  53.6 2.1 %collective-permute-done.12._array = bf16[192,256]{1,0:T(8,128)(2,1)S(1)} collective-permute-done((bf16[192,256]{1,0:T(8,128)(2,1)S(1)}, bf16[192,256]{1,0:T(8,128)(2,1)S(1)}, u32[]{:S(2)}, u32[]{:S(2)}) %collective-permute-start.12) | collective-permute-done | bytes 98336 | tf_op jit(solution)/shard_map/ppermute | solution.py:26
  56.6 1.0 %scatter.7 = (bf16[2048,768]{1,0:T(8,128)(2,1)S(1)}, bf16[2048,256]{1,0:T(8,128)(2,1)S(1)}) custom-call(s32[1,2048]{1,0:T(1,128)S(1)} %bitcast.18, bf16[2048,768]{1,0:T(8,128)(2,1)S(1)} %dense.6._after.result, bf16[2048,256]{1,0:T(8,128)(2,1)S(1)} %copy-done.1, bf16[192,256]{1,0:T(8,128)(2,1)S(1)} %gate.1._after.side, ...), custom_call_target="tpu_custom_call", output_to_operand_aliasing={{0}: (4, {}), {1}: (5, {})} | custom-call | flops 805306368 | bytes 4194304 | tf_op jit(solution)/shard_map/scatter/pallas_call | solution.py:221
  57.6 2.4 %final.1 = bf16[2048,768]{1,0:T(8,128)(2,1)} custom-call(bf16[2048,768]{1,0:T(8,128)(2,1)S(1)} %get-tuple-element.49.base, bf16[2048,256]{1,0:T(8,128)(2,1)S(1)} %get-tuple-element.50.turned, bf16[192,256]{1,0:T(8,128)(2,1)S(1)} %down1.1._after.own, bf16[192,256]{1,0:T(8,128)(2,1)S(1)} %gate.1._after.side, ...), custom_call_target="tpu_custom_call" | custom-call | flops 805306368 | bytes 8388608 | tf_op jit(solution)/shard_map/final/pallas_call | solution.py:342
  (44 shorter events, 4.1 us)
Async XLA Ops:
  5.6 2.7 %copy-start.2 = (bf16[2048,768]{1,0:T(8,128)(2,1)S(1)}, bf16[2048,768]{1,0:T(8,128)(2,1)}, u32[]{:S(2)}) copy-start(bf16[2048,768]{1,0:T(8,128)(2,1)} %x.5) | copy-start | bytes 9437188
  5.6 2.7 %copy-start.4 = (s32[1,1,2048]{2,1,0:T(1,128)S(1)}, s32[1,1,2048]{2,1,0:T(1,128)}, u32[]{:S(2)}) copy-start(s32[1,1,2048]{2,1,0:T(1,128)} %param.9) | copy-start | bytes 24580
  5.6 3.8 %collective-permute-start = (bf16[384,256]{1,0:T(8,128)(2,1)S(1)}, bf16[384,256]{1,0:T(8,128)(2,1)S(1)}, u32[]{:S(2)}, u32[]{:S(2)}) collective-permute-start(bf16[384,256]{1,0:T(8,128)(2,1)S(1)} %get-tuple-element.29._after), channel_id=1, source_target_pairs={{0,1},{1,0},{2,3},{3,2},{4,5},{5,4},{6,7},{7,6},{8,9},{9,8},{10,11... | collective-permute-start | bytes 589832 | tf_op jit(solution)/shard_map/ppermute | solution.py:26
  9.5 4.7 %copy-start = (bf16[1,1,4,256,256]{4,3,2,1,0:T(8,128)(2,1)S(1)}, bf16[1,1,4,256,256]{4,3,2,1,0:T(8,128)(2,1)}, u32[]{:S(2)}) copy-start(bf16[1,1,4,256,256]{4,3,2,1,0:T(8,128)(2,1)} %param.14) | copy-start | bytes 1572868
  9.5 4.7 %collective-permute-start.1 = (bf16[192,256]{1,0:T(8,128)(2,1)S(1)}, bf16[192,256]{1,0:T(8,128)(2,1)S(1)}, u32[]{:S(2)}, u32[]{:S(2)}) collective-permute-start(bf16[192,256]{1,0:T(8,128)(2,1)S(1)} %get-tuple-element.31._after), channel_id=1, source_target_pairs={{0,8},{1,9},{2,10},{3,11},{4,12},{5,13},{6,14},{7,15},{8,0},{9,1},... | collective-permute-start | bytes 294920 | tf_op jit(solution)/shard_map/ppermute | solution.py:26
  14.2 9.1 %slice-start = ((s8[8388608]{0:T(1024)(128)(4,1)}), s8[4194304]{0:T(1024)(128)(4,1)S(1)}, s32[]{:S(2)}) async-start(s8[8388608]{0:T(1024)(128)(4,1)} %bitcast.3), calls=%async_computation | async-start | bytes 8388608
  14.4 7.0 %collective-permute-start.2 = (bf16[192,256]{1,0:T(8,128)(2,1)S(1)}, bf16[192,256]{1,0:T(8,128)(2,1)S(1)}, u32[]{:S(2)}, u32[]{:S(2)}) collective-permute-start(bf16[192,256]{1,0:T(8,128)(2,1)S(1)} %get-tuple-element.32._after.mine), channel_id=1, source_target_pairs={{0,24},{1,25},{2,26},{3,27},{4,28},{5,29},{6,30},{7,31},{8,16},{9,... | collective-permute-start | bytes 294920 | tf_op jit(solution)/shard_map/ppermute | solution.py:26
  16.3 7.0 %slice-start.1 = ((s8[8388608]{0:T(1024)(128)(4,1)}), s8[4194304]{0:T(1024)(128)(4,1)S(1)}, s32[]{:S(2)}) async-start(s8[8388608]{0:T(1024)(128)(4,1)} %bitcast.3), calls=%async_computation.1 | async-start | bytes 8388608
  19.5 30.2 %collective-permute-start.10 = (bf16[768,256]{1,0:T(8,128)(2,1)S(1)}, bf16[768,256]{1,0:T(8,128)(2,1)S(1)}, u32[]{:S(2)}, u32[]{:S(2)}) collective-permute-start(bf16[768,256]{1,0:T(8,128)(2,1)S(1)} %get-tuple-element.41), channel_id=1, source_target_pairs={{0,1},{1,0},{2,3},{3,2},{4,5},{5,4},{6,7},{7,6},{8,9},{9,8},{10,11... | collective-permute-start | bytes 1179656 | tf_op jit(solution)/shard_map/ppermute | solution.py:26
  21.4 15.4 %collective-permute-start.7 = (bf16[768,256]{1,0:T(8,128)(2,1)S(1)}, bf16[768,256]{1,0:T(8,128)(2,1)S(1)}, u32[]{:S(2)}, u32[]{:S(2)}) collective-permute-start(bf16[768,256]{1,0:T(8,128)(2,1)S(1)} %get-tuple-element.41), channel_id=1, source_target_pairs={{0,8},{1,9},{2,10},{3,11},{4,12},{5,13},{6,14},{7,15},{8,0},{9,1},... | collective-permute-start | bytes 1179656 | tf_op jit(solution)/shard_map/ppermute | solution.py:26
  21.4 6.2 %collective-permute-start.3 = (bf16[192,256]{1,0:T(8,128)(2,1)S(1)}, bf16[192,256]{1,0:T(8,128)(2,1)S(1)}, u32[]{:S(2)}, u32[]{:S(2)}) collective-permute-start(bf16[192,256]{1,0:T(8,128)(2,1)S(1)} %sum_x.1._after.mine), channel_id=1, source_target_pairs={{0,2},{1,3},{2,0},{3,1},{4,6},{5,7},{6,4},{7,5},{8,10},{9,11},{10,... | collective-permute-start | bytes 294920 | tf_op jit(solution)/shard_map/ppermute | solution.py:26
  26.8 6.7 %collective-permute-start.5 = (bf16[192,256]{1,0:T(8,128)(2,1)S(1)}, bf16[192,256]{1,0:T(8,128)(2,1)S(1)}, u32[]{:S(2)}, u32[]{:S(2)}) collective-permute-start(bf16[192,256]{1,0:T(8,128)(2,1)S(1)} %get-tuple-element.37.coef1), channel_id=1, source_target_pairs={{0,24},{1,25},{2,26},{3,27},{4,28},{5,29},{6,30},{7,31},{8,16},{9,... | collective-permute-start | bytes 294920 | tf_op jit(solution)/shard_map/ppermute | solution.py:26
  27.7 5.8 %collective-permute-start.4 = (bf16[192,256]{1,0:T(8,128)(2,1)S(1)}, bf16[192,256]{1,0:T(8,128)(2,1)S(1)}, u32[]{:S(2)}, u32[]{:S(2)}) collective-permute-start(bf16[192,256]{1,0:T(8,128)(2,1)S(1)} %sum_z.1._after.own), channel_id=1, source_target_pairs={{0,6},{1,7},{2,4},{3,5},{4,2},{5,3},{6,0},{7,1},{8,14},{9,15},{10,... | collective-permute-start | bytes 294920 | tf_op jit(solution)/shard_map/ppermute | solution.py:26
  33.4 3.4 %copy-start.1 = (bf16[2048,256]{1,0:T(8,128)(2,1)S(1)}, bf16[2048,256]{1,0:T(8,128)(2,1)}, u32[]{:S(2)}) copy-start(bf16[2048,256]{1,0:T(8,128)(2,1)} %basis.7) | copy-start | bytes 3145732
  34.0 9.7 %collective-permute-start.6 = (bf16[384,256]{1,0:T(8,128)(2,1)S(1)}, bf16[384,256]{1,0:T(8,128)(2,1)S(1)}, u32[]{:S(2)}, u32[]{:S(2)}) collective-permute-start(bf16[384,256]{1,0:T(8,128)(2,1)S(1)} %get-tuple-element.39._after), channel_id=1, source_target_pairs={{0,96},{1,97},{2,98},{3,99},{4,100},{5,101},{6,102},{7,103},{8,104... | collective-permute-start | bytes 589832 | tf_op jit(solution)/shard_map/ppermute | solution.py:26
  40.2 9.5 %collective-permute-start.11 = (bf16[768,256]{1,0:T(8,128)(2,1)S(1)}, bf16[768,256]{1,0:T(8,128)(2,1)S(1)}, u32[]{:S(2)}, u32[]{:S(2)}) collective-permute-start(bf16[768,256]{1,0:T(8,128)(2,1)S(1)} %get-tuple-element.45.side_x), channel_id=1, source_target_pairs={{0,1},{1,0},{2,3},{3,2},{4,5},{5,4},{6,7},{7,6},{8,9},{9,8},{10,11... | collective-permute-start | bytes 1179656 | tf_op jit(solution)/shard_map/ppermute | solution.py:26
  42.9 6.5 %collective-permute-start.9 = (bf16[384,256]{1,0:T(8,128)(2,1)S(1)}, bf16[384,256]{1,0:T(8,128)(2,1)S(1)}, u32[]{:S(2)}, u32[]{:S(2)}) collective-permute-start(bf16[384,256]{1,0:T(8,128)(2,1)S(1)} %both.1._after), channel_id=1, source_target_pairs={{0,2},{1,3},{2,0},{3,1},{4,6},{5,7},{6,4},{7,5},{8,10},{9,11},{10,... | collective-permute-start | bytes 589832 | tf_op jit(solution)/shard_map/ppermute | solution.py:26
  43.7 6.5 %collective-permute-start.8 = (bf16[192,256]{1,0:T(8,128)(2,1)S(1)}, bf16[192,256]{1,0:T(8,128)(2,1)S(1)}, u32[]{:S(2)}, u32[]{:S(2)}) collective-permute-start(bf16[192,256]{1,0:T(8,128)(2,1)S(1)} %half.1._after), channel_id=1, source_target_pairs={{0,32},{1,33},{2,34},{3,35},{4,36},{5,37},{6,38},{7,39},{8,40},{9,... | collective-permute-start | bytes 294920 | tf_op jit(solution)/shard_map/ppermute | solution.py:26
  44.0 5.7 %copy-start.3 = (bf16[1,1,4,256,256]{4,3,2,1,0:T(8,128)(2,1)S(1)}, bf16[1,1,4,256,256]{4,3,2,1,0:T(8,128)(2,1)}, u32[]{:S(2)}) copy-start(bf16[1,1,4,256,256]{4,3,2,1,0:T(8,128)(2,1)} %param.13) | copy-start | bytes 1572868
  50.4 7.2 %collective-permute-start.13 = (bf16[192,256]{1,0:T(8,128)(2,1)S(1)}, bf16[192,256]{1,0:T(8,128)(2,1)S(1)}, u32[]{:S(2)}, u32[]{:S(2)}) collective-permute-start(bf16[192,256]{1,0:T(8,128)(2,1)S(1)} %down1.1._after.own), channel_id=1, source_target_pairs={{0,1},{1,0},{2,3},{3,2},{4,5},{5,4},{6,7},{7,6},{8,9},{9,8},{10,11... | collective-permute-start | bytes 294920 | tf_op jit(solution)/shard_map/ppermute | solution.py:26
  51.4 4.4 %collective-permute-start.12 = (bf16[192,256]{1,0:T(8,128)(2,1)S(1)}, bf16[192,256]{1,0:T(8,128)(2,1)S(1)}, u32[]{:S(2)}, u32[]{:S(2)}) collective-permute-start(bf16[192,256]{1,0:T(8,128)(2,1)S(1)} %down1.1._after.own), channel_id=1, source_target_pairs={{0,8},{1,9},{2,10},{3,11},{4,12},{5,13},{6,14},{7,15},{8,0},{9,1},... | collective-permute-start | bytes 294920 | tf_op jit(solution)/shard_map/ppermute | solution.py:26
  55.7 1.9 %collective-permute-start.14 = (bf16[192,256]{1,0:T(8,128)(2,1)S(1)}, bf16[192,256]{1,0:T(8,128)(2,1)S(1)}, u32[]{:S(2)}, u32[]{:S(2)}) collective-permute-start(bf16[192,256]{1,0:T(8,128)(2,1)S(1)} %gate.1._after.side), channel_id=1, source_target_pairs={{0,1},{1,0},{2,3},{3,2},{4,5},{5,4},{6,7},{7,6},{8,9},{9,8},{10,11... | collective-permute-start | bytes 294920 | tf_op jit(solution)/shard_map/ppermute | solution.py:26

commit v3 on v2

v3 whole, which is shorter than its diff:
```python
import functools

import jax
import jax.numpy as jnp
from jax import lax
from jax.experimental import pallas as pl
from jax.experimental.pallas import tpu as pltpu
from jax.sharding import PartitionSpec as P

AXES = ("gx", "gy")
F32 = jnp.float32
BF16 = jnp.bfloat16
LEAF = 2048
RANK = 256
NCOL = 768
HALF = NCOL // 2
QUARTER = NCOL // 4
VMEM = pl.BlockSpec(memory_space=pltpu.VMEM)
HBM = pl.BlockSpec(memory_space=pltpu.HBM)
ANY = pl.BlockSpec(memory_space=pl.ANY)
MIB = 1 << 20


def permute(array, dx=0, dy=0):
    pairs = [(gx * 8 + gy, (gx ^ dx) * 8 + (gy ^ dy)) for gx in range(16) for gy in range(8)]
    return lax.ppermute(array, AXES, pairs)


def nn(a, b):
    return jnp.dot(a, b, preferred_element_type=F32)


def nt(a, b):
    return lax.dot_general(a, b, (((1,), (1,)), ((), ())), preferred_element_type=F32)


def add(a, b):
    return (a[...].astype(F32) + b[...].astype(F32)).astype(BF16)


def core_index():
    return lax.rem(lax.axis_index("gy"), 2)


def part_index():
    x = lax.rem(lax.axis_index("gx"), 4)
    return jnp.where((x == 1) | (x == 2), 1, 0)


def call(kernel, name, outs, in_specs, flops=0, moved=0, scratch=(), limit=16, aliases=None, out_specs=None):
    return pl.pallas_call(
        kernel,
        out_shape=[jax.ShapeDtypeStruct(*o) for o in outs],
        in_specs=in_specs,
        out_specs=[VMEM] * len(outs) if out_specs is None else out_specs,
        scratch_shapes=list(scratch),
        input_output_aliases=aliases or {},
        compiler_params=pltpu.CompilerParams(vmem_limit_bytes=limit * MIB),
        cost_estimate=pl.CostEstimate(flops=flops, bytes_accessed=moved, transcendentals=0),
        name=name,
    )


def picks(order_row, base, rows):
    it = lax.broadcasted_iota(jnp.int32, (rows, LEAF), 0)
    return jnp.where(it == (order_row - base), 1.0, 0.0).astype(BF16)


def front_kernel(
    order_hbm, basis_hbm, x_hbm, leaf_hbm, coarse_hbm, top,
    send, keep, c_both, x, order, rows, leaf, coarse,
    basis, turned, lift, sems,
):
    pairs = [(order_hbm, order), (basis_hbm, basis), (x_hbm, x), (leaf_hbm, leaf), (coarse_hbm, coarse)]
    y = lax.axis_index("gx") // 4
    z = lax.axis_index("gy") // 4
    flip = jnp.where(lax.rem(y, 2) == 0, y + 1, y - 1)
    for d, there in enumerate((y, flip, 3 - y, 3 - flip)):
        r = pl.multiple_of((there * 2 + z) * RANK, RANK)
        s = pl.multiple_of(y * 2 * RANK, 2 * RANK)
        pairs.append((top.at[pl.ds(r, RANK), pl.ds(s, 2 * RANK)], rows.at[d]))
    fetches = [pltpu.make_async_copy(here, there, sems.at[i]) for i, (here, there) in enumerate(pairs)]
    for fetch in fetches:
        fetch.start()
    fetches[0].wait()
    fetches[1].wait()
    flat = basis[...].T
    for j in range(LEAF // 512):
        turned[:, j * 512 : (j + 1) * 512] = nt(flat, picks(order[...], j * 512, 512)).astype(BF16)
    fetches[2].wait()
    c = nn(turned[...], x[...]).astype(BF16).T
    c_both[:NCOL] = c
    send[HALF:] = c
    fetches[3].wait()
    lift[...] = nn(c, leaf[0]).astype(BF16)
    core = core_index()
    keep[...] = lift[pl.ds(pl.multiple_of(core * HALF, HALF), HALF), :]
    send[:HALF] = lift[pl.ds(pl.multiple_of((1 - core) * HALF, HALF), HALF), :]
    for fetch in fetches[4:]:
        fetch.wait()


def pair_kernel(keep, recv, _after, _c_both, send2, keep2, c_both, total):
    total[...] = (keep[...].astype(F32) + recv[:HALF].astype(F32)).astype(BF16)
    part = part_index()
    keep2[...] = total[pl.ds(pl.multiple_of(part * QUARTER, QUARTER), QUARTER), :]
    send2[...] = total[pl.ds(pl.multiple_of((1 - part) * QUARTER, QUARTER), QUARTER), :]
    c_both[NCOL:] = recv[HALF:]


def coarse_kernel(keep, recv, couple, _after, coef1, lift1):
    c = add(keep, recv)
    coef1[...] = c
    lift1[...] = nn(c, couple[0]).astype(BF16)


def sum_kernel(mine, recv, _after, total):
    total[...] = add(mine, recv)


def both_tops(own, other, keep_own):
    low = lax.axis_index("gy") < 4
    b = other[...]
    a = own[...] if keep_own else jnp.zeros_like(b)
    return jnp.concatenate([jnp.where(low, a, b), jnp.where(low, b, a)], axis=1)


def top_send_kernel(own, other, rows, _after, send):
    both = both_tops(own, other, True)
    send[:QUARTER] = nt(both, rows[2]).astype(BF16)
    send[QUARTER:] = nt(both, rows[3]).astype(BF16)


def top_stay_kernel(own, other, rows, _after, stay0, stay1):
    stay0[...] = nt(both_tops(own, other, False), rows[0])
    stay1[...] = nt(both_tops(own, other, True), rows[1])


def half_kernel(stay1, recv, _after, send):
    send[...] = (stay1[...] + recv[QUARTER:].astype(F32)).astype(BF16)


def near1_kernel(side_x, sides, couple, _after, near1):
    near1[...] = (
        nt(side_x[...], couple[1]) + nt(sides[:QUARTER], couple[2]) + nt(sides[QUARTER:], couple[3])
    )


def near0_kernel(sides, recv, couple, _after, near0):
    near0[...] = nt(couple[1], sides[:NCOL]) + nt(couple[2], recv[HALF:]) + nt(couple[3], sides[NCOL:])


def down1_kernel(stay0, first, second, near1, couple, _after, down1):
    d2 = (stay0[...] + first[:QUARTER].astype(F32) + second[...].astype(F32)).astype(BF16)
    down1[...] = (near1[...] + nt(d2, couple[0])).astype(BF16)


def gather_kernel(blocks, first, order, x, _after, *refs):
    out = refs[first]
    for start, size in blocks:
        parts = []
        for s in range(start, start + size, 128):
            column = jnp.broadcast_to(order[:, s : s + 128].astype(F32), (128, 128)).T
            lane = lax.broadcasted_iota(jnp.int32, (128, 128), 1).astype(F32)
            parts.append(
                jnp.concatenate(
                    [jnp.where(column == lane + 128.0 * j, 1.0, 0.0).astype(BF16) for j in range(LEAF // 128)], axis=1
                )
            )
        out[start : start + size] = nn(jnp.concatenate(parts, axis=0), x[...]).astype(BF16)


def dense_kernel(blocks, first, dense, ordered, _after, *refs):
    out = refs[first]
    for start, size in blocks:
        out[start : start + size] = nn(dense[start : start + size], ordered[...]).astype(BF16)


def scatter_kernel(blocks, first, order, result, basis, _after, *refs):
    out, turned = refs[first : first + 2]
    for start, size in blocks:
        hot = picks(order[...], start, size)
        out[start : start + size] = nn(hot, result[...]).astype(BF16)
        turned[start : start + size] = nn(hot, basis[...]).astype(BF16)


def both_kernel(coef1, side_x, _after, both):
    both[:QUARTER] = coef1[...]
    both[QUARTER:] = side_x[...]


def join_kernel(own, side, _after, joined):
    part = part_index()
    joined[pl.ds(pl.multiple_of(part * QUARTER, QUARTER), QUARTER), :] = own[...]
    joined[pl.ds(pl.multiple_of((1 - part) * QUARTER, QUARTER), QUARTER), :] = side[...]


def leaf_half(base, turned, down1, near0, couple, cols, out, after_block):
    down0 = (near0[:, cols] + nt(couple[0], down1[...])).astype(BF16)
    for start, size in ((0, 512), (512, 512), (1024, 512), (1536, 256), (1792, 128), (1920, 128)):
        rows = pl.ds(start, size)
        out[rows] = (base[rows, cols].astype(F32) + nn(turned[rows], down0)).astype(BF16)
        after_block(rows)


def half_columns(own):
    core = core_index()
    return pl.ds(pl.multiple_of((core if own else 1 - core) * HALF, HALF), HALF)


def own_half_kernel(base, turned, down1, near0, couple, out_hbm, out, sems):
    cols = half_columns(True)
    copies = []

    def write(rows):
        if rows.start < LEAF // 2:
            copies.append(pltpu.make_async_copy(out.at[rows], out_hbm.at[rows, cols], sems.at[len(copies)]))
            copies[-1].start()

    leaf_half(base, turned, down1, near0, couple, cols, out, write)
    for copy in copies:
        copy.wait()


def final_kernel(base, turned, down1, near0, couple, own, _product, out_hbm, out, sems):
    lower = pl.ds(LEAF // 2, LEAF // 2)
    copies = [pltpu.make_async_copy(own.at[lower], out_hbm.at[lower, half_columns(True)], sems.at[0])]
    copies[0].start()
    cols = half_columns(False)

    def write(rows):
        copies.append(pltpu.make_async_copy(out.at[rows], out_hbm.at[rows, cols], sems.at[len(copies)]))
        copies[-1].start()

    leaf_half(base, turned, down1, near0, couple, cols, out, write)
    for copy in copies:
        copy.wait()


def leaf_part(kernel, name, blocks, operands, previous, widths, after, carry=()):
    outs = [((LEAF, width), BF16) for width in widths]
    kept = list(previous) + list(carry)
    count = len(operands) + 1
    skip = len(outs) - len(previous)
    got = call(
        functools.partial(kernel, blocks, len(kept)),
        name,
        outs + [(c.shape, c.dtype) for c in carry],
        [VMEM] * len(operands) + [ANY] + [VMEM] * len(previous) + [ANY] * len(carry),
        flops=2 * sum(size for _, size in blocks) * LEAF * sum(widths),
        moved=4 * MIB,
        aliases={count + i: skip + i for i in range(len(kept))},
        out_specs=[VMEM] * len(outs) + [ANY] * len(carry),
    )(*operands, after, *kept)
    return (got[: len(outs)], *got[len(outs) :])


def local(right_block, point_order, leaf_dense, basis_in, basis_out, leaf_couple, coarse_couple, top_coupling):
    couple = ((4, RANK, RANK), BF16)
    quarter = ((QUARTER, RANK), BF16)
    quarter_f32 = ((QUARTER, RANK), F32)
    half = ((HALF, RANK), BF16)
    small = 2 * QUARTER * RANK * RANK
    widths = [NCOL, RANK]
    gather = functools.partial(leaf_part, gather_kernel, "gather")
    dense = functools.partial(leaf_part, dense_kernel, "dense")
    scatter = functools.partial(leaf_part, scatter_kernel, "scatter")

    inputs = (
        point_order.reshape(1, LEAF),
        basis_in,
        right_block,
        leaf_couple.reshape(4, RANK, RANK),
        coarse_couple.reshape(4, RANK, RANK),
        top_coupling,
    )
    send, keep, c_both, x, order, rows, leaf, coarse = call(
        front_kernel,
        "front",
        [
            ((HALF + NCOL, RANK), BF16),
            half,
            ((2 * NCOL, RANK), BF16),
            ((LEAF, NCOL), BF16),
            ((1, LEAF), jnp.int32),
            ((4, RANK, 2 * RANK), BF16),
            couple,
            couple,
        ],
        [HBM] * 6,
        flops=2 * LEAF * LEAF * RANK + 2 * LEAF * RANK * NCOL,
        moved=7 * MIB,
        scratch=[
            pltpu.VMEM((LEAF, RANK), BF16),
            pltpu.VMEM((RANK, LEAF), BF16),
            pltpu.VMEM((NCOL, RANK), BF16),
            pltpu.SemaphoreType.DMA((9,)),
        ],
    )(*(pltpu.with_memory_space_constraint(a, pltpu.HBM) for a in inputs))
    recv = permute(send, dy=1)
    (ordered,) = gather([(0, 512)], [order, x], [], [NCOL], send)

    send2, keep2, c_both = call(
        pair_kernel,
        "pair",
        [quarter, quarter, ((2 * NCOL, RANK), BF16)],
        [VMEM, VMEM, ANY, VMEM],
        scratch=[pltpu.VMEM((HALF, RANK), BF16)],
        aliases={3: 2},
    )(keep, recv, ordered[0], c_both)
    recv2 = permute(send2, dx=1)
    (ordered,) = gather([(512, 640), (1152, 512)], [order, x], ordered, [NCOL], send2)

    coef1, lift1 = call(coarse_kernel, "coarse", [quarter, quarter], [VMEM, VMEM, VMEM, ANY], flops=small)(
        keep2, recv2, coarse, ordered[0]
    )
    recv3 = permute(lift1, dx=3)
    ordered, c_both = gather([(1664, 384)], [order, x], ordered, [NCOL], lift1, [c_both])
    sides = permute(c_both, dx=1)
    (result,) = dense([(0, 256)], [leaf_dense, ordered[0]], [], [NCOL], c_both)

    pair = call(sum_kernel, "sum_x", [quarter], [VMEM, VMEM, ANY])(lift1, recv3, result[0])[0]
    recv4 = permute(pair, dy=2)
    result, coef1 = dense([(256, 640)], [leaf_dense, ordered[0]], result, [NCOL], pair, [coef1])
    coarse_x = permute(coef1, dx=3)

    coef2 = call(sum_kernel, "sum_z", [quarter], [VMEM, VMEM, ANY])(pair, recv4, result[0])[0]
    recv5 = permute(coef2, dy=6)
    (result,) = dense([(896, 640)], [leaf_dense, ordered[0]], result, [NCOL], coef2)
    both = call(both_kernel, "both", [half], [VMEM, VMEM, ANY])(coef1, coarse_x, result[0])[0]
    coarse_yz = permute(both, dy=2)

    send6 = call(top_send_kernel, "top_send", [half], [VMEM, VMEM, VMEM, ANY], flops=4 * small)(
        coef2, recv5, rows, both
    )[0]
    recv6 = permute(send6, dx=12)
    stay0, stay1 = call(
        top_stay_kernel, "top_stay", [quarter_f32, quarter_f32], [VMEM, VMEM, VMEM, ANY], flops=4 * small
    )(coef2, recv5, rows, send6)
    (result,) = dense([(1536, 512)], [leaf_dense, ordered[0]], result, [NCOL], stay0)
    (scattered,) = scatter([(0, 640)], [order, result[0], basis_out], [], widths, stay0)

    send7 = call(half_kernel, "half", [quarter], [VMEM, VMEM, ANY])(stay1, recv6, scattered[0])[0]
    recv7 = permute(send7, dx=4)
    near1 = call(near1_kernel, "near1", [quarter_f32], [VMEM, VMEM, VMEM, ANY], flops=3 * small)(
        coarse_x, coarse_yz, coarse, send7
    )[0]
    (scattered,) = scatter([(640, 352), (992, 352)], [order, result[0], basis_out], scattered, widths, near1)

    down1 = call(down1_kernel, "down1", [quarter], [VMEM] * 5 + [ANY], flops=small)(
        stay0, recv6, recv7, near1, coarse, scattered[0]
    )[0]
    side = permute(down1, dx=1)
    near0 = call(near0_kernel, "near0", [((RANK, NCOL), F32)], [VMEM] * 3 + [ANY], flops=12 * small)(
        sides, recv, leaf, down1
    )[0]
    (scattered,) = scatter([(1344, 352), (1696, 352)], [order, result[0], basis_out], scattered, widths, near0)

    mine = call(join_kernel, "join", [half], [VMEM, VMEM, ANY])(down1, side, scattered[0])[0]
    other = permute(mine, dy=1)
    whole = ((LEAF, NCOL), BF16)
    product, own = call(
        own_half_kernel,
        "own_half",
        [whole, ((LEAF, HALF), BF16)],
        [VMEM] * 5,
        flops=LEAF * RANK * NCOL,
        moved=2 * MIB,
        scratch=[pltpu.SemaphoreType.DMA((2,))],
        out_specs=[HBM, VMEM],
    )(*scattered, mine, near0, leaf)
    return call(
        final_kernel,
        "final",
        [whole],
        [VMEM] * 6 + [HBM],
        flops=LEAF * RANK * NCOL,
        moved=4 * MIB,
        scratch=[pltpu.VMEM((LEAF, HALF), BF16), pltpu.SemaphoreType.DMA((7,))],
        out_specs=[HBM],
        aliases={6: 0},
    )(*scattered, other, near0, leaf, own, product)[0]


def solution(mesh):
    in_specs = (
        P(("gx", "gy"), None),
        P("gx", "gy", None),
        P(("gx", "gy"), None),
        P(("gx", "gy"), None),
        P(("gx", "gy"), None),
        P("gx", "gy", None, None, None),
        P("gx", "gy", None, None, None),
        P(),
    )
    out_specs = P(("gx", "gy"), None)
    return jax.shard_map(local, mesh=mesh, in_specs=in_specs, out_specs=out_specs, check_vma=False)
```

time: 60.3 us -> 55.6 us (0.922)
  waiting for transfers between devices: 4.6 us -> 0.54 us
    ppermute x15 -> x12, waiting for transfers between devices: 4.6 us -> 0.54 us  [permute(): return lax.ppermute(array, AXES, pairs)]
    ppermute x15 -> x12, starting transfers between devices: 20.6 us -> 20.3 us  [permute(): return lax.ppermute(array, AXES, pairs)]
    pallas_call x8 -> x9, Pallas kernels: 10.5 us -> 10.2 us  [the longest x1 5.53 us: local(): call(front_kernel, 'front', [((HALF + NCOL, RANK), BF16), half, ((2 * NCO...]
    pallas_call x9 -> x10, Pallas kernels: 23.4 us -> 23.5 us  [leaf_part(): call(functools.partial(kernel, blocks, len(kept)), name, outs + [(c.shape...]
  transfers between devices with their start and end apart: 15 -> 12, of which waited for: 2 -> 1; matrix products, arithmetic and copies ran while one was open for 0% -> 0% of each run, Pallas kernels for 43% -> 48%
where the time goes in v3:
time: 55.6 us; the launch traced here: 55.5 us
  Pallas kernels  34.2 us (62%)
  starting transfers between devices  20.3 us (37%)
    pallas_call x10, Pallas kernels, leaf_part(): call(functools.partial(kernel, blocks, len(kept)), name, outs + [(c.shape...  23.5 us
    ppermute x12, starting transfers between devices, permute(): return lax.ppermute(array, AXES, pairs)  20.3 us
    pallas_call x1, Pallas kernels, local(): call(front_kernel, 'front', [((HALF + NCOL, RANK), BF16), half, ((2 * NCO...  5.53 us
    pallas_call x1, Pallas kernels, local(): call(final_kernel, 'final', [whole], [VMEM] * 6 + [HBM], flops=LEAF * RAN...  1.74 us
    pallas_call x1, Pallas kernels, local(): call(own_half_kernel, 'own_half', [whole, ((LEAF, HALF), BF16)], [VMEM] *...  1.44 us
  transfers between devices with their start and end apart: 12, of which 1 were waited for; matrix products, arithmetic and copies ran while one was open for 0% of the time, Pallas kernels for 48%

profile of v3, /device:TPU:1, one launch (start us, length us, event | category | flops | bytes accessed | tf_op | source)
XLA Modules:
  0.0 55.5 jit_solution(16361360293615669149)
XLA Ops:
  0.0 5.5 %front.1 = (bf16[1152,256]{1,0:T(8,128)(2,1)S(1)}, bf16[384,256]{1,0:T(8,128)(2,1)S(1)}, bf16[1536,256]{1,0:T(8,128)(2,1)S(1)}, bf16[2048,768]{1,0:T(8,128)(2,1)...) custom-call(s32[1,2048]{1,0:T(1,128)} %bitcast.7, ...), custom_call_target="tpu_custom_call" | custom-call | flops 2952790016 | bytes 7340032 | tf_op jit(solution)/shard_map/front/pallas_call | solution.py:277
  5.5 1.5 %collective-permute-start = (bf16[1152,256]{1,0:T(8,128)(2,1)S(1)}, bf16[1152,256]{1,0:T(8,128)(2,1)S(1)}, u32[]{:S(2)}, u32[]{:S(2)}) collective-permute-start(bf16[1152,256]{1,0:T(8,128)(2,1)S(1)} %get-tuple-element.35._after), channel_id=1, source_target_pairs={{0,1},{1,0},{2,3},{3,2},{4,5},{5,4},{6,7},{7,6},{8,9},{9,8},{10,11... | collective-permute-start | bytes 1769480 | tf_op jit(solution)/shard_map/ppermute | solution.py:26
  7.0 1.8 %gather.3._after.refs_0_ = bf16[2048,768]{1,0:T(8,128)(2,1)S(1)} custom-call(s32[1,2048]{1,0:T(1,128)S(1)} %get-tuple-element.32.order, bf16[2048,768]{1,0:T(8,128)(2,1)S(1)} %get-tuple-element.33.x, bf16[1152,256]{1,0:T(8,128)(2,1)S(1)} %get-tuple-element.35._after), custom_call_target="tpu_custom_call" | custom-call | flops 1610612736 | bytes 4194304 | tf_op jit(solution)/shard_map/gather/pallas_call | solution.py:245
  9.0 1.4 %collective-permute-start.1 = (bf16[192,256]{1,0:T(8,128)(2,1)S(1)}, bf16[192,256]{1,0:T(8,128)(2,1)S(1)}, u32[]{:S(2)}, u32[]{:S(2)}) collective-permute-start(bf16[192,256]{1,0:T(8,128)(2,1)S(1)} %get-tuple-element.38._after), channel_id=1, source_target_pairs={{0,8},{1,9},{2,10},{3,11},{4,12},{5,13},{6,14},{7,15},{8,0},{9,1},... | collective-permute-start | bytes 294920 | tf_op jit(solution)/shard_map/ppermute | solution.py:26
  10.4 3.9 %gather.4._after.refs_0_ = bf16[2048,768]{1,0:T(8,128)(2,1)S(1)} custom-call(s32[1,2048]{1,0:T(1,128)S(1)} %get-tuple-element.32.order, bf16[2048,768]{1,0:T(8,128)(2,1)S(1)} %get-tuple-element.33.x, bf16[192,256]{1,0:T(8,128)(2,1)S(1)} %get-tuple-element.38._after, bf16[2048,768]{1,0:T(8,128)(2,1)S(1)} %gather.3._after.refs_0_), custom_call_target="tpu_custom_call", output_to_operand_aliasing={{}: (3, {})} | custom-call | flops 3623878656 | bytes 4194304 | tf_op jit(solution)/shard_map/gather/pallas_call | solution.py:245
  14.5 1.9 %collective-permute-start.2 = (bf16[192,256]{1,0:T(8,128)(2,1)S(1)}, bf16[192,256]{1,0:T(8,128)(2,1)S(1)}, u32[]{:S(2)}, u32[]{:S(2)}) collective-permute-start(bf16[192,256]{1,0:T(8,128)(2,1)S(1)} %get-tuple-element.40._after.mine), channel_id=1, source_target_pairs={{0,24},{1,25},{2,26},{3,27},{4,28},{5,29},{6,30},{7,31},{8,16},{9,... | collective-permute-start | bytes 294920 | tf_op jit(solution)/shard_map/ppermute | solution.py:26
  16.4 1.4 %gather.5 = (bf16[2048,768]{1,0:T(8,128)(2,1)S(1)}, bf16[1536,256]{1,0:T(8,128)(2,1)S(1)}) custom-call(s32[1,2048]{1,0:T(1,128)S(1)} %get-tuple-element.32.order, bf16[2048,768]{1,0:T(8,128)(2,1)S(1)} %get-tuple-element.33.x, bf16[192,256]{1,0:T(8,128)(2,1)S(1)} %get-tuple-element.40._after.mine, ...), custom_call_target="tpu_custom_call", output_to_operand_aliasing={{0}: (3, {}), {1}: (4, {})} | custom-call | flops 1207959552 | bytes 4194304 | tf_op jit(solution)/shard_map/gather/pallas_call | solution.py:245
  18.2 1.0 %dense.8._after.refs_0_ = bf16[2048,768]{1,0:T(8,128)(2,1)S(1)} custom-call(bf16[2048,2048]{1,0:T(8,128)(2,1)S(1)} %bitcast.4, bf16[2048,768]{1,0:T(8,128)(2,1)S(1)} %get-tuple-element.42.ordered, bf16[1536,256]{1,0:T(8,128)(2,1)S(1)} %get-tuple-element.43._after), custom_call_target="tpu_custom_call" | custom-call | flops 805306368 | bytes 4194304 | tf_op jit(solution)/shard_map/dense/pallas_call | solution.py:245
  19.2 0.5 collective-permute-done.2.recv
  19.7 1.9 %collective-permute-start.3 = (bf16[192,256]{1,0:T(8,128)(2,1)S(1)}, bf16[192,256]{1,0:T(8,128)(2,1)S(1)}, u32[]{:S(2)}, u32[]{:S(2)}) collective-permute-start(bf16[192,256]{1,0:T(8,128)(2,1)S(1)} %sum_x.1._after.mine), channel_id=1, source_target_pairs={{0,2},{1,3},{2,0},{3,1},{4,6},{5,7},{6,4},{7,5},{8,10},{9,11},{10,... | collective-permute-start | bytes 294920 | tf_op jit(solution)/shard_map/ppermute | solution.py:26
  21.6 2.2 %dense.10 = (bf16[2048,768]{1,0:T(8,128)(2,1)S(1)}, bf16[192,256]{1,0:T(8,128)(2,1)S(1)}) custom-call(bf16[2048,2048]{1,0:T(8,128)(2,1)S(1)} %bitcast.4, bf16[2048,768]{1,0:T(8,128)(2,1)S(1)} %get-tuple-element.42.ordered, bf16[192,256]{1,0:T(8,128)(2,1)S(1)} %sum_x.1._after.mine, ...), custom_call_target="tpu_custom_call", output_to_operand_aliasing={{0}: (3, {}), {1}: (4, {})} | custom-call | flops 2013265920 | bytes 4194304 | tf_op jit(solution)/shard_map/dense/pallas_call | solution.py:245
  23.8 1.4 %collective-permute-start.5 = (bf16[192,256]{1,0:T(8,128)(2,1)S(1)}, bf16[192,256]{1,0:T(8,128)(2,1)S(1)}, u32[]{:S(2)}, u32[]{:S(2)}) collective-permute-start(bf16[192,256]{1,0:T(8,128)(2,1)S(1)} %get-tuple-element.47.coef1), channel_id=1, source_target_pairs={{0,24},{1,25},{2,26},{3,27},{4,28},{5,29},{6,30},{7,31},{8,16},{9,... | collective-permute-start | bytes 294920 | tf_op jit(solution)/shard_map/ppermute | solution.py:26
  25.3 2.3 %collective-permute-start.4 = (bf16[192,256]{1,0:T(8,128)(2,1)S(1)}, bf16[192,256]{1,0:T(8,128)(2,1)S(1)}, u32[]{:S(2)}, u32[]{:S(2)}) collective-permute-start(bf16[192,256]{1,0:T(8,128)(2,1)S(1)} %sum_z.1._after.own), channel_id=1, source_target_pairs={{0,6},{1,7},{2,4},{3,5},{4,2},{5,3},{6,0},{7,1},{8,14},{9,15},{10,... | collective-permute-start | bytes 294920 | tf_op jit(solution)/shard_map/ppermute | solution.py:26
  27.6 2.2 %dense.12._after.refs_0_ = bf16[2048,768]{1,0:T(8,128)(2,1)S(1)} custom-call(bf16[2048,2048]{1,0:T(8,128)(2,1)S(1)} %bitcast.4, bf16[2048,768]{1,0:T(8,128)(2,1)S(1)} %get-tuple-element.42.ordered, bf16[192,256]{1,0:T(8,128)(2,1)S(1)} %sum_z.1._after.own, bf16[2048,768]{1,0:T(8,128)(2,1)S(1)} %get-tuple-element.45._after.refs_0_), custom_call_target="tpu_custom_call", output_to_operand_aliasing={{}: (3, {})} | custom-call | flops 2013265920 | bytes 4194304 | tf_op jit(solution)/shard_map/dense/pallas_call | solution.py:245
  29.8 0.8 %collective-permute-start.9 = (bf16[384,256]{1,0:T(8,128)(2,1)S(1)}, bf16[384,256]{1,0:T(8,128)(2,1)S(1)}, u32[]{:S(2)}, u32[]{:S(2)}) collective-permute-start(bf16[384,256]{1,0:T(8,128)(2,1)S(1)} %both.1._after), channel_id=1, source_target_pairs={{0,2},{1,3},{2,0},{3,1},{4,6},{5,7},{6,4},{7,5},{8,10},{9,11},{10,... | collective-permute-start | bytes 589832 | tf_op jit(solution)/shard_map/ppermute | solution.py:26
  31.0 2.8 %collective-permute-start.7 = (bf16[384,256]{1,0:T(8,128)(2,1)S(1)}, bf16[384,256]{1,0:T(8,128)(2,1)S(1)}, u32[]{:S(2)}, u32[]{:S(2)}) collective-permute-start(bf16[384,256]{1,0:T(8,128)(2,1)S(1)} %top_send.1._after), channel_id=1, source_target_pairs={{0,96},{1,97},{2,98},{3,99},{4,100},{5,101},{6,102},{7,103},{8,104... | collective-permute-start | bytes 589832 | tf_op jit(solution)/shard_map/ppermute | solution.py:26
  34.1 1.8 %dense.14.result = bf16[2048,768]{1,0:T(8,128)(2,1)S(1)} custom-call(bf16[2048,2048]{1,0:T(8,128)(2,1)S(1)} %bitcast.4, bf16[2048,768]{1,0:T(8,128)(2,1)S(1)} %get-tuple-element.42.ordered, f32[192,256]{1,0:T(8,128)S(1)} %get-tuple-element.48._after.stay0, bf16[2048,768]{1,0:T(8,128)(2,1)S(1)} %dense.12._after.refs_0_), custom_call_target="tpu_custom_call", output_to_operand_aliasing={{}: (3, {})} | custom-call | flops 1610612736 | bytes 4194304 | tf_op jit(solution)/shard_map/dense/pallas_call | solution.py:245
  35.9 2.9 %scatter.3 = (bf16[2048,768]{1,0:T(8,128)(2,1)S(1)}, bf16[2048,256]{1,0:T(8,128)(2,1)S(1)}) custom-call(s32[1,2048]{1,0:T(1,128)S(1)} %get-tuple-element.32.order, bf16[2048,768]{1,0:T(8,128)(2,1)S(1)} %dense.14.result, bf16[2048,256]{1,0:T(8,128)(2,1)S(1)} %copy-done, f32[192,256]{1,0:T(8,128)S(1)} %get-tuple-element.48._after.stay0), custom_call_target="tpu_custom_call" | custom-call | flops 2684354560 | bytes 4194304 | tf_op jit(solution)/shard_map/scatter/pallas_call | solution.py:245
  39.3 3.2 %scatter.4 = (bf16[2048,768]{1,0:T(8,128)(2,1)S(1)}, bf16[2048,256]{1,0:T(8,128)(2,1)S(1)}) custom-call(s32[1,2048]{1,0:T(1,128)S(1)} %get-tuple-element.32.order, bf16[2048,768]{1,0:T(8,128)(2,1)S(1)} %dense.14.result, bf16[2048,256]{1,0:T(8,128)(2,1)S(1)} %copy-done, f32[192,256]{1,0:T(8,128)S(1)} %near1.1._after, ...), custom_call_target="tpu_custom_call", output_to_operand_aliasing={{0}: (4, {}), {1}: (5, {})} | custom-call | flops 2952790016 | bytes 4194304 | tf_op jit(solution)/shard_map/scatter/pallas_call | solution.py:245
  43.0 0.5 near0.1._after
  43.5 3.2 %scatter.5 = (bf16[2048,768]{1,0:T(8,128)(2,1)S(1)}, bf16[2048,256]{1,0:T(8,128)(2,1)S(1)}) custom-call(s32[1,2048]{1,0:T(1,128)S(1)} %get-tuple-element.32.order, bf16[2048,768]{1,0:T(8,128)(2,1)S(1)} %dense.14.result, bf16[2048,256]{1,0:T(8,128)(2,1)S(1)} %copy-done, f32[256,768]{1,0:T(8,128)S(1)} %near0.1._after, ...), custom_call_target="tpu_custom_call", output_to_operand_aliasing={{0}: (4, {}), {1}: (5, {})} | custom-call | flops 2952790016 | bytes 4194304 | tf_op jit(solution)/shard_map/scatter/pallas_call | solution.py:245
  46.7 5.4 %collective-permute-start.11 = (bf16[384,256]{1,0:T(8,128)(2,1)S(1)}, bf16[384,256]{1,0:T(8,128)(2,1)S(1)}, u32[]{:S(2)}, u32[]{:S(2)}) collective-permute-start(bf16[384,256]{1,0:T(8,128)(2,1)S(1)} %join.1.down1), channel_id=1, source_target_pairs={{0,1},{1,0},{2,3},{3,2},{4,5},{5,4},{6,7},{7,6},{8,9},{9,8},{10,11... | collective-permute-start | bytes 589832 | tf_op jit(solution)/shard_map/ppermute | solution.py:26
  52.1 1.4 %own_half.1 = (bf16[2048,768]{1,0:T(8,128)(2,1)}, bf16[2048,384]{1,0:T(8,128)(2,1)S(1)}) custom-call(bf16[2048,768]{1,0:T(8,128)(2,1)S(1)} %get-tuple-element.55._after.base, bf16[2048,256]{1,0:T(8,128)(2,1)S(1)} %get-tuple-element.56.turned, bf16[384,256]{1,0:T(8,128)(2,1)S(1)} %join.1.down1, f32[256,768]{1,0:T(8,128)S(1)} %near0.1._after, ...), custom_call_target="tpu_custom_call" | custom-call | flops 402653184 | bytes 2097152 | tf_op jit(solution)/shard_map/own_half/pallas_call | solution.py:362
  53.6 1.7 %final.1 = bf16[2048,768]{1,0:T(8,128)(2,1)} custom-call(bf16[2048,768]{1,0:T(8,128)(2,1)S(1)} %get-tuple-element.55._after.base, bf16[2048,256]{1,0:T(8,128)(2,1)S(1)} %get-tuple-element.56.turned, bf16[384,256]{1,0:T(8,128)(2,1)S(1)} %collective-permute-done.11.down1, f32[256,768]{1,0:T(8,128)S(1)} %near0.1._after, ...), custom_call_target="tpu_custom_call", output_to_operand_aliasing={{}: (6, {})} | custom-call | flops 402653184 | bytes 4194304 | tf_op jit(solution)/shard_map/final/pallas_call | solution.py:372
  (32 shorter events, 2.4 us)
Async XLA Ops:
  5.5 3.3 %collective-permute-start = (bf16[1152,256]{1,0:T(8,128)(2,1)S(1)}, bf16[1152,256]{1,0:T(8,128)(2,1)S(1)}, u32[]{:S(2)}, u32[]{:S(2)}) collective-permute-start(bf16[1152,256]{1,0:T(8,128)(2,1)S(1)} %get-tuple-element.35._after), channel_id=1, source_target_pairs={{0,1},{1,0},{2,3},{3,2},{4,5},{5,4},{6,7},{7,6},{8,9},{9,8},{10,11... | collective-permute-start | bytes 1769480 | tf_op jit(solution)/shard_map/ppermute | solution.py:26
  8.9 9.3 %slice-start = ((s8[8388608]{0:T(1024)(128)(4,1)}), s8[4194304]{0:T(1024)(128)(4,1)S(1)}, s32[]{:S(2)}) async-start(s8[8388608]{0:T(1024)(128)(4,1)} %bitcast.3), calls=%async_computation | async-start | bytes 8388608
  9.0 9.2 %slice-start.1 = ((s8[8388608]{0:T(1024)(128)(4,1)}), s8[4194304]{0:T(1024)(128)(4,1)S(1)}, s32[]{:S(2)}) async-start(s8[8388608]{0:T(1024)(128)(4,1)} %bitcast.3), calls=%async_computation.1 | async-start | bytes 8388608
  9.0 5.2 %collective-permute-start.1 = (bf16[192,256]{1,0:T(8,128)(2,1)S(1)}, bf16[192,256]{1,0:T(8,128)(2,1)S(1)}, u32[]{:S(2)}, u32[]{:S(2)}) collective-permute-start(bf16[192,256]{1,0:T(8,128)(2,1)S(1)} %get-tuple-element.38._after), channel_id=1, source_target_pairs={{0,8},{1,9},{2,10},{3,11},{4,12},{5,13},{6,14},{7,15},{8,0},{9,1},... | collective-permute-start | bytes 294920 | tf_op jit(solution)/shard_map/ppermute | solution.py:26
  14.5 5.2 %collective-permute-start.2 = (bf16[192,256]{1,0:T(8,128)(2,1)S(1)}, bf16[192,256]{1,0:T(8,128)(2,1)S(1)}, u32[]{:S(2)}, u32[]{:S(2)}) collective-permute-start(bf16[192,256]{1,0:T(8,128)(2,1)S(1)} %get-tuple-element.40._after.mine), channel_id=1, source_target_pairs={{0,24},{1,25},{2,26},{3,27},{4,28},{5,29},{6,30},{7,31},{8,16},{9,... | collective-permute-start | bytes 294920 | tf_op jit(solution)/shard_map/ppermute | solution.py:26
  17.8 25.2 %collective-permute-start.6 = (bf16[1536,256]{1,0:T(8,128)(2,1)S(1)}, bf16[1536,256]{1,0:T(8,128)(2,1)S(1)}, u32[]{:S(2)}, u32[]{:S(2)}) collective-permute-start(bf16[1536,256]{1,0:T(8,128)(2,1)S(1)} %get-tuple-element.43._after), channel_id=1, source_target_pairs={{0,8},{1,9},{2,10},{3,11},{4,12},{5,13},{6,14},{7,15},{8,0},{9,1},... | collective-permute-start | bytes 2359304 | tf_op jit(solution)/shard_map/ppermute | solution.py:26
  19.7 5.5 %collective-permute-start.3 = (bf16[192,256]{1,0:T(8,128)(2,1)S(1)}, bf16[192,256]{1,0:T(8,128)(2,1)S(1)}, u32[]{:S(2)}, u32[]{:S(2)}) collective-permute-start(bf16[192,256]{1,0:T(8,128)(2,1)S(1)} %sum_x.1._after.mine), channel_id=1, source_target_pairs={{0,2},{1,3},{2,0},{3,1},{4,6},{5,7},{6,4},{7,5},{8,10},{9,11},{10,... | collective-permute-start | bytes 294920 | tf_op jit(solution)/shard_map/ppermute | solution.py:26
  23.8 6.0 %collective-permute-start.5 = (bf16[192,256]{1,0:T(8,128)(2,1)S(1)}, bf16[192,256]{1,0:T(8,128)(2,1)S(1)}, u32[]{:S(2)}, u32[]{:S(2)}) collective-permute-start(bf16[192,256]{1,0:T(8,128)(2,1)S(1)} %get-tuple-element.47.coef1), channel_id=1, source_target_pairs={{0,24},{1,25},{2,26},{3,27},{4,28},{5,29},{6,30},{7,31},{8,16},{9,... | collective-permute-start | bytes 294920 | tf_op jit(solution)/shard_map/ppermute | solution.py:26
  25.3 5.4 %collective-permute-start.4 = (bf16[192,256]{1,0:T(8,128)(2,1)S(1)}, bf16[192,256]{1,0:T(8,128)(2,1)S(1)}, u32[]{:S(2)}, u32[]{:S(2)}) collective-permute-start(bf16[192,256]{1,0:T(8,128)(2,1)S(1)} %sum_z.1._after.own), channel_id=1, source_target_pairs={{0,6},{1,7},{2,4},{3,5},{4,2},{5,3},{6,0},{7,1},{8,14},{9,15},{10,... | collective-permute-start | bytes 294920 | tf_op jit(solution)/shard_map/ppermute | solution.py:26
  29.8 9.1 %collective-permute-start.9 = (bf16[384,256]{1,0:T(8,128)(2,1)S(1)}, bf16[384,256]{1,0:T(8,128)(2,1)S(1)}, u32[]{:S(2)}, u32[]{:S(2)}) collective-permute-start(bf16[384,256]{1,0:T(8,128)(2,1)S(1)} %both.1._after), channel_id=1, source_target_pairs={{0,2},{1,3},{2,0},{3,1},{4,6},{5,7},{6,4},{7,5},{8,10},{9,11},{10,... | collective-permute-start | bytes 589832 | tf_op jit(solution)/shard_map/ppermute | solution.py:26
  31.0 7.8 %collective-permute-start.7 = (bf16[384,256]{1,0:T(8,128)(2,1)S(1)}, bf16[384,256]{1,0:T(8,128)(2,1)S(1)}, u32[]{:S(2)}, u32[]{:S(2)}) collective-permute-start(bf16[384,256]{1,0:T(8,128)(2,1)S(1)} %top_send.1._after), channel_id=1, source_target_pairs={{0,96},{1,97},{2,98},{3,99},{4,100},{5,101},{6,102},{7,103},{8,104... | collective-permute-start | bytes 589832 | tf_op jit(solution)/shard_map/ppermute | solution.py:26
  34.1 1.8 %copy-start = (bf16[2048,256]{1,0:T(8,128)(2,1)S(1)}, bf16[2048,256]{1,0:T(8,128)(2,1)}, u32[]{:S(2)}) copy-start(bf16[2048,256]{1,0:T(8,128)(2,1)} %basis.5) | copy-start | bytes 3145732
  38.9 3.6 %collective-permute-start.8 = (bf16[192,256]{1,0:T(8,128)(2,1)S(1)}, bf16[192,256]{1,0:T(8,128)(2,1)S(1)}, u32[]{:S(2)}, u32[]{:S(2)}) collective-permute-start(bf16[192,256]{1,0:T(8,128)(2,1)S(1)} %half.1._after), channel_id=1, source_target_pairs={{0,32},{1,33},{2,34},{3,35},{4,36},{5,37},{6,38},{7,39},{8,40},{9,... | collective-permute-start | bytes 294920 | tf_op jit(solution)/shard_map/ppermute | solution.py:26
  42.7 4.0 %collective-permute-start.10 = (bf16[192,256]{1,0:T(8,128)(2,1)S(1)}, bf16[192,256]{1,0:T(8,128)(2,1)S(1)}, u32[]{:S(2)}, u32[]{:S(2)}) collective-permute-start(bf16[192,256]{1,0:T(8,128)(2,1)S(1)} %down1.1._after.own), channel_id=1, source_target_pairs={{0,8},{1,9},{2,10},{3,11},{4,12},{5,13},{6,14},{7,15},{8,0},{9,1},... | collective-permute-start | bytes 294920 | tf_op jit(solution)/shard_map/ppermute | solution.py:26
  46.7 6.9 %collective-permute-start.11 = (bf16[384,256]{1,0:T(8,128)(2,1)S(1)}, bf16[384,256]{1,0:T(8,128)(2,1)S(1)}, u32[]{:S(2)}, u32[]{:S(2)}) collective-permute-start(bf16[384,256]{1,0:T(8,128)(2,1)S(1)} %join.1.down1), channel_id=1, source_target_pairs={{0,1},{1,0},{2,3},{3,2},{4,5},{5,4},{6,7},{7,6},{8,9},{9,8},{10,11... | collective-permute-start | bytes 589832 | tf_op jit(solution)/shard_map/ppermute | solution.py:26

commit v4 on v3

--- a/solution.py
+++ b/solution.py
@@ -42,6 +42,11 @@
     return lax.rem(lax.axis_index("gy"), 2)
 
 
+def half_columns(own):
+    core = core_index()
+    return pl.ds(pl.multiple_of((core if own else 1 - core) * HALF, HALF), HALF)
+
+
 def part_index():
     x = lax.rem(lax.axis_index("gx"), 4)
     return jnp.where((x == 1) | (x == 2), 1, 0)
@@ -68,8 +73,8 @@
 
 def front_kernel(
     order_hbm, basis_hbm, x_hbm, leaf_hbm, coarse_hbm, top,
-    send, keep, c_both, x, order, rows, leaf, coarse,
-    basis, turned, lift, sems,
+    send, c_both, x, order, turned, rows, leaf, coarse,
+    basis, sems,
 ):
     pairs = [(order_hbm, order), (basis_hbm, basis), (x_hbm, x), (leaf_hbm, leaf), (coarse_hbm, coarse)]
     y = lax.axis_index("gx") // 4
@@ -88,24 +93,32 @@
     for j in range(LEAF // 512):
         turned[:, j * 512 : (j + 1) * 512] = nt(flat, picks(order[...], j * 512, 512)).astype(BF16)
     fetches[2].wait()
-    c = nn(turned[...], x[...]).astype(BF16).T
-    c_both[:NCOL] = c
-    send[HALF:] = c
     fetches[3].wait()
-    lift[...] = nn(c, leaf[0]).astype(BF16)
-    core = core_index()
-    keep[...] = lift[pl.ds(pl.multiple_of(core * HALF, HALF), HALF), :]
-    send[:HALF] = lift[pl.ds(pl.multiple_of((1 - core) * HALF, HALF), HALF), :]
+    cols = half_columns(False)
+    c = nn(turned[...], x[:, cols]).astype(BF16).T
+    c_both[cols] = c
+    send[...] = nn(c, leaf[0]).astype(BF16)
     for fetch in fetches[4:]:
         fetch.wait()
 
 
-def pair_kernel(keep, recv, _after, _c_both, send2, keep2, c_both, total):
-    total[...] = (keep[...].astype(F32) + recv[:HALF].astype(F32)).astype(BF16)
+def own_coef_kernel(turned, x, leaf, _c_both, _after, keep, c_both, c_own):
+    cols = half_columns(True)
+    c = nn(turned[...], x[:, cols]).astype(BF16).T
+    c_both[cols] = c
+    keep[...] = nn(c, leaf[0]).astype(BF16)
+    c_own[...] = c_both[:NCOL]
+
+
+def pair_kernel(keep, recv, send2, keep2, total):
+    total[...] = add(keep, recv)
     part = part_index()
     keep2[...] = total[pl.ds(pl.multiple_of(part * QUARTER, QUARTER), QUARTER), :]
     send2[...] = total[pl.ds(pl.multiple_of((1 - part) * QUARTER, QUARTER), QUARTER), :]
-    c_both[NCOL:] = recv[HALF:]
+
+
+def fill_kernel(recv, _c_both, _after, c_both):
+    c_both[NCOL:] = recv[...]
 
 
 def coarse_kernel(keep, recv, couple, _after, coef1, lift1):
@@ -147,7 +160,7 @@
 
 
 def near0_kernel(sides, recv, couple, _after, near0):
-    near0[...] = nt(couple[1], sides[:NCOL]) + nt(couple[2], recv[HALF:]) + nt(couple[3], sides[NCOL:])
+    near0[...] = nt(couple[1], sides[:NCOL]) + nt(couple[2], recv[...]) + nt(couple[3], sides[NCOL:])
 
 
 def down1_kernel(stay0, first, second, near1, couple, _after, down1):
@@ -203,23 +216,22 @@
         after_block(rows)
 
 
-def half_columns(own):
-    core = core_index()
-    return pl.ds(pl.multiple_of((core if own else 1 - core) * HALF, HALF), HALF)
-
-
-def own_half_kernel(base, turned, down1, near0, couple, out_hbm, out, sems):
-    cols = half_columns(True)
-    copies = []
-
-    def write(rows):
-        if rows.start < LEAF // 2:
-            copies.append(pltpu.make_async_copy(out.at[rows], out_hbm.at[rows, cols], sems.at[len(copies)]))
-            copies[-1].start()
-
-    leaf_half(base, turned, down1, near0, couple, cols, out, write)
-    for copy in copies:
-        copy.wait()
+def own_half_kernel(which, base, turned, down1, near0, couple, *refs):
+    out_hbm, out, sems = refs[-3 - (which == 1)], refs[-2 - (which == 1)], refs[-1]
+
+    @pl.when(core_index() == which)
+    def _():
+        cols = half_columns(True)
+        copies = []
+
+        def write(rows):
+            if rows.start < LEAF // 2:
+                copies.append(pltpu.make_async_copy(out.at[rows], out_hbm.at[rows, cols], sems.at[len(copies)]))
+                copies[-1].start()
+
+        leaf_half(base, turned, down1, near0, couple, cols, out, write)
+        for copy in copies:
+            copy.wait()
 
 
 def final_kernel(base, turned, down1, near0, couple, own, _product, out_hbm, out, sems):
@@ -274,59 +286,61 @@
         coarse_couple.reshape(4, RANK, RANK),
         top_coupling,
     )
-    send, keep, c_both, x, order, rows, leaf, coarse = call(
+    both_coefs = ((2 * NCOL, RANK), BF16)
+    send, c_both, x, order, turned_basis, rows, leaf, coarse = call(
         front_kernel,
         "front",
         [
-            ((HALF + NCOL, RANK), BF16),
             half,
-            ((2 * NCOL, RANK), BF16),
+            both_coefs,
             ((LEAF, NCOL), BF16),
             ((1, LEAF), jnp.int32),
+            ((RANK, LEAF), BF16),
             ((4, RANK, 2 * RANK), BF16),
             couple,
             couple,
         ],
         [HBM] * 6,
-        flops=2 * LEAF * LEAF * RANK + 2 * LEAF * RANK * NCOL,
+        flops=2 * LEAF * LEAF * RANK + LEAF * RANK * NCOL,
         moved=7 * MIB,
-        scratch=[
-            pltpu.VMEM((LEAF, RANK), BF16),
-            pltpu.VMEM((RANK, LEAF), BF16),
-            pltpu.VMEM((NCOL, RANK), BF16),
-            pltpu.SemaphoreType.DMA((9,)),
-        ],
+        scratch=[pltpu.VMEM((LEAF, RANK), BF16), pltpu.SemaphoreType.DMA((9,))],
     )(*(pltpu.with_memory_space_constraint(a, pltpu.HBM) for a in inputs))
     recv = permute(send, dy=1)
-    (ordered,) = gather([(0, 512)], [order, x], [], [NCOL], send)
-
-    send2, keep2, c_both = call(
-        pair_kernel,
-        "pair",
-        [quarter, quarter, ((2 * NCOL, RANK), BF16)],
-        [VMEM, VMEM, ANY, VMEM],
-        scratch=[pltpu.VMEM((HALF, RANK), BF16)],
-        aliases={3: 2},
-    )(keep, recv, ordered[0], c_both)
+    keep, c_both, c_own = call(
+        own_coef_kernel,
+        "own_coef",
+        [half, both_coefs, ((NCOL, RANK), BF16)],
+        [VMEM] * 4 + [ANY],
+        flops=LEAF * RANK * NCOL,
+        moved=2 * MIB,
+        aliases={3: 1},
+    )(turned_basis, x, leaf, c_both, send)
+    c_core = permute(c_own, dy=1)
+
+    send2, keep2 = call(
+        pair_kernel, "pair", [quarter, quarter], [VMEM, VMEM], scratch=[pltpu.VMEM((HALF, RANK), BF16)]
+    )(keep, recv)
     recv2 = permute(send2, dx=1)
-    (ordered,) = gather([(512, 640), (1152, 512)], [order, x], ordered, [NCOL], send2)
+    (ordered,) = gather([(0, 640), (640, 512)], [order, x], [], [NCOL], send2)
 
     coef1, lift1 = call(coarse_kernel, "coarse", [quarter, quarter], [VMEM, VMEM, VMEM, ANY], flops=small)(
         keep2, recv2, coarse, ordered[0]
     )
     recv3 = permute(lift1, dx=3)
-    ordered, c_both = gather([(1664, 384)], [order, x], ordered, [NCOL], lift1, [c_both])
+    (ordered,) = gather([(1152, 512), (1664, 384)], [order, x], ordered, [NCOL], lift1)
+    c_both = call(fill_kernel, "fill", [both_coefs], [VMEM, VMEM, ANY], aliases={1: 0})(
+        c_core, c_both, ordered[0]
+    )[0]
     sides = permute(c_both, dx=1)
-    (result,) = dense([(0, 256)], [leaf_dense, ordered[0]], [], [NCOL], c_both)
-
-    pair = call(sum_kernel, "sum_x", [quarter], [VMEM, VMEM, ANY])(lift1, recv3, result[0])[0]
+
+    pair = call(sum_kernel, "sum_x", [quarter], [VMEM, VMEM, ANY])(lift1, recv3, c_both)[0]
     recv4 = permute(pair, dy=2)
-    result, coef1 = dense([(256, 640)], [leaf_dense, ordered[0]], result, [NCOL], pair, [coef1])
+    result, coef1 = dense([(0, 576)], [leaf_dense, ordered[0]], [], [NCOL], pair, [coef1])
     coarse_x = permute(coef1, dx=3)
 
     coef2 = call(sum_kernel, "sum_z", [quarter], [VMEM, VMEM, ANY])(pair, recv4, result[0])[0]
     recv5 = permute(coef2, dy=6)
-    (result,) = dense([(896, 640)], [leaf_dense, ordered[0]], result, [NCOL], coef2)
+    (result,) = dense([(576, 640)], [leaf_dense, ordered[0]], result, [NCOL], coef2)
     both = call(both_kernel, "both", [half], [VMEM, VMEM, ANY])(coef1, coarse_x, result[0])[0]
     coarse_yz = permute(both, dy=2)
 
@@ -337,38 +351,48 @@
     stay0, stay1 = call(
         top_stay_kernel, "top_stay", [quarter_f32, quarter_f32], [VMEM, VMEM, VMEM, ANY], flops=4 * small
     )(coef2, recv5, rows, send6)
-    (result,) = dense([(1536, 512)], [leaf_dense, ordered[0]], result, [NCOL], stay0)
-    (scattered,) = scatter([(0, 640)], [order, result[0], basis_out], [], widths, stay0)
+    (result,) = dense([(1216, 416), (1632, 416)], [leaf_dense, ordered[0]], result, [NCOL], stay0)
+    (scattered,) = scatter([(0, 512)], [order, result[0], basis_out], [], widths, stay0)
 
     send7 = call(half_kernel, "half", [quarter], [VMEM, VMEM, ANY])(stay1, recv6, scattered[0])[0]
     recv7 = permute(send7, dx=4)
     near1 = call(near1_kernel, "near1", [quarter_f32], [VMEM, VMEM, VMEM, ANY], flops=3 * small)(
         coarse_x, coarse_yz, coarse, send7
     )[0]
-    (scattered,) = scatter([(640, 352), (992, 352)], [order, result[0], basis_out], scattered, widths, near1)
+    (scattered,) = scatter([(512, 768)], [order, result[0], basis_out], scattered, widths, near1)
 
     down1 = call(down1_kernel, "down1", [quarter], [VMEM] * 5 + [ANY], flops=small)(
         stay0, recv6, recv7, near1, coarse, scattered[0]
     )[0]
     side = permute(down1, dx=1)
     near0 = call(near0_kernel, "near0", [((RANK, NCOL), F32)], [VMEM] * 3 + [ANY], flops=12 * small)(
-        sides, recv, leaf, down1
+        sides, c_core, leaf, down1
     )[0]
-    (scattered,) = scatter([(1344, 352), (1696, 352)], [order, result[0], basis_out], scattered, widths, near0)
+    (scattered,) = scatter([(1280, 768)], [order, result[0], basis_out], scattered, widths, near0)
 
     mine = call(join_kernel, "join", [half], [VMEM, VMEM, ANY])(down1, side, scattered[0])[0]
+    whole = ((LEAF, NCOL), BF16)
+    halves = [whole, ((LEAF, HALF), BF16)]
+    costs = dict(flops=LEAF * RANK * NCOL, moved=2 * MIB, scratch=[pltpu.SemaphoreType.DMA((2,))])
+    product, own, mine = call(
+        functools.partial(own_half_kernel, 1),
+        "own_half_1",
+        halves + [half],
+        [VMEM] * 5,
+        out_specs=[HBM, VMEM, VMEM],
+        aliases={2: 2},
+        **costs,
+    )(*scattered, mine, near0, leaf)
     other = permute(mine, dy=1)
-    whole = ((LEAF, NCOL), BF16)
     product, own = call(
-        own_half_kernel,
-        "own_half",
-        [whole, ((LEAF, HALF), BF16)],
-        [VMEM] * 5,
-        flops=LEAF * RANK * NCOL,
-        moved=2 * MIB,
-        scratch=[pltpu.SemaphoreType.DMA((2,))],
+        functools.partial(own_half_kernel, 0),
+        "own_half_0",
+        halves,
+        [VMEM] * 5 + [HBM, ANY],
         out_specs=[HBM, VMEM],
-    )(*scattered, mine, near0, leaf)
+        aliases={5: 0, 6: 1},
+        **costs,
+    )(*scattered, mine, near0, leaf, product, own)
     return call(
         final_kernel,
         "final",

time: 55.6 us -> 54.2 us (0.975)
  starting transfers between devices: 20.3 us -> 18.4 us
    ppermute x12 -> x13, starting transfers between devices: 20.3 us -> 18.4 us  [permute(): return lax.ppermute(array, AXES, pairs)]
    pallas_call x10 -> x8, Pallas kernels: 23.5 us -> 23.2 us  [leaf_part(): call(functools.partial(kernel, blocks, len(kept)), name, outs + [(c.shape...]
    pallas_call x3 -> x6, Pallas kernels: 7.08 us -> 7.22 us  [the longest x1 4.66 us: local(): call(front_kernel, 'front', [half, both_coefs, ((LEAF, NCOL), BF16), ((1,...]
  transfers between devices with their start and end apart: 12 -> 13, of which waited for: 1 -> 1; matrix products, arithmetic and copies ran while one was open for 0% -> 0% of each run, Pallas kernels for 48% -> 49%
where the time goes in v4:
time: 54.2 us; the launch traced here: 54.1 us
  Pallas kernels  34.1 us (63%)
  starting transfers between devices  18.4 us (34%)
  waiting for transfers between devices  1.08 us (2%)
    pallas_call x8, Pallas kernels, leaf_part(): call(functools.partial(kernel, blocks, len(kept)), name, outs + [(c.shape...  23.2 us
    ppermute x13, starting transfers between devices, permute(): return lax.ppermute(array, AXES, pairs)  18.4 us
    pallas_call x1, Pallas kernels, local(): call(front_kernel, 'front', [half, both_coefs, ((LEAF, NCOL), BF16), ((1,...  4.66 us
    pallas_call x1, Pallas kernels, local(): call(final_kernel, 'final', [whole], [VMEM] * 6 + [HBM], flops=LEAF * RAN...  1.76 us
    pallas_call x1, Pallas kernels, local(): call(functools.partial(own_half_kernel, 1), 'own_half_1', halves + [half]...  1.44 us
  transfers between devices with their start and end apart: 13, of which 1 were waited for; matrix products, arithmetic and copies ran while one was open for 0% of the time, Pallas kernels for 49%

profile of v4, /device:TPU:1, one launch (start us, length us, event | category | flops | bytes accessed | tf_op | source)
XLA Modules:
  0.0 54.1 jit_solution(11178748301239514527)
XLA Ops:
  0.0 4.7 %front.1 = (bf16[384,256]{1,0:T(8,128)(2,1)S(1)}, bf16[1536,256]{1,0:T(8,128)(2,1)S(1)}, bf16[2048,768]{1,0:T(8,128)(2,1)S(1)}, s32[1,2048]{1,0:T(1,128)S(1)}, b...) custom-call(s32[1,2048]{1,0:T(1,128)} %bitcast.7, ...), custom_call_target="tpu_custom_call" | custom-call | flops 2550136832 | bytes 7340032 | tf_op jit(solution)/shard_map/front/pallas_call | solution.py:290
  4.7 1.5 %collective-permute-start = (bf16[384,256]{1,0:T(8,128)(2,1)S(1)}, bf16[384,256]{1,0:T(8,128)(2,1)S(1)}, u32[]{:S(2)}, u32[]{:S(2)}) collective-permute-start(bf16[384,256]{1,0:T(8,128)(2,1)S(1)} %get-tuple-element.40._after), channel_id=1, source_target_pairs={{0,1},{1,0},{2,3},{3,2},{4,5},{5,4},{6,7},{7,6},{8,9},{9,8},{10,11... | collective-permute-start | bytes 589832 | tf_op jit(solution)/shard_map/ppermute | solution.py:26
  6.2 1.0 %own_coef.1 = (bf16[384,256]{1,0:T(8,128)(2,1)S(1)}, bf16[1536,256]{1,0:T(8,128)(2,1)S(1)}, bf16[768,256]{1,0:T(8,128)(2,1)S(1)}) custom-call(bf16[256,2048]{1,0:T(8,128)(2,1)S(1)} %get-tuple-element.37.turned, bf16[2048,768]{1,0:T(8,128)(2,1)S(1)} %get-tuple-element.36.x, ...), custom_call_target="tpu_custom_call", output_to_operand_aliasing={{1}: (3, {})} | custom-call | flops 402653184 | bytes 2097152 | tf_op jit(solution)/shard_map/own_coef/pallas_call | solution.py:309
  7.4 1.4 %collective-permute-start.1 = (bf16[192,256]{1,0:T(8,128)(2,1)S(1)}, bf16[192,256]{1,0:T(8,128)(2,1)S(1)}, u32[]{:S(2)}, u32[]{:S(2)}) collective-permute-start(bf16[192,256]{1,0:T(8,128)(2,1)S(1)} %get-tuple-element.43._after), channel_id=1, source_target_pairs={{0,8},{1,9},{2,10},{3,11},{4,12},{5,13},{6,14},{7,15},{8,0},{9,1},... | collective-permute-start | bytes 294920 | tf_op jit(solution)/shard_map/ppermute | solution.py:26
  8.7 3.9 %gather.2._after.refs_0_ = bf16[2048,768]{1,0:T(8,128)(2,1)S(1)} custom-call(s32[1,2048]{1,0:T(1,128)S(1)} %get-tuple-element.35.order, bf16[2048,768]{1,0:T(8,128)(2,1)S(1)} %get-tuple-element.36.x, bf16[192,256]{1,0:T(8,128)(2,1)S(1)} %get-tuple-element.43._after), custom_call_target="tpu_custom_call" | custom-call | flops 3623878656 | bytes 4194304 | tf_op jit(solution)/shard_map/gather/pallas_call | solution.py:257
  12.9 1.9 %collective-permute-start.2 = (bf16[192,256]{1,0:T(8,128)(2,1)S(1)}, bf16[192,256]{1,0:T(8,128)(2,1)S(1)}, u32[]{:S(2)}, u32[]{:S(2)}) collective-permute-start(bf16[192,256]{1,0:T(8,128)(2,1)S(1)} %get-tuple-element.45._after.mine), channel_id=1, source_target_pairs={{0,24},{1,25},{2,26},{3,27},{4,28},{5,29},{6,30},{7,31},{8,16},{9,... | collective-permute-start | bytes 294920 | tf_op jit(solution)/shard_map/ppermute | solution.py:26
  14.8 3.1 %gather.3._after.ordered = bf16[2048,768]{1,0:T(8,128)(2,1)S(1)} custom-call(s32[1,2048]{1,0:T(1,128)S(1)} %get-tuple-element.35.order, bf16[2048,768]{1,0:T(8,128)(2,1)S(1)} %get-tuple-element.36.x, bf16[192,256]{1,0:T(8,128)(2,1)S(1)} %get-tuple-element.45._after.mine, bf16[2048,768]{1,0:T(8,128)(2,1)S(1)} %gather.2._after.refs_0_), custom_call_target="tpu_custom_call", output_to_operand_aliasing={{}: (3, {})} | custom-call | flops 2818572288 | bytes 4194304 | tf_op jit(solution)/shard_map/gather/pallas_call | solution.py:257
  18.0 0.4 collective-permute-start.7
  18.4 1.9 %collective-permute-start.4 = (bf16[192,256]{1,0:T(8,128)(2,1)S(1)}, bf16[192,256]{1,0:T(8,128)(2,1)S(1)}, u32[]{:S(2)}, u32[]{:S(2)}) collective-permute-start(bf16[192,256]{1,0:T(8,128)(2,1)S(1)} %sum_x.1._after.mine), channel_id=1, source_target_pairs={{0,2},{1,3},{2,0},{3,1},{4,6},{5,7},{6,4},{7,5},{8,10},{9,11},{10,... | collective-permute-start | bytes 294920 | tf_op jit(solution)/shard_map/ppermute | solution.py:26
  20.3 2.0 %dense.6 = (bf16[2048,768]{1,0:T(8,128)(2,1)S(1)}, bf16[192,256]{1,0:T(8,128)(2,1)S(1)}) custom-call(bf16[2048,2048]{1,0:T(8,128)(2,1)S(1)} %bitcast.4, bf16[2048,768]{1,0:T(8,128)(2,1)S(1)} %gather.3._after.ordered, bf16[192,256]{1,0:T(8,128)(2,1)S(1)} %sum_x.1._after.mine, ...), custom_call_target="tpu_custom_call", output_to_operand_aliasing={{1}: (3, {})} | custom-call | flops 1811939328 | bytes 4194304 | tf_op jit(solution)/shard_map/dense/pallas_call | solution.py:257
  22.3 1.2 %collective-permute-start.6 = (bf16[192,256]{1,0:T(8,128)(2,1)S(1)}, bf16[192,256]{1,0:T(8,128)(2,1)S(1)}, u32[]{:S(2)}, u32[]{:S(2)}) collective-permute-start(bf16[192,256]{1,0:T(8,128)(2,1)S(1)} %get-tuple-element.51.coef1), channel_id=1, source_target_pairs={{0,24},{1,25},{2,26},{3,27},{4,28},{5,29},{6,30},{7,31},{8,16},{9,... | collective-permute-start | bytes 294920 | tf_op jit(solution)/shard_map/ppermute | solution.py:26
  23.5 2.8 %collective-permute-start.5 = (bf16[192,256]{1,0:T(8,128)(2,1)S(1)}, bf16[192,256]{1,0:T(8,128)(2,1)S(1)}, u32[]{:S(2)}, u32[]{:S(2)}) collective-permute-start(bf16[192,256]{1,0:T(8,128)(2,1)S(1)} %sum_z.1._after.own), channel_id=1, source_target_pairs={{0,6},{1,7},{2,4},{3,5},{4,2},{5,3},{6,0},{7,1},{8,14},{9,15},{10,... | collective-permute-start | bytes 294920 | tf_op jit(solution)/shard_map/ppermute | solution.py:26
  26.3 2.2 %dense.8._after.refs_0_ = bf16[2048,768]{1,0:T(8,128)(2,1)S(1)} custom-call(bf16[2048,2048]{1,0:T(8,128)(2,1)S(1)} %bitcast.4, bf16[2048,768]{1,0:T(8,128)(2,1)S(1)} %gather.3._after.ordered, bf16[192,256]{1,0:T(8,128)(2,1)S(1)} %sum_z.1._after.own, bf16[2048,768]{1,0:T(8,128)(2,1)S(1)} %get-tuple-element.49._after.refs_0_), custom_call_target="tpu_custom_call", output_to_operand_aliasing={{}: (3, {})} | custom-call | flops 2013265920 | bytes 4194304 | tf_op jit(solution)/shard_map/dense/pallas_call | solution.py:257
  29.2 2.8 %collective-permute-start.8 = (bf16[384,256]{1,0:T(8,128)(2,1)S(1)}, bf16[384,256]{1,0:T(8,128)(2,1)S(1)}, u32[]{:S(2)}, u32[]{:S(2)}) collective-permute-start(bf16[384,256]{1,0:T(8,128)(2,1)S(1)} %top_send.1._after), channel_id=1, source_target_pairs={{0,96},{1,97},{2,98},{3,99},{4,100},{5,101},{6,102},{7,103},{8,104... | collective-permute-start | bytes 589832 | tf_op jit(solution)/shard_map/ppermute | solution.py:26
  32.4 2.8 %dense.10.result = bf16[2048,768]{1,0:T(8,128)(2,1)S(1)} custom-call(bf16[2048,2048]{1,0:T(8,128)(2,1)S(1)} %bitcast.4, bf16[2048,768]{1,0:T(8,128)(2,1)S(1)} %gather.3._after.ordered, f32[192,256]{1,0:T(8,128)S(1)} %get-tuple-element.52._after.stay0, bf16[2048,768]{1,0:T(8,128)(2,1)S(1)} %dense.8._after.refs_0_), custom_call_target="tpu_custom_call", output_to_operand_aliasing={{}: (3, {})} | custom-call | flops 2617245696 | bytes 4194304 | tf_op jit(solution)/shard_map/dense/pallas_call | solution.py:257
  35.2 2.3 %scatter.3 = (bf16[2048,768]{1,0:T(8,128)(2,1)S(1)}, bf16[2048,256]{1,0:T(8,128)(2,1)S(1)}) custom-call(s32[1,2048]{1,0:T(1,128)S(1)} %get-tuple-element.35.order, bf16[2048,768]{1,0:T(8,128)(2,1)S(1)} %dense.10.result, bf16[2048,256]{1,0:T(8,128)(2,1)S(1)} %copy-done, f32[192,256]{1,0:T(8,128)S(1)} %get-tuple-element.52._after.stay0), custom_call_target="tpu_custom_call" | custom-call | flops 2147483648 | bytes 4194304 | tf_op jit(solution)/shard_map/scatter/pallas_call | solution.py:257
  38.0 3.4 %scatter.4 = (bf16[2048,768]{1,0:T(8,128)(2,1)S(1)}, bf16[2048,256]{1,0:T(8,128)(2,1)S(1)}) custom-call(s32[1,2048]{1,0:T(1,128)S(1)} %get-tuple-element.35.order, bf16[2048,768]{1,0:T(8,128)(2,1)S(1)} %dense.10.result, bf16[2048,256]{1,0:T(8,128)(2,1)S(1)} %copy-done, f32[192,256]{1,0:T(8,128)S(1)} %near1.1._after, ...), custom_call_target="tpu_custom_call", output_to_operand_aliasing={{0}: (4, {}), {1}: (5, {})} | custom-call | flops 3221225472 | bytes 4194304 | tf_op jit(solution)/shard_map/scatter/pallas_call | solution.py:257
  41.6 1.2 %collective-permute-start.11 = (bf16[192,256]{1,0:T(8,128)(2,1)S(1)}, bf16[192,256]{1,0:T(8,128)(2,1)S(1)}, u32[]{:S(2)}, u32[]{:S(2)}) collective-permute-start(bf16[192,256]{1,0:T(8,128)(2,1)S(1)} %down1.1._after.own), channel_id=1, source_target_pairs={{0,8},{1,9},{2,10},{3,11},{4,12},{5,13},{6,14},{7,15},{8,0},{9,1},... | collective-permute-start | bytes 294920 | tf_op jit(solution)/shard_map/ppermute | solution.py:26
  42.8 0.5 near0.1._after
  43.3 3.4 %scatter.5 = (bf16[2048,768]{1,0:T(8,128)(2,1)S(1)}, bf16[2048,256]{1,0:T(8,128)(2,1)S(1)}) custom-call(s32[1,2048]{1,0:T(1,128)S(1)} %get-tuple-element.35.order, bf16[2048,768]{1,0:T(8,128)(2,1)S(1)} %dense.10.result, bf16[2048,256]{1,0:T(8,128)(2,1)S(1)} %copy-done, f32[256,768]{1,0:T(8,128)S(1)} %near0.1._after, ...), custom_call_target="tpu_custom_call", output_to_operand_aliasing={{0}: (4, {}), {1}: (5, {})} | custom-call | flops 3221225472 | bytes 4194304 | tf_op jit(solution)/shard_map/scatter/pallas_call | solution.py:257
  46.8 1.4 %own_half_1.1 = (bf16[2048,768]{1,0:T(8,128)(2,1)}, bf16[2048,384]{1,0:T(8,128)(2,1)S(1)}, bf16[384,256]{1,0:T(8,128)(2,1)S(1)}) custom-call(bf16[2048,768]{1,0:T(8,128)(2,1)S(1)} %get-tuple-element.58._after.base, bf16[2048,256]{1,0:T(8,128)(2,1)S(1)} %get-tuple-element.59.turned, bf16[384,256]{1,0:T(8,128)(2,1)S(1)} %join.1.down1, ...), custom_call_target="tpu_custom_call", output_to_operand_aliasing={{2}: (2, {})} | custom-call | flops 402653184 | bytes 2097152 | tf_op jit(solution)/shard_map/own_half_1/pallas_call | solution.py:377
  48.2 2.8 %collective-permute-start.12 = (bf16[384,256]{1,0:T(8,128)(2,1)S(1)}, bf16[384,256]{1,0:T(8,128)(2,1)S(1)}, u32[]{:S(2)}, u32[]{:S(2)}) collective-permute-start(bf16[384,256]{1,0:T(8,128)(2,1)S(1)} %get-tuple-element.60.down1), channel_id=1, source_target_pairs={{0,1},{1,0},{2,3},{3,2},{4,5},{5,4},{6,7},{7,6},{8,9},{9,8},{10,11... | collective-permute-start | bytes 589832 | tf_op jit(solution)/shard_map/ppermute | solution.py:26
  51.1 1.0 %collective-permute-done.12.down1 = bf16[384,256]{1,0:T(8,128)(2,1)S(1)} collective-permute-done((bf16[384,256]{1,0:T(8,128)(2,1)S(1)}, bf16[384,256]{1,0:T(8,128)(2,1)S(1)}, u32[]{:S(2)}, u32[]{:S(2)}) %collective-permute-start.12) | collective-permute-done | bytes 196640 | tf_op jit(solution)/shard_map/ppermute | solution.py:26
  52.1 1.8 %final.1 = bf16[2048,768]{1,0:T(8,128)(2,1)} custom-call(bf16[2048,768]{1,0:T(8,128)(2,1)S(1)} %get-tuple-element.58._after.base, bf16[2048,256]{1,0:T(8,128)(2,1)S(1)} %get-tuple-element.59.turned, bf16[384,256]{1,0:T(8,128)(2,1)S(1)} %collective-permute-done.12.down1, f32[256,768]{1,0:T(8,128)S(1)} %near0.1._after, ...), custom_call_target="tpu_custom_call", output_to_operand_aliasing={{}: (6, {})} | custom-call | flops 402653184 | bytes 4194304 | tf_op jit(solution)/shard_map/final/pallas_call | solution.py:396
  (35 shorter events, 2.2 us)
Async XLA Ops:
  4.7 2.6 %collective-permute-start = (bf16[384,256]{1,0:T(8,128)(2,1)S(1)}, bf16[384,256]{1,0:T(8,128)(2,1)S(1)}, u32[]{:S(2)}, u32[]{:S(2)}) collective-permute-start(bf16[384,256]{1,0:T(8,128)(2,1)S(1)} %get-tuple-element.40._after), channel_id=1, source_target_pairs={{0,1},{1,0},{2,3},{3,2},{4,5},{5,4},{6,7},{7,6},{8,9},{9,8},{10,11... | collective-permute-start | bytes 589832 | tf_op jit(solution)/shard_map/ppermute | solution.py:26
  7.2 10.8 %collective-permute-start.3 = (bf16[768,256]{1,0:T(8,128)(2,1)S(1)}, bf16[768,256]{1,0:T(8,128)(2,1)S(1)}, u32[]{:S(2)}, u32[]{:S(2)}) collective-permute-start(bf16[768,256]{1,0:T(8,128)(2,1)S(1)} %get-tuple-element.46), channel_id=1, source_target_pairs={{0,1},{1,0},{2,3},{3,2},{4,5},{5,4},{6,7},{7,6},{8,9},{9,8},{10,11... | collective-permute-start | bytes 1179656 | tf_op jit(solution)/shard_map/ppermute | solution.py:26
  7.4 5.3 %collective-permute-start.1 = (bf16[192,256]{1,0:T(8,128)(2,1)S(1)}, bf16[192,256]{1,0:T(8,128)(2,1)S(1)}, u32[]{:S(2)}, u32[]{:S(2)}) collective-permute-start(bf16[192,256]{1,0:T(8,128)(2,1)S(1)} %get-tuple-element.43._after), channel_id=1, source_target_pairs={{0,8},{1,9},{2,10},{3,11},{4,12},{5,13},{6,14},{7,15},{8,0},{9,1},... | collective-permute-start | bytes 294920 | tf_op jit(solution)/shard_map/ppermute | solution.py:26
  12.9 7.4 %slice-start = ((s8[8388608]{0:T(1024)(128)(4,1)}), s8[4194304]{0:T(1024)(128)(4,1)S(1)}, s32[]{:S(2)}) async-start(s8[8388608]{0:T(1024)(128)(4,1)} %bitcast.3), calls=%async_computation | async-start | bytes 8388608
  12.9 7.4 %slice-start.1 = ((s8[8388608]{0:T(1024)(128)(4,1)}), s8[4194304]{0:T(1024)(128)(4,1)S(1)}, s32[]{:S(2)}) async-start(s8[8388608]{0:T(1024)(128)(4,1)} %bitcast.3), calls=%async_computation.1 | async-start | bytes 8388608
  12.9 5.5 %collective-permute-start.2 = (bf16[192,256]{1,0:T(8,128)(2,1)S(1)}, bf16[192,256]{1,0:T(8,128)(2,1)S(1)}, u32[]{:S(2)}, u32[]{:S(2)}) collective-permute-start(bf16[192,256]{1,0:T(8,128)(2,1)S(1)} %get-tuple-element.45._after.mine), channel_id=1, source_target_pairs={{0,24},{1,25},{2,26},{3,27},{4,28},{5,29},{6,30},{7,31},{8,16},{9,... | collective-permute-start | bytes 294920 | tf_op jit(solution)/shard_map/ppermute | solution.py:26
  18.0 24.8 %collective-permute-start.7 = (bf16[1536,256]{1,0:T(8,128)(2,1)S(1)}, bf16[1536,256]{1,0:T(8,128)(2,1)S(1)}, u32[]{:S(2)}, u32[]{:S(2)}) collective-permute-start(bf16[1536,256]{1,0:T(8,128)(2,1)S(1)} %fill.1._after), channel_id=1, source_target_pairs={{0,8},{1,9},{2,10},{3,11},{4,12},{5,13},{6,14},{7,15},{8,0},{9,1},... | collective-permute-start | bytes 2359304 | tf_op jit(solution)/shard_map/ppermute | solution.py:26
  18.4 5.1 %collective-permute-start.4 = (bf16[192,256]{1,0:T(8,128)(2,1)S(1)}, bf16[192,256]{1,0:T(8,128)(2,1)S(1)}, u32[]{:S(2)}, u32[]{:S(2)}) collective-permute-start(bf16[192,256]{1,0:T(8,128)(2,1)S(1)} %sum_x.1._after.mine), channel_id=1, source_target_pairs={{0,2},{1,3},{2,0},{3,1},{4,6},{5,7},{6,4},{7,5},{8,10},{9,11},{10,... | collective-permute-start | bytes 294920 | tf_op jit(solution)/shard_map/ppermute | solution.py:26
  22.3 6.2 %collective-permute-start.6 = (bf16[192,256]{1,0:T(8,128)(2,1)S(1)}, bf16[192,256]{1,0:T(8,128)(2,1)S(1)}, u32[]{:S(2)}, u32[]{:S(2)}) collective-permute-start(bf16[192,256]{1,0:T(8,128)(2,1)S(1)} %get-tuple-element.51.coef1), channel_id=1, source_target_pairs={{0,24},{1,25},{2,26},{3,27},{4,28},{5,29},{6,30},{7,31},{8,16},{9,... | collective-permute-start | bytes 294920 | tf_op jit(solution)/shard_map/ppermute | solution.py:26
  23.5 5.4 %collective-permute-start.5 = (bf16[192,256]{1,0:T(8,128)(2,1)S(1)}, bf16[192,256]{1,0:T(8,128)(2,1)S(1)}, u32[]{:S(2)}, u32[]{:S(2)}) collective-permute-start(bf16[192,256]{1,0:T(8,128)(2,1)S(1)} %sum_z.1._after.own), channel_id=1, source_target_pairs={{0,6},{1,7},{2,4},{3,5},{4,2},{5,3},{6,0},{7,1},{8,14},{9,15},{10,... | collective-permute-start | bytes 294920 | tf_op jit(solution)/shard_map/ppermute | solution.py:26
  28.5 9.1 %collective-permute-start.10 = (bf16[384,256]{1,0:T(8,128)(2,1)S(1)}, bf16[384,256]{1,0:T(8,128)(2,1)S(1)}, u32[]{:S(2)}, u32[]{:S(2)}) collective-permute-start(bf16[384,256]{1,0:T(8,128)(2,1)S(1)} %both.1._after), channel_id=1, source_target_pairs={{0,2},{1,3},{2,0},{3,1},{4,6},{5,7},{6,4},{7,5},{8,10},{9,11},{10,... | collective-permute-start | bytes 589832 | tf_op jit(solution)/shard_map/ppermute | solution.py:26
  29.2 8.3 %collective-permute-start.8 = (bf16[384,256]{1,0:T(8,128)(2,1)S(1)}, bf16[384,256]{1,0:T(8,128)(2,1)S(1)}, u32[]{:S(2)}, u32[]{:S(2)}) collective-permute-start(bf16[384,256]{1,0:T(8,128)(2,1)S(1)} %top_send.1._after), channel_id=1, source_target_pairs={{0,96},{1,97},{2,98},{3,99},{4,100},{5,101},{6,102},{7,103},{8,104... | collective-permute-start | bytes 589832 | tf_op jit(solution)/shard_map/ppermute | solution.py:26
  32.3 2.8 %copy-start = (bf16[2048,256]{1,0:T(8,128)(2,1)S(1)}, bf16[2048,256]{1,0:T(8,128)(2,1)}, u32[]{:S(2)}) copy-start(bf16[2048,256]{1,0:T(8,128)(2,1)} %basis.5) | copy-start | bytes 3145732
  37.6 3.8 %collective-permute-start.9 = (bf16[192,256]{1,0:T(8,128)(2,1)S(1)}, bf16[192,256]{1,0:T(8,128)(2,1)S(1)}, u32[]{:S(2)}, u32[]{:S(2)}) collective-permute-start(bf16[192,256]{1,0:T(8,128)(2,1)S(1)} %half.1._after), channel_id=1, source_target_pairs={{0,32},{1,33},{2,34},{3,35},{4,36},{5,37},{6,38},{7,39},{8,40},{9,... | collective-permute-start | bytes 294920 | tf_op jit(solution)/shard_map/ppermute | solution.py:26
  41.6 5.1 %collective-permute-start.11 = (bf16[192,256]{1,0:T(8,128)(2,1)S(1)}, bf16[192,256]{1,0:T(8,128)(2,1)S(1)}, u32[]{:S(2)}, u32[]{:S(2)}) collective-permute-start(bf16[192,256]{1,0:T(8,128)(2,1)S(1)} %down1.1._after.own), channel_id=1, source_target_pairs={{0,8},{1,9},{2,10},{3,11},{4,12},{5,13},{6,14},{7,15},{8,0},{9,1},... | collective-permute-start | bytes 294920 | tf_op jit(solution)/shard_map/ppermute | solution.py:26
  48.2 3.9 %collective-permute-start.12 = (bf16[384,256]{1,0:T(8,128)(2,1)S(1)}, bf16[384,256]{1,0:T(8,128)(2,1)S(1)}, u32[]{:S(2)}, u32[]{:S(2)}) collective-permute-start(bf16[384,256]{1,0:T(8,128)(2,1)S(1)} %get-tuple-element.60.down1), channel_id=1, source_target_pairs={{0,1},{1,0},{2,3},{3,2},{4,5},{5,4},{6,7},{7,6},{8,9},{9,8},{10,11... | collective-permute-start | bytes 589832 | tf_op jit(solution)/shard_map/ppermute | solution.py:26

commit v5 on v4

--- a/solution.py
+++ b/solution.py
@@ -15,6 +15,7 @@
 NCOL = 768
 HALF = NCOL // 2
 QUARTER = NCOL // 4
+EARLY = 2
 VMEM = pl.BlockSpec(memory_space=pltpu.VMEM)
 HBM = pl.BlockSpec(memory_space=pltpu.HBM)
 ANY = pl.BlockSpec(memory_space=pl.ANY)
@@ -50,6 +51,11 @@
 def part_index():
     x = lax.rem(lax.axis_index("gx"), 4)
     return jnp.where((x == 1) | (x == 2), 1, 0)
+
+
+def early_index():
+    gx, gy = lax.axis_index("gx"), lax.axis_index("gy")
+    return lax.rem(gx, 4) + gx // 4 + gy // 2 <= EARLY
 
 
 def call(kernel, name, outs, in_specs, flops=0, moved=0, scratch=(), limit=16, aliases=None, out_specs=None):
@@ -72,11 +78,12 @@
 
 
 def front_kernel(
-    order_hbm, basis_hbm, x_hbm, leaf_hbm, coarse_hbm, top,
-    send, c_both, x, order, turned, rows, leaf, coarse,
+    order_hbm, basis_hbm, x_hbm, leaf_hbm, coarse_hbm, basis_out_hbm, top,
+    send, c_both, x, order, turned, rows, leaf, coarse, basis_out,
     basis, sems,
 ):
     pairs = [(order_hbm, order), (basis_hbm, basis), (x_hbm, x), (leaf_hbm, leaf), (coarse_hbm, coarse)]
+    pairs.append((basis_out_hbm, basis_out))
     y = lax.axis_index("gx") // 4
     z = lax.axis_index("gy") // 4
     flip = jnp.where(lax.rem(y, 2) == 0, y + 1, y - 1)
@@ -110,7 +117,7 @@
     c_own[...] = c_both[:NCOL]
 
 
-def pair_kernel(keep, recv, send2, keep2, total):
+def pair_kernel(keep, recv, _after, send2, keep2, total):
     total[...] = add(keep, recv)
     part = part_index()
     keep2[...] = total[pl.ds(pl.multiple_of(part * QUARTER, QUARTER), QUARTER), :]
@@ -189,12 +196,28 @@
         out[start : start + size] = nn(dense[start : start + size], ordered[...]).astype(BF16)
 
 
-def scatter_kernel(blocks, first, order, result, basis, _after, *refs):
+def early_kernel(order, basis, _after, turned):
+    @pl.when(early_index())
+    def _():
+        for start in range(0, LEAF, 512):
+            turned[start : start + 512] = nn(picks(order[...], start, 512), basis[...]).astype(BF16)
+
+
+def scatter_kernel(early_blocks, blocks, first, order, result, basis, _after, *refs):
     out, turned = refs[first : first + 2]
-    for start, size in blocks:
-        hot = picks(order[...], start, size)
-        out[start : start + size] = nn(hot, result[...]).astype(BF16)
-        turned[start : start + size] = nn(hot, basis[...]).astype(BF16)
+    early = early_index()
+
+    @pl.when(early)
+    def _():
+        for start, size in early_blocks:
+            out[start : start + size] = nn(picks(order[...], start, size), result[...]).astype(BF16)
+
+    @pl.when(jnp.logical_not(early))
+    def _():
+        for start, size in blocks:
+            hot = picks(order[...], start, size)
+            out[start : start + size] = nn(hot, result[...]).astype(BF16)
+            turned[start : start + size] = nn(hot, basis[...]).astype(BF16)
 
 
 def both_kernel(coef1, side_x, _after, both):
@@ -276,7 +299,10 @@
     widths = [NCOL, RANK]
     gather = functools.partial(leaf_part, gather_kernel, "gather")
     dense = functools.partial(leaf_part, dense_kernel, "dense")
-    scatter = functools.partial(leaf_part, scatter_kernel, "scatter")
+
+    def scatter(early_blocks, blocks, *rest):
+        return leaf_part(functools.partial(scatter_kernel, early_blocks), "scatter", blocks, *rest)
+
 
     inputs = (
         point_order.reshape(1, LEAF),
@@ -284,10 +310,11 @@
         right_block,
         leaf_couple.reshape(4, RANK, RANK),
         coarse_couple.reshape(4, RANK, RANK),
+        basis_out,
         top_coupling,
     )
     both_coefs = ((2 * NCOL, RANK), BF16)
-    send, c_both, x, order, turned_basis, rows, leaf, coarse = call(
+    send, c_both, x, order, turned_basis, rows, leaf, coarse, basis = call(
         front_kernel,
         "front",
         [
@@ -299,11 +326,12 @@
             ((4, RANK, 2 * RANK), BF16),
             couple,
             couple,
+            ((LEAF, RANK), BF16),
         ],
-        [HBM] * 6,
+        [HBM] * 7,
         flops=2 * LEAF * LEAF * RANK + LEAF * RANK * NCOL,
         moved=7 * MIB,
-        scratch=[pltpu.VMEM((LEAF, RANK), BF16), pltpu.SemaphoreType.DMA((9,))],
+        scratch=[pltpu.VMEM((LEAF, RANK), BF16), pltpu.SemaphoreType.DMA((10,))],
     )(*(pltpu.with_memory_space_constraint(a, pltpu.HBM) for a in inputs))
     recv = permute(send, dy=1)
     keep, c_both, c_own = call(
@@ -317,9 +345,13 @@
     )(turned_basis, x, leaf, c_both, send)
     c_core = permute(c_own, dy=1)
 
+    turned = call(early_kernel, "early", [((LEAF, RANK), BF16)], [VMEM, VMEM, ANY], moved=2 * MIB)(
+        order, basis, c_own
+    )
+
     send2, keep2 = call(
-        pair_kernel, "pair", [quarter, quarter], [VMEM, VMEM], scratch=[pltpu.VMEM((HALF, RANK), BF16)]
-    )(keep, recv)
+        pair_kernel, "pair", [quarter, quarter], [VMEM, VMEM, ANY], scratch=[pltpu.VMEM((HALF, RANK), BF16)]
+    )(keep, recv, turned[0])
     recv2 = permute(send2, dx=1)
     (ordered,) = gather([(0, 640), (640, 512)], [order, x], [], [NCOL], send2)
 
@@ -352,14 +384,14 @@
         top_stay_kernel, "top_stay", [quarter_f32, quarter_f32], [VMEM, VMEM, VMEM, ANY], flops=4 * small
     )(coef2, recv5, rows, send6)
     (result,) = dense([(1216, 416), (1632, 416)], [leaf_dense, ordered[0]], result, [NCOL], stay0)
-    (scattered,) = scatter([(0, 512)], [order, result[0], basis_out], [], widths, stay0)
+    (scattered,) = scatter([(0, 256)], [(0, 512)], [order, result[0], basis], turned, widths, stay0)
 
     send7 = call(half_kernel, "half", [quarter], [VMEM, VMEM, ANY])(stay1, recv6, scattered[0])[0]
     recv7 = permute(send7, dx=4)
     near1 = call(near1_kernel, "near1", [quarter_f32], [VMEM, VMEM, VMEM, ANY], flops=3 * small)(
         coarse_x, coarse_yz, coarse, send7
     )[0]
-    (scattered,) = scatter([(512, 768)], [order, result[0], basis_out], scattered, widths, near1)
+    (scattered,) = scatter([(256, 512), (768, 512)], [(512, 768)], [order, result[0], basis], scattered, widths, near1)
 
     down1 = call(down1_kernel, "down1", [quarter], [VMEM] * 5 + [ANY], flops=small)(
         stay0, recv6, recv7, near1, coarse, scattered[0]
@@ -368,7 +400,7 @@
     near0 = call(near0_kernel, "near0", [((RANK, NCOL), F32)], [VMEM] * 3 + [ANY], flops=12 * small)(
         sides, c_core, leaf, down1
     )[0]
-    (scattered,) = scatter([(1280, 768)], [order, result[0], basis_out], scattered, widths, near0)
+    (scattered,) = scatter([(1280, 768)], [(1280, 768)], [order, result[0], basis], scattered, widths, near0)
 
     mine = call(join_kernel, "join", [half], [VMEM, VMEM, ANY])(down1, side, scattered[0])[0]
     whole = ((LEAF, NCOL), BF16)

time: 54.2 us -> 53.3 us (0.983)
  starting transfers between devices: 18.4 us -> 16.9 us
    pallas_call x1 -> x2, Pallas kernels: 0.09 us -> 2.43 us  [the longest x1 2.34 us: local(): call(early_kernel, 'early', [((LEAF, RANK), BF16)], [VMEM, VMEM, ANY], mo...]
    pallas_call x8, Pallas kernels: 23.2 us -> 21 us  [leaf_part(): call(functools.partial(kernel, blocks, len(kept)), name, outs + [(c.shape...]
    ppermute x13, starting transfers between devices: 18.4 us -> 16.9 us  [permute(): return lax.ppermute(array, AXES, pairs)]
  transfers between devices with their start and end apart: 13 -> 13, of which waited for: 1 -> 2; matrix products, arithmetic and copies ran while one was open for 0% -> 0% of each run, Pallas kernels for 49% -> 49%
where the time goes in v5:
time: 53.3 us; the launch traced here: 53.2 us
  Pallas kernels  34.2 us (64%)
  starting transfers between devices  16.9 us (32%)
  waiting for transfers between devices  1.59 us (3%)
    pallas_call x8, Pallas kernels, leaf_part(): call(functools.partial(kernel, blocks, len(kept)), name, outs + [(c.shape...  21 us
    ppermute x13, starting transfers between devices, permute(): return lax.ppermute(array, AXES, pairs)  16.9 us
    pallas_call x1, Pallas kernels, local(): call(front_kernel, 'front', [half, both_coefs, ((LEAF, NCOL), BF16), ((1,...  4.67 us
    pallas_call x1, Pallas kernels, local(): call(early_kernel, 'early', [((LEAF, RANK), BF16)], [VMEM, VMEM, ANY], mo...  2.34 us
    pallas_call x1, Pallas kernels, local(): call(final_kernel, 'final', [whole], [VMEM] * 6 + [HBM], flops=LEAF * RAN...  1.75 us
    ppermute x13, waiting for transfers between devices, permute(): return lax.ppermute(array, AXES, pairs)  1.59 us
    pallas_call x1, Pallas kernels, local(): call(functools.partial(own_half_kernel, 1), 'own_half_1', halves + [half]...  1.45 us
  transfers between devices with their start and end apart: 13, of which 2 were waited for; matrix products, arithmetic and copies ran while one was open for 0% of the time, Pallas kernels for 49%

profile of v5, /device:TPU:1, one launch (start us, length us, event | category | flops | bytes accessed | tf_op | source)
XLA Modules:
  0.0 53.2 jit_solution(14095637009437986585)
XLA Ops:
  0.0 4.7 %front.1 = (bf16[384,256]{1,0:T(8,128)(2,1)S(1)}, bf16[1536,256]{1,0:T(8,128)(2,1)S(1)}, bf16[2048,768]{1,0:T(8,128)(2,1)S(1)}, s32[1,2048]{1,0:T(1,128)S(1)}, b...) custom-call(s32[1,2048]{1,0:T(1,128)} %bitcast.7, ...), custom_call_target="tpu_custom_call" | custom-call | flops 2550136832 | bytes 7340032 | tf_op jit(solution)/shard_map/front/pallas_call | solution.py:317
  4.7 1.5 %collective-permute-start = (bf16[384,256]{1,0:T(8,128)(2,1)S(1)}, bf16[384,256]{1,0:T(8,128)(2,1)S(1)}, u32[]{:S(2)}, u32[]{:S(2)}) collective-permute-start(bf16[384,256]{1,0:T(8,128)(2,1)S(1)} %get-tuple-element.41._after), channel_id=1, source_target_pairs={{0,1},{1,0},{2,3},{3,2},{4,5},{5,4},{6,7},{7,6},{8,9},{9,8},{10,11... | collective-permute-start | bytes 589832 | tf_op jit(solution)/shard_map/ppermute | solution.py:27
  6.2 1.0 %own_coef.1 = (bf16[384,256]{1,0:T(8,128)(2,1)S(1)}, bf16[1536,256]{1,0:T(8,128)(2,1)S(1)}, bf16[768,256]{1,0:T(8,128)(2,1)S(1)}) custom-call(bf16[256,2048]{1,0:T(8,128)(2,1)S(1)} %get-tuple-element.38.turned, bf16[2048,768]{1,0:T(8,128)(2,1)S(1)} %get-tuple-element.37.x, ...), custom_call_target="tpu_custom_call", output_to_operand_aliasing={{1}: (3, {})} | custom-call | flops 402653184 | bytes 2097152 | tf_op jit(solution)/shard_map/own_coef/pallas_call | solution.py:337
  7.3 2.3 %early.1._after.refs_0_ = bf16[2048,256]{1,0:T(8,128)(2,1)S(1)} custom-call(s32[1,2048]{1,0:T(1,128)S(1)} %get-tuple-element.36.order, bf16[2048,256]{1,0:T(8,128)(2,1)S(1)} %get-tuple-element.43.basis, bf16[768,256]{1,0:T(8,128)(2,1)S(1)} %get-tuple-element.44._after), custom_call_target="tpu_custom_call" | custom-call | bytes 2097152 | tf_op jit(solution)/shard_map/early/pallas_call | solution.py:348
  9.7 1.4 %collective-permute-start.1 = (bf16[192,256]{1,0:T(8,128)(2,1)S(1)}, bf16[192,256]{1,0:T(8,128)(2,1)S(1)}, u32[]{:S(2)}, u32[]{:S(2)}) collective-permute-start(bf16[192,256]{1,0:T(8,128)(2,1)S(1)} %get-tuple-element.46._after), channel_id=1, source_target_pairs={{0,8},{1,9},{2,10},{3,11},{4,12},{5,13},{6,14},{7,15},{8,0},{9,1},... | collective-permute-start | bytes 294920 | tf_op jit(solution)/shard_map/ppermute | solution.py:27
  11.1 3.9 %gather.2._after.refs_0_ = bf16[2048,768]{1,0:T(8,128)(2,1)S(1)} custom-call(s32[1,2048]{1,0:T(1,128)S(1)} %get-tuple-element.36.order, bf16[2048,768]{1,0:T(8,128)(2,1)S(1)} %get-tuple-element.37.x, bf16[192,256]{1,0:T(8,128)(2,1)S(1)} %get-tuple-element.46._after), custom_call_target="tpu_custom_call" | custom-call | flops 3623878656 | bytes 4194304 | tf_op jit(solution)/shard_map/gather/pallas_call | solution.py:280
  15.2 2.1 %collective-permute-start.2 = (bf16[192,256]{1,0:T(8,128)(2,1)S(1)}, bf16[192,256]{1,0:T(8,128)(2,1)S(1)}, u32[]{:S(2)}, u32[]{:S(2)}) collective-permute-start(bf16[192,256]{1,0:T(8,128)(2,1)S(1)} %get-tuple-element.48._after.mine), channel_id=1, source_target_pairs={{0,24},{1,25},{2,26},{3,27},{4,28},{5,29},{6,30},{7,31},{8,16},{9,... | collective-permute-start | bytes 294920 | tf_op jit(solution)/shard_map/ppermute | solution.py:27
  17.3 3.0 %gather.3._after.ordered = bf16[2048,768]{1,0:T(8,128)(2,1)S(1)} custom-call(s32[1,2048]{1,0:T(1,128)S(1)} %get-tuple-element.36.order, bf16[2048,768]{1,0:T(8,128)(2,1)S(1)} %get-tuple-element.37.x, bf16[192,256]{1,0:T(8,128)(2,1)S(1)} %get-tuple-element.48._after.mine, bf16[2048,768]{1,0:T(8,128)(2,1)S(1)} %gather.2._after.refs_0_), custom_call_target="tpu_custom_call", output_to_operand_aliasing={{}: (3, {})} | custom-call | flops 2818572288 | bytes 4194304 | tf_op jit(solution)/shard_map/gather/pallas_call | solution.py:280
  20.5 1.4 %collective-permute-start.4 = (bf16[192,256]{1,0:T(8,128)(2,1)S(1)}, bf16[192,256]{1,0:T(8,128)(2,1)S(1)}, u32[]{:S(2)}, u32[]{:S(2)}) collective-permute-start(bf16[192,256]{1,0:T(8,128)(2,1)S(1)} %sum_x.1._after.mine), channel_id=1, source_target_pairs={{0,2},{1,3},{2,0},{3,1},{4,6},{5,7},{6,4},{7,5},{8,10},{9,11},{10,... | collective-permute-start | bytes 294920 | tf_op jit(solution)/shard_map/ppermute | solution.py:27
  21.9 2.0 %dense.6 = (bf16[2048,768]{1,0:T(8,128)(2,1)S(1)}, bf16[192,256]{1,0:T(8,128)(2,1)S(1)}) custom-call(bf16[2048,2048]{1,0:T(8,128)(2,1)S(1)} %bitcast.4, bf16[2048,768]{1,0:T(8,128)(2,1)S(1)} %gather.3._after.ordered, bf16[192,256]{1,0:T(8,128)(2,1)S(1)} %sum_x.1._after.mine, ...), custom_call_target="tpu_custom_call", output_to_operand_aliasing={{1}: (3, {})} | custom-call | flops 1811939328 | bytes 4194304 | tf_op jit(solution)/shard_map/dense/pallas_call | solution.py:280
  23.9 1.3 %collective-permute-start.6 = (bf16[192,256]{1,0:T(8,128)(2,1)S(1)}, bf16[192,256]{1,0:T(8,128)(2,1)S(1)}, u32[]{:S(2)}, u32[]{:S(2)}) collective-permute-start(bf16[192,256]{1,0:T(8,128)(2,1)S(1)} %get-tuple-element.53.coef1), channel_id=1, source_target_pairs={{0,24},{1,25},{2,26},{3,27},{4,28},{5,29},{6,30},{7,31},{8,16},{9,... | collective-permute-start | bytes 294920 | tf_op jit(solution)/shard_map/ppermute | solution.py:27
  25.2 1.9 %collective-permute-start.5 = (bf16[192,256]{1,0:T(8,128)(2,1)S(1)}, bf16[192,256]{1,0:T(8,128)(2,1)S(1)}, u32[]{:S(2)}, u32[]{:S(2)}) collective-permute-start(bf16[192,256]{1,0:T(8,128)(2,1)S(1)} %sum_z.1._after.own), channel_id=1, source_target_pairs={{0,6},{1,7},{2,4},{3,5},{4,2},{5,3},{6,0},{7,1},{8,14},{9,15},{10,... | collective-permute-start | bytes 294920 | tf_op jit(solution)/shard_map/ppermute | solution.py:27
  27.1 2.2 %dense.8._after.refs_0_ = bf16[2048,768]{1,0:T(8,128)(2,1)S(1)} custom-call(bf16[2048,2048]{1,0:T(8,128)(2,1)S(1)} %bitcast.4, bf16[2048,768]{1,0:T(8,128)(2,1)S(1)} %gather.3._after.ordered, bf16[192,256]{1,0:T(8,128)(2,1)S(1)} %sum_z.1._after.own, bf16[2048,768]{1,0:T(8,128)(2,1)S(1)} %get-tuple-element.51._after.refs_0_), custom_call_target="tpu_custom_call", output_to_operand_aliasing={{}: (3, {})} | custom-call | flops 2013265920 | bytes 4194304 | tf_op jit(solution)/shard_map/dense/pallas_call | solution.py:280
  30.3 1.7 %collective-permute-start.8 = (bf16[384,256]{1,0:T(8,128)(2,1)S(1)}, bf16[384,256]{1,0:T(8,128)(2,1)S(1)}, u32[]{:S(2)}, u32[]{:S(2)}) collective-permute-start(bf16[384,256]{1,0:T(8,128)(2,1)S(1)} %top_send.1._after), channel_id=1, source_target_pairs={{0,96},{1,97},{2,98},{3,99},{4,100},{5,101},{6,102},{7,103},{8,104... | collective-permute-start | bytes 589832 | tf_op jit(solution)/shard_map/ppermute | solution.py:27
  32.3 2.8 %dense.10.result = bf16[2048,768]{1,0:T(8,128)(2,1)S(1)} custom-call(bf16[2048,2048]{1,0:T(8,128)(2,1)S(1)} %bitcast.4, bf16[2048,768]{1,0:T(8,128)(2,1)S(1)} %gather.3._after.ordered, f32[192,256]{1,0:T(8,128)S(1)} %get-tuple-element.54._after.stay0, bf16[2048,768]{1,0:T(8,128)(2,1)S(1)} %dense.8._after.refs_0_), custom_call_target="tpu_custom_call", output_to_operand_aliasing={{}: (3, {})} | custom-call | flops 2617245696 | bytes 4194304 | tf_op jit(solution)/shard_map/dense/pallas_call | solution.py:280
  35.1 1.0 %scatter.3 = (bf16[2048,768]{1,0:T(8,128)(2,1)S(1)}, bf16[2048,256]{1,0:T(8,128)(2,1)S(1)}) custom-call(s32[1,2048]{1,0:T(1,128)S(1)} %get-tuple-element.36.order, bf16[2048,768]{1,0:T(8,128)(2,1)S(1)} %dense.10.result, bf16[2048,256]{1,0:T(8,128)(2,1)S(1)} %get-tuple-element.43.basis, ...), custom_call_target="tpu_custom_call", output_to_operand_aliasing={{1}: (4, {})} | custom-call | flops 2147483648 | bytes 4194304 | tf_op jit(solution)/shard_map/scatter/pallas_call | solution.py:280
  36.2 0.5 collective-permute-start.9
  37.0 3.4 %scatter.4 = (bf16[2048,768]{1,0:T(8,128)(2,1)S(1)}, bf16[2048,256]{1,0:T(8,128)(2,1)S(1)}) custom-call(s32[1,2048]{1,0:T(1,128)S(1)} %get-tuple-element.36.order, bf16[2048,768]{1,0:T(8,128)(2,1)S(1)} %dense.10.result, bf16[2048,256]{1,0:T(8,128)(2,1)S(1)} %get-tuple-element.43.basis, ...), custom_call_target="tpu_custom_call", output_to_operand_aliasing={{0}: (4, {}), {1}: (5, {})} | custom-call | flops 3221225472 | bytes 4194304 | tf_op jit(solution)/shard_map/scatter/pallas_call | solution.py:280
  40.7 0.7 %collective-permute-start.11 = (bf16[192,256]{1,0:T(8,128)(2,1)S(1)}, bf16[192,256]{1,0:T(8,128)(2,1)S(1)}, u32[]{:S(2)}, u32[]{:S(2)}) collective-permute-start(bf16[192,256]{1,0:T(8,128)(2,1)S(1)} %down1.1._after.own), channel_id=1, source_target_pairs={{0,8},{1,9},{2,10},{3,11},{4,12},{5,13},{6,14},{7,15},{8,0},{9,1},... | collective-permute-start | bytes 294920 | tf_op jit(solution)/shard_map/ppermute | solution.py:27
  41.9 2.6 %scatter.5 = (bf16[2048,768]{1,0:T(8,128)(2,1)S(1)}, bf16[2048,256]{1,0:T(8,128)(2,1)S(1)}) custom-call(s32[1,2048]{1,0:T(1,128)S(1)} %get-tuple-element.36.order, bf16[2048,768]{1,0:T(8,128)(2,1)S(1)} %dense.10.result, bf16[2048,256]{1,0:T(8,128)(2,1)S(1)} %get-tuple-element.43.basis, ...), custom_call_target="tpu_custom_call", output_to_operand_aliasing={{0}: (4, {}), {1}: (5, {})} | custom-call | flops 3221225472 | bytes 4194304 | tf_op jit(solution)/shard_map/scatter/pallas_call | solution.py:280
  44.6 1.4 %own_half_1.1 = (bf16[2048,768]{1,0:T(8,128)(2,1)}, bf16[2048,384]{1,0:T(8,128)(2,1)S(1)}, bf16[384,256]{1,0:T(8,128)(2,1)S(1)}) custom-call(bf16[2048,768]{1,0:T(8,128)(2,1)S(1)} %get-tuple-element.60._after.base, bf16[2048,256]{1,0:T(8,128)(2,1)S(1)} %get-tuple-element.61.turned, bf16[384,256]{1,0:T(8,128)(2,1)S(1)} %join.1.down1, ...), custom_call_target="tpu_custom_call", output_to_operand_aliasing={{2}: (2, {})} | custom-call | flops 402653184 | bytes 2097152 | tf_op jit(solution)/shard_map/own_half_1/pallas_call | solution.py:409
  46.0 4.2 %collective-permute-start.12 = (bf16[384,256]{1,0:T(8,128)(2,1)S(1)}, bf16[384,256]{1,0:T(8,128)(2,1)S(1)}, u32[]{:S(2)}, u32[]{:S(2)}) collective-permute-start(bf16[384,256]{1,0:T(8,128)(2,1)S(1)} %get-tuple-element.62.down1), channel_id=1, source_target_pairs={{0,1},{1,0},{2,3},{3,2},{4,5},{5,4},{6,7},{7,6},{8,9},{9,8},{10,11... | collective-permute-start | bytes 589832 | tf_op jit(solution)/shard_map/ppermute | solution.py:27
  50.2 1.0 %collective-permute-done.12.down1 = bf16[384,256]{1,0:T(8,128)(2,1)S(1)} collective-permute-done((bf16[384,256]{1,0:T(8,128)(2,1)S(1)}, bf16[384,256]{1,0:T(8,128)(2,1)S(1)}, u32[]{:S(2)}, u32[]{:S(2)}) %collective-permute-start.12) | collective-permute-done | bytes 196640 | tf_op jit(solution)/shard_map/ppermute | solution.py:27
  51.3 1.7 %final.1 = bf16[2048,768]{1,0:T(8,128)(2,1)} custom-call(bf16[2048,768]{1,0:T(8,128)(2,1)S(1)} %get-tuple-element.60._after.base, bf16[2048,256]{1,0:T(8,128)(2,1)S(1)} %get-tuple-element.61.turned, bf16[384,256]{1,0:T(8,128)(2,1)S(1)} %collective-permute-done.12.down1, f32[256,768]{1,0:T(8,128)S(1)} %near0.1._after, ...), custom_call_target="tpu_custom_call", output_to_operand_aliasing={{}: (6, {})} | custom-call | flops 402653184 | bytes 4194304 | tf_op jit(solution)/shard_map/final/pallas_call | solution.py:428
  (34 shorter events, 2.9 us)
Async XLA Ops:
  4.7 4.9 %collective-permute-start = (bf16[384,256]{1,0:T(8,128)(2,1)S(1)}, bf16[384,256]{1,0:T(8,128)(2,1)S(1)}, u32[]{:S(2)}, u32[]{:S(2)}) collective-permute-start(bf16[384,256]{1,0:T(8,128)(2,1)S(1)} %get-tuple-element.41._after), channel_id=1, source_target_pairs={{0,1},{1,0},{2,3},{3,2},{4,5},{5,4},{6,7},{7,6},{8,9},{9,8},{10,11... | collective-permute-start | bytes 589832 | tf_op jit(solution)/shard_map/ppermute | solution.py:27
  7.2 13.2 %collective-permute-start.3 = (bf16[768,256]{1,0:T(8,128)(2,1)S(1)}, bf16[768,256]{1,0:T(8,128)(2,1)S(1)}, u32[]{:S(2)}, u32[]{:S(2)}) collective-permute-start(bf16[768,256]{1,0:T(8,128)(2,1)S(1)} %get-tuple-element.44._after), channel_id=1, source_target_pairs={{0,1},{1,0},{2,3},{3,2},{4,5},{5,4},{6,7},{7,6},{8,9},{9,8},{10,11... | collective-permute-start | bytes 1179656 | tf_op jit(solution)/shard_map/ppermute | solution.py:27
  9.7 5.3 %collective-permute-start.1 = (bf16[192,256]{1,0:T(8,128)(2,1)S(1)}, bf16[192,256]{1,0:T(8,128)(2,1)S(1)}, u32[]{:S(2)}, u32[]{:S(2)}) collective-permute-start(bf16[192,256]{1,0:T(8,128)(2,1)S(1)} %get-tuple-element.46._after), channel_id=1, source_target_pairs={{0,8},{1,9},{2,10},{3,11},{4,12},{5,13},{6,14},{7,15},{8,0},{9,1},... | collective-permute-start | bytes 294920 | tf_op jit(solution)/shard_map/ppermute | solution.py:27
  15.2 6.7 %slice-start = ((s8[8388608]{0:T(1024)(128)(4,1)}), s8[4194304]{0:T(1024)(128)(4,1)S(1)}, s32[]{:S(2)}) async-start(s8[8388608]{0:T(1024)(128)(4,1)} %bitcast.3), calls=%async_computation | async-start | bytes 8388608
  15.2 6.7 %slice-start.1 = ((s8[8388608]{0:T(1024)(128)(4,1)}), s8[4194304]{0:T(1024)(128)(4,1)S(1)}, s32[]{:S(2)}) async-start(s8[8388608]{0:T(1024)(128)(4,1)} %bitcast.3), calls=%async_computation.1 | async-start | bytes 8388608
  15.2 5.3 %collective-permute-start.2 = (bf16[192,256]{1,0:T(8,128)(2,1)S(1)}, bf16[192,256]{1,0:T(8,128)(2,1)S(1)}, u32[]{:S(2)}, u32[]{:S(2)}) collective-permute-start(bf16[192,256]{1,0:T(8,128)(2,1)S(1)} %get-tuple-element.48._after.mine), channel_id=1, source_target_pairs={{0,24},{1,25},{2,26},{3,27},{4,28},{5,29},{6,30},{7,31},{8,16},{9,... | collective-permute-start | bytes 294920 | tf_op jit(solution)/shard_map/ppermute | solution.py:27
  20.4 21.0 %collective-permute-start.7 = (bf16[1536,256]{1,0:T(8,128)(2,1)S(1)}, bf16[1536,256]{1,0:T(8,128)(2,1)S(1)}, u32[]{:S(2)}, u32[]{:S(2)}) collective-permute-start(bf16[1536,256]{1,0:T(8,128)(2,1)S(1)} %fill.1._after), channel_id=1, source_target_pairs={{0,8},{1,9},{2,10},{3,11},{4,12},{5,13},{6,14},{7,15},{8,0},{9,1},... | collective-permute-start | bytes 2359304 | tf_op jit(solution)/shard_map/ppermute | solution.py:27
  20.5 4.7 %collective-permute-start.4 = (bf16[192,256]{1,0:T(8,128)(2,1)S(1)}, bf16[192,256]{1,0:T(8,128)(2,1)S(1)}, u32[]{:S(2)}, u32[]{:S(2)}) collective-permute-start(bf16[192,256]{1,0:T(8,128)(2,1)S(1)} %sum_x.1._after.mine), channel_id=1, source_target_pairs={{0,2},{1,3},{2,0},{3,1},{4,6},{5,7},{6,4},{7,5},{8,10},{9,11},{10,... | collective-permute-start | bytes 294920 | tf_op jit(solution)/shard_map/ppermute | solution.py:27
  23.9 5.5 %collective-permute-start.6 = (bf16[192,256]{1,0:T(8,128)(2,1)S(1)}, bf16[192,256]{1,0:T(8,128)(2,1)S(1)}, u32[]{:S(2)}, u32[]{:S(2)}) collective-permute-start(bf16[192,256]{1,0:T(8,128)(2,1)S(1)} %get-tuple-element.53.coef1), channel_id=1, source_target_pairs={{0,24},{1,25},{2,26},{3,27},{4,28},{5,29},{6,30},{7,31},{8,16},{9,... | collective-permute-start | bytes 294920 | tf_op jit(solution)/shard_map/ppermute | solution.py:27
  25.2 4.8 %collective-permute-start.5 = (bf16[192,256]{1,0:T(8,128)(2,1)S(1)}, bf16[192,256]{1,0:T(8,128)(2,1)S(1)}, u32[]{:S(2)}, u32[]{:S(2)}) collective-permute-start(bf16[192,256]{1,0:T(8,128)(2,1)S(1)} %sum_z.1._after.own), channel_id=1, source_target_pairs={{0,6},{1,7},{2,4},{3,5},{4,2},{5,3},{6,0},{7,1},{8,14},{9,15},{10,... | collective-permute-start | bytes 294920 | tf_op jit(solution)/shard_map/ppermute | solution.py:27
  29.4 7.4 %collective-permute-start.10 = (bf16[384,256]{1,0:T(8,128)(2,1)S(1)}, bf16[384,256]{1,0:T(8,128)(2,1)S(1)}, u32[]{:S(2)}, u32[]{:S(2)}) collective-permute-start(bf16[384,256]{1,0:T(8,128)(2,1)S(1)} %both.1._after), channel_id=1, source_target_pairs={{0,2},{1,3},{2,0},{3,1},{4,6},{5,7},{6,4},{7,5},{8,10},{9,11},{10,... | collective-permute-start | bytes 589832 | tf_op jit(solution)/shard_map/ppermute | solution.py:27
  30.3 5.9 %collective-permute-start.8 = (bf16[384,256]{1,0:T(8,128)(2,1)S(1)}, bf16[384,256]{1,0:T(8,128)(2,1)S(1)}, u32[]{:S(2)}, u32[]{:S(2)}) collective-permute-start(bf16[384,256]{1,0:T(8,128)(2,1)S(1)} %top_send.1._after), channel_id=1, source_target_pairs={{0,96},{1,97},{2,98},{3,99},{4,100},{5,101},{6,102},{7,103},{8,104... | collective-permute-start | bytes 589832 | tf_op jit(solution)/shard_map/ppermute | solution.py:27
  36.2 4.3 %collective-permute-start.9 = (bf16[192,256]{1,0:T(8,128)(2,1)S(1)}, bf16[192,256]{1,0:T(8,128)(2,1)S(1)}, u32[]{:S(2)}, u32[]{:S(2)}) collective-permute-start(bf16[192,256]{1,0:T(8,128)(2,1)S(1)} %half.1._after), channel_id=1, source_target_pairs={{0,32},{1,33},{2,34},{3,35},{4,36},{5,37},{6,38},{7,39},{8,40},{9,... | collective-permute-start | bytes 294920 | tf_op jit(solution)/shard_map/ppermute | solution.py:27
  40.7 3.8 %collective-permute-start.11 = (bf16[192,256]{1,0:T(8,128)(2,1)S(1)}, bf16[192,256]{1,0:T(8,128)(2,1)S(1)}, u32[]{:S(2)}, u32[]{:S(2)}) collective-permute-start(bf16[192,256]{1,0:T(8,128)(2,1)S(1)} %down1.1._after.own), channel_id=1, source_target_pairs={{0,8},{1,9},{2,10},{3,11},{4,12},{5,13},{6,14},{7,15},{8,0},{9,1},... | collective-permute-start | bytes 294920 | tf_op jit(solution)/shard_map/ppermute | solution.py:27
  46.0 5.3 %collective-permute-start.12 = (bf16[384,256]{1,0:T(8,128)(2,1)S(1)}, bf16[384,256]{1,0:T(8,128)(2,1)S(1)}, u32[]{:S(2)}, u32[]{:S(2)}) collective-permute-start(bf16[384,256]{1,0:T(8,128)(2,1)S(1)} %get-tuple-element.62.down1), channel_id=1, source_target_pairs={{0,1},{1,0},{2,3},{3,2},{4,5},{5,4},{6,7},{7,6},{8,9},{9,8},{10,11... | collective-permute-start | bytes 589832 | tf_op jit(solution)/shard_map/ppermute | solution.py:27
